TPU v7x, 1024 devices: a whole 4x4x32 slice. The times are simulated.
1024 devices in a mesh: dp: 128 (over y, z), tensor: 8 (over x, core).
Axes of the slice: x: 4, y: 4, z: 32, core: 2. Of those that a mesh axis runs over, the one named last changes fastest.
Arguments:
- activations: bfloat16 [32768, 4096], P('dp'), may hold values from -6 to 6
- cotangents: bfloat16 [32768, 1024], P('dp', 'tensor'), may hold values from -3 to 3
- left_stats: float32 [8, 4, 1024, 1024], P('tensor', None, 'dp'), may hold values from -6 to 6
- right_stats: float32 [8, 4, 128, 128], P('tensor', None, 'dp'), may hold values from -6 to 6
- left_roots: float32 [8, 4, 1024, 1024], P('tensor', None, 'dp'), may hold values from -1 to 4
- right_roots: float32 [8, 4, 128, 128], P('tensor'), may hold values from -1 to 4
Outputs:
- update: bfloat16 [4096, 1024], P(None, 'tensor')
- left_new: float32 [8, 4, 1024, 1024], P('tensor', None, 'dp')
- right_new: float32 [8, 4, 128, 128], P('tensor', None, 'dp')
All inputs are finite; a program needn't handle non-finite values.
Results may differ from a plain program's by a relative error of at most 0.0052.
Values may be sent and summed in bfloat16 or wider, within the bound.
No kernel may reach another device: no remote copies, remote signals or barrier semaphores. Data moves between devices by JAX's collectives and lax.ppermute only.
A program may use at most 32 MiB of HBM per device.

v0:
```python
import jax
import jax.numpy as jnp
from jax import lax
from jax.sharding import PartitionSpec as P

BLOCK = 1024


stat_decay = 0.95
highest = lax.Precision.HIGHEST


def shards(activations, cotangents, left_stats, right_stats, left_roots, right_roots):
    dp_count = lax.axis_size("dp")
    tensor_count = lax.axis_size("tensor")
    tokens = activations.shape[0]
    block_count = activations.shape[1] // BLOCK
    col_width = cotangents.shape[1]
    col_count = col_width // dp_count
    blocked = activations.reshape(tokens, block_count, BLOCK)
    own_rows = lax.psum_scatter(
        jnp.einsum("tbr,tc->rbc", blocked, cotangents, preferred_element_type=jnp.float32),
        "dp",
        scatter_dimension=0,
        tiled=True,
    )
    left_rows = left_roots[0]
    right_full = right_roots[0]
    own_mixed = jnp.einsum("rbc,bcd->rbd", own_rows, right_full, precision=highest)
    col_first = lax.axis_index("dp") * col_count
    grad_piece = lax.all_gather(own_rows, "dp", axis=0, tiled=True)
    mixed_piece = lax.all_gather(own_mixed, "dp", axis=0, tiled=True)
    outer_term = jnp.einsum("rbc,sbc->brs", own_rows, grad_piece, precision=highest)
    outer_part = outer_term
    own_cols = lax.dynamic_slice_in_dim(grad_piece, col_first, col_count, 2)
    inner_part = jnp.einsum("sbk,sbc->bkc", own_cols, grad_piece, precision=highest)
    precon = jnp.einsum("brs,sbd->brd", left_rows, mixed_piece, precision=highest)
    outer_part, inner_part, precon = (outer_part, inner_part, precon)
    left_new = stat_decay * left_stats + (1.0 - stat_decay) * (outer_part / col_width)[None]
    right_new = stat_decay * right_stats + (1.0 - stat_decay) * (inner_part / BLOCK)[None]
    directions = precon.astype(jnp.bfloat16)
    wide_dirs = directions.astype(jnp.float32)
    grad_local = jnp.sum(own_rows * own_rows, axis=(0, 2))
    dir_local = jnp.sum(wide_dirs * wide_dirs, axis=(1, 2))
    grad_sq, dir_sq = lax.psum((grad_local, dir_local), "dp")
    layer_sq = lax.psum(jnp.sum(grad_sq), "tensor")
    layer_rms = jnp.sqrt(layer_sq / (activations.shape[1] * col_width * tensor_count))
    factor = jnp.sqrt(grad_sq / dir_sq) / layer_rms
    gathered = (
        lax.all_gather(directions, "dp", axis=1, tiled=True).astype(jnp.float32)
        * factor[:, None, None]
    ).astype(jnp.bfloat16)
    update = gathered.reshape(block_count * BLOCK, col_width)
    return (update, left_new, right_new)


def solution(mesh):
    in_specs = (
        P("dp", None),
        P("dp", "tensor"),
        P("tensor", None, "dp", None),
        P("tensor", None, "dp", None),
        P("tensor", None, "dp", None),
        P("tensor", None, None, None),
    )
    out_specs = (P(None, "tensor"), P("tensor", None, "dp", None), P("tensor", None, "dp", None))
    return jax.shard_map(shards, mesh=mesh, in_specs=in_specs, out_specs=out_specs, check_vma=False)
```

profile of v0, /device:TPU:1, one launch (start us, length us, event | category | flops | bytes accessed | tf_op | source)
XLA Modules:
  0.0 1285.8 jit_solution(13987209975873917500)
XLA Ops:
  7.2 0.0 copy-start
  7.2 0.0 all-reduce.4.cloned.1.call-start
  7.2 2.1 fusion.8
  9.4 1.8 copy.20
  11.2 0.0 copy-start.4
  11.2 0.0 all-reduce.4.cloned.1.call-update
  11.2 0.0 all-gather.4.cloned.1.call-start
  11.3 1.3 dynamic-slice
  13.2 505.3 %all-reduce.4.cloned.1.call-done = f32[1024,4,128]{2,1,0:T(4,128)} async-done(((f32[1024,4,128]{2,1,0:T(4,128)}), f32[1024,4,128]{2,1,0:T(4,128)}) %all-reduce.4.cloned.1.call-update) | async-done | bytes 2097168
  518.5 0.8 multiply_reduce_fusion.1
  519.3 0.0 copy-start.2
  519.3 0.0 copy-done
  519.4 0.9 convolution_bitcast_fusion
  520.3 0.0 all-gather.4.cloned.1.call-update
  520.3 0.0 all-gather.8.cloned.1.call-start
  520.4 0.0 copy-done.2
  520.4 0.7 all-gather.8.cloned.1.call-update
  521.0 0.0 all-gather.6.cloned.1.call-start
  521.1 248.3 %all-gather.4.cloned.1.call-done = f32[1024,4,128]{2,0,1:T(8,128)} async-done(((f32[8,4,128]{2,0,1:T(8,128)}), f32[1024,4,128]{2,0,1:T(8,128)}) %all-gather.4.cloned.1.call-update) | async-done | bytes 2097168 | tf_op jit(solution)/shard_map/all_gather | solution.py:32
  769.4 0.0 copy-done.4
  769.4 3.4 multiply_reduce_fusion
  772.8 0.0 all-gather.6.cloned.1.call-update
  772.8 222.1 %all-reduce.1 = (f32[4]{0:T(128)S(1)}, f32[4]{0:T(128)S(1)}) all-reduce(f32[4]{0:T(128)S(1)} %get-tuple-element.5, f32[4]{0:T(128)S(1)} %get-tuple-element.7), channel_id=1, replica_groups=mesh['dp'=128,'tensor'=8] {'dp'}, use_global_device_ids=true, to_apply=%region_2.0 | all-reduce | flops 8 | bytes 64 | tf_op jit(solution)/shard_map/psum | solution.py:45
  994.9 0.6 reduce_sum.29
  995.5 91.7 %psum.23 = f32[]{:T(128)} all-reduce(f32[]{:T(128)} %reduce_sum.29), channel_id=1, replica_groups=mesh['dp'=128,'tensor'=8] {'tensor'}, use_global_device_ids=true, to_apply=%region_6.0 | all-reduce | flops 1 | bytes 8 | tf_op jit(solution)/shard_map/psum | solution.py:46
  1087.9 0.0 all-gather.8.cloned.1.call-done
  1087.9 0.0 copy-start.1
  1087.9 2.9 constant_dynamic-slice_fusion.1
  1090.8 0.0 copy-done.1
  1090.8 0.0 copy-start.6
  1090.8 0.0 copy-start.3
  1090.8 0.0 copy-start.5
  1090.9 3.5 fusion.3
  1094.3 0.0 copy-done.6
  1094.3 0.6 multiply_add_fusion
  1094.9 0.0 copy-done.3
  1094.9 0.0 copy-done.5
  1095.0 2.5 fusion.17
  1097.5 179.3 %all-gather.6.cloned.1.call-done = bf16[4,1024,128]{2,1,0:T(8,128)(2,1)} async-done(((bf16[4,8,128]{2,1,0:T(8,128)(2,1)}), bf16[4,1024,128]{2,1,0:T(8,128)(2,1)}) %all-gather.6.cloned.1.call-update) | async-done | bytes 1048592 | tf_op jit(solution)/shard_map/all_gather | solution.py:50
  1276.8 2.5 multiply_convert_fusion
  (2 shorter events, 0.0 us)
Async XLA Ops:
  7.2 512.2 %copy-start = (f32[1,4,128,128]{3,2,1,0:T(8,128)S(1)}, f32[1,4,128,128]{3,2,1,0:T(8,128)}, u32[]{:S(2)}) copy-start(f32[1,4,128,128]{3,2,1,0:T(8,128)} %param.11) | copy-start | bytes 786436
  7.2 511.3 %all-reduce.4.cloned.1.call-start = ((), (), s32[]{:S(2)}) async-start(), calls=%async_computation.3 | async-start | bytes 4194304
  11.2 758.2 %copy-start.4 = (f32[1,4,8,1024]{3,2,1,0:T(8,128)S(1)}, f32[1,4,8,1024]{3,2,1,0:T(8,128)}, u32[]{:S(2)}) copy-start(f32[1,4,8,1024]{3,2,1,0:T(8,128)} %param.10) | copy-start | bytes 393220
  11.2 758.2 %all-gather.4.cloned.1.call-start = ((), (), s32[]{:S(2)}) async-start(), calls=%async_computation | async-start | bytes 2113536 | tf_op jit(solution)/shard_map/all_gather | solution.py:32
  519.3 1.0 copy-start.2
  520.3 567.6 %all-gather.8.cloned.1.call-start = ((), (), s32[]{:S(2)}) async-start(), calls=%async_computation.2 | async-start | bytes 2113536 | tf_op jit(solution)/shard_map/all_gather | solution.py:31
  521.0 755.7 %all-gather.6.cloned.1.call-start = ((), (), s32[]{:S(2)}) async-start(), calls=%async_computation.1 | async-start | bytes 1056768 | tf_op jit(solution)/shard_map/all_gather | solution.py:50
  1087.9 2.9 copy-start.1
  1090.8 3.5 copy-start.6
  1090.8 4.1 copy-start.3
  1090.8 4.1 copy-start.5
Sparse Core Ops, SparseCore 0:
  11.4 507.0 all-reduce.3
  523.2 246.1 all-gather.3
  774.1 259.7 all-gather.7
  1037.8 238.9 all-gather.5
where the time goes:
time: 1310 us; the launch traced here: 1290 us
  waiting for transfers between devices  934 us (71%)
  blocking collectives  314 us (24%)
  between operations  15.2 us (1%)
    unnamed x5, waiting for transfers between devices  506 us
    all_gather x1, waiting for transfers between devices, shards(): mixed_piece = lax.all_gather(own_mixed, 'dp', axis=0, tiled=True)  248 us
    psum x1, blocking collectives, shards(): grad_sq, dir_sq = lax.psum((grad_local, dir_local), 'dp')  222 us
    all_gather x1, waiting for transfers between devices, shards(): lax.all_gather(directions, 'dp', axis=1, tiled=True).astype(jnp.float32)  179 us
    psum x1, blocking collectives, shards(): layer_sq = lax.psum(jnp.sum(grad_sq), 'tensor')  91.7 us
  transfers between devices with their start and end apart: 4, of which 3 were waited for; matrix products, arithmetic and copies ran while one was open for 1% of the time, Pallas kernels for 0%

commit v1 on v0

v1 whole, which is shorter than its diff:
```python
import jax
import jax.numpy as jnp
from jax import lax
from jax.sharding import Mesh, PartitionSpec as P

BLOCK = 1024
stat_decay = 0.95
highest = lax.Precision.HIGHEST
f32 = jnp.float32
bf16 = jnp.bfloat16


def everyone(piece, axis, count):
    return lax.all_to_all(
        jnp.broadcast_to(piece[None], (count, *piece.shape)), axis, 0, 0, tiled=True
    )


def shards(activations, cotangents, left_stats, right_stats, left_roots, right_roots):
    ny = lax.axis_size("y")
    nz = lax.axis_size("z")
    y = lax.axis_index("y")
    z = lax.axis_index("z")
    features = activations.shape[1]
    width = cotangents.shape[1]
    blocks = features // BLOCK
    mine = left_roots.shape[2]
    per_row = BLOCK // width

    partial = lax.dot_general(
        activations, cotangents, (((0,), (0,)), ((), ())), preferred_element_type=f32
    ).reshape(blocks, BLOCK, width)
    roots = left_roots[0]
    roots_high = roots.astype(bf16)
    roots_low = (roots - roots_high.astype(f32)).astype(bf16)
    root_rows = mine * per_row
    sent = jnp.concatenate(
        [
            partial.astype(bf16),
            roots_high.reshape(blocks, root_rows, width),
            roots_low.reshape(blocks, root_rows, width),
        ],
        axis=1,
    )
    got = lax.all_to_all(sent, "y", 0, 0, tiled=True)
    kept = lax.dynamic_index_in_dim(partial, y, 0, keepdims=False)
    others = jnp.where((jnp.arange(ny) == y)[:, None, None], 0.0, got[:, :BLOCK].astype(f32))
    column_part = kept + jnp.sum(others, axis=0)
    roots_high = got[:, BLOCK : BLOCK + root_rows].reshape(ny * mine, BLOCK)
    roots_low = got[:, BLOCK + root_rows :].reshape(ny * mine, BLOCK)

    got = lax.all_to_all(
        column_part.astype(bf16).reshape(nz, BLOCK // nz, width), "z", 0, 0, tiled=True
    )
    own = jnp.sum(got.astype(f32), axis=0).astype(bf16)
    gradient = everyone(own, "z", nz).reshape(BLOCK, width)

    inner = lax.dot_general(
        gradient, gradient, (((0,), (0,)), ((), ())), preferred_element_type=f32
    )
    wide = gradient.astype(f32)
    grad_sq = jnp.sum(wide * wide)
    layer_sq = lax.psum(grad_sq, ("y", "tensor"))
    layer_rms = jnp.sqrt(layer_sq / (features * width * lax.axis_size("tensor")))

    right = lax.dynamic_index_in_dim(right_roots[0], y, 0, keepdims=False)
    mixed = jnp.dot(roots_high, gradient, preferred_element_type=f32) + jnp.dot(
        roots_low, gradient, preferred_element_type=f32
    )
    direction = jnp.dot(mixed, right, precision=highest).astype(bf16)
    direction = everyone(direction, "z", nz).reshape(nz, ny, mine, width)
    wide = direction.astype(f32)
    dir_sq = jnp.sum(wide * wide)
    factor = jnp.sqrt(grad_sq / dir_sq) / layer_rms
    update = (wide * factor).transpose(1, 0, 2, 3).reshape(BLOCK, width).astype(bf16)

    rows = lax.dynamic_index_in_dim(gradient.reshape(ny, nz, mine, width), z, 1, keepdims=False)
    outer = lax.dot_general(
        rows.reshape(ny * mine, width), gradient, (((1,), (1,)), ((), ())), preferred_element_type=f32
    )
    outer = outer.astype(bf16).reshape(ny, root_rows, width)
    inner = lax.dynamic_index_in_dim(inner.reshape(ny, nz, width), z, 1, keepdims=True).astype(bf16)
    inner = jnp.broadcast_to(inner, (ny, 16, width))
    sent = jnp.concatenate(
        [jnp.broadcast_to(update[None], (ny, BLOCK, width)), outer, inner], axis=1
    )
    got = lax.all_to_all(sent, "y", 0, 0, tiled=True)
    update = got[:, :BLOCK].reshape(blocks * BLOCK, width)
    outer = got[:, BLOCK : BLOCK + root_rows].astype(f32).reshape(blocks, mine, BLOCK)
    inner = got[:, BLOCK + root_rows : BLOCK + root_rows + 1].astype(f32)
    left_new = stat_decay * left_stats + ((1.0 - stat_decay) / width) * outer[None]
    right_new = stat_decay * right_stats + ((1.0 - stat_decay) / BLOCK) * inner[None]
    return (update, left_new, right_new)


def solution(mesh):
    dp, tensor = mesh.devices.shape
    blocks = 4
    fine = Mesh(mesh.devices.reshape(blocks, dp // blocks, tensor), ("y", "z", "tensor"))
    dp = ("y", "z")
    in_specs = (
        P(dp, None),
        P(dp, "tensor"),
        P("tensor", None, dp, None),
        P("tensor", None, dp, None),
        P("tensor", None, dp, None),
        P("tensor", None, None, None),
    )
    out_specs = (P(None, "tensor"), P("tensor", None, dp, None), P("tensor", None, dp, None))
    return jax.shard_map(shards, mesh=fine, in_specs=in_specs, out_specs=out_specs, check_vma=False)
```

time: 1310 us -> 243 us (0.19); the launches traced: 1290 us -> 242 us
  waiting for transfers between devices: 934 us -> 44.1 us
  blocking collectives: 314 us -> 156 us
  starting transfers between devices: 0.16 us -> 17.7 us
    unnamed x5 -> x0, waiting for transfers between devices: 506 us -> none
    all_gather x3 -> x0, waiting for transfers between devices: 428 us -> none  [the longest x1 248 us: shards(): mixed_piece = lax.all_gather(own_mixed, 'dp', axis=0, tiled=True)]
    psum x2 -> x1, blocking collectives: 314 us -> 67.7 us  [shards(): layer_sq = lax.psum(grad_sq, ('y', 'tensor'))]
    all_to_all x0 -> x2, blocking collectives: none -> 88.5 us  [the longest x1 70.8 us: shards(): lax.all_to_all(column_part.astype(bf16).reshape(nz, BLOCK // nz, width),...]
    all_to_all x0 -> x3, waiting for transfers between devices: none -> 44.1 us  [the longest x2 35.5 us: everyone(): lax.all_to_all(jnp.broadcast_to(piece[None], (count, *piece.shape)), axis...]
    all_to_all x0 -> x3, starting transfers between devices: none -> 17.7 us  [the longest x2 12.7 us: everyone(): lax.all_to_all(jnp.broadcast_to(piece[None], (count, *piece.shape)), axis...]
  transfers between devices with their start and end apart: 4 -> 3, of which waited for: 3 -> 2; matrix products, arithmetic and copies ran while one was open for 1% -> 2% of each run, Pallas kernels for 0% -> 0%
where the time goes in v1:
time: 243 us; the launch traced here: 242 us
  blocking collectives  156 us (64%)
  waiting for transfers between devices  44.1 us (18%)
  starting transfers between devices  17.7 us (7%)
  local copies, waits for them, and re-layouts  10.2 us (4%)
  other arithmetic  7.49 us (3%)
  matrix products  3.32 us (1%)
  between operations  2.92 us (1%)
    all_to_all x1, blocking collectives, shards(): lax.all_to_all(column_part.astype(bf16).reshape(nz, BLOCK // nz, width),...  70.8 us
    psum x1, blocking collectives, shards(): layer_sq = lax.psum(grad_sq, ('y', 'tensor'))  67.7 us
    all_to_all x2, waiting for transfers between devices, everyone(): lax.all_to_all(jnp.broadcast_to(piece[None], (count, *piece.shape)), axis...  35.5 us
    all_to_all x1, blocking collectives, shards(): got = lax.all_to_all(sent, 'y', 0, 0, tiled=True)  17.7 us
    all_to_all x2, starting transfers between devices, everyone(): lax.all_to_all(jnp.broadcast_to(piece[None], (count, *piece.shape)), axis...  12.7 us
    all_to_all x1, waiting for transfers between devices, shards(): got = lax.all_to_all(sent, 'y', 0, 0, tiled=True)  8.57 us
    all_to_all x1, starting transfers between devices, shards(): got = lax.all_to_all(sent, 'y', 0, 0, tiled=True)  5.02 us
  transfers between devices with their start and end apart: 3, of which 2 were waited for; matrix products, arithmetic and copies ran while one was open for 2% of the time, Pallas kernels for 0%

profile of v1, /device:TPU:1, one launch (start us, length us, event | category | flops | bytes accessed | tf_op | source)
XLA Modules:
  0.0 241.9 jit_solution(3125930473869551641)
XLA Ops:
  0.6 0.0 copy-start
  0.6 1.6 copy-done
  2.2 1.6 fusion.11
  3.8 0.0 copy-start.1
  3.8 0.0 copy-start.2
  3.9 1.3 copy-done.1
  5.2 0.1 convert_element_type.65
  5.3 0.0 copy-done.2
  5.4 1.1 pad_maximum_fusion
  6.5 5.0 %all-to-all-start = ((bf16[4,1152,128]{2,1,0:T(8,128)(2,1)}), bf16[4,1152,128]{2,1,0:T(8,128)(2,1)S(1)}, u32[]{:S(2)}, u32[]{:S(2)}) async-start(bf16[4,1152,128]{2,1,0:T(8,128)(2,1)} %pad_maximum_fusion), calls=%async_computation | async-start | bytes 2359296 | tf_op jit(solution)/shard_map/all_to_all | solution.py:45
  11.5 1.9 constant_dynamic-slice_fusion
  13.4 8.6 %all-to-all-done = bf16[4,1152,128]{2,1,0:T(8,128)(2,1)S(1)} async-done(((bf16[4,1152,128]{2,1,0:T(8,128)(2,1)}), bf16[4,1152,128]{2,1,0:T(8,128)(2,1)S(1)}, u32[]{:S(2)}, u32[]{:S(2)}) %all-to-all-start) | async-done | bytes 1179680 | tf_op jit(solution)/shard_map/all_to_all | solution.py:45
  22.0 0.3 select_reduce_fusion
  22.3 1.1 add_convert_fusion
  23.4 70.8 %all_to_all.25 = bf16[32,32,128]{2,1,0:T(8,128)(2,1)} all-to-all(bf16[32,32,128]{2,1,0:T(8,128)(2,1)S(1)} %add_convert_fusion), channel_id=1, replica_groups=mesh['y'=4,'z'=32,'tensor'=8] {'z'}, dimensions={0} | all-to-all | bytes 524288 | tf_op jit(solution)/shard_map/all_to_all | solution.py:52
  94.2 1.0 reduce_sum.43
  95.2 0.7 broadcast_in_dim.24
  95.9 7.0 %all-to-all-start.2 = ((bf16[32,32,128]{2,1,0:T(8,128)(2,1)}), bf16[32,32,128]{2,1,0:T(8,128)(2,1)S(1)}, u32[]{:S(2)}, u32[]{:S(2)}) async-start(bf16[32,32,128]{2,1,0:T(8,128)(2,1)} %broadcast_in_dim.24), calls=%async_computation.2 | async-start | bytes 524288 | tf_op jit(solution)/shard_map/all_to_all | solution.py:14
  102.9 0.7 fusion.10
  103.6 0.9 reshape.86
  104.5 0.9 reshape.88
  105.3 35.5 %all-to-all-done.2 = bf16[32,32,128]{2,1,0:T(8,128)(2,1)S(1)} async-done(((bf16[32,32,128]{2,1,0:T(8,128)(2,1)}), bf16[32,32,128]{2,1,0:T(8,128)(2,1)S(1)}, u32[]{:S(2)}, u32[]{:S(2)}) %all-to-all-start.2) | async-done | bytes 262176 | tf_op jit(solution)/shard_map/all_to_all | solution.py:14
  140.8 0.2 fusion.12
  141.0 0.2 convolution_add_fusion
  141.2 1.0 convolution_convert_fusion.1
  142.2 0.7 broadcast_in_dim.42
  142.9 5.7 %all-to-all-start.3 = ((bf16[32,32,128]{2,1,0:T(8,128)(2,1)}), bf16[32,32,128]{2,1,0:T(8,128)(2,1)S(1)}, u32[]{:S(2)}, u32[]{:S(2)}) async-start(bf16[32,32,128]{2,1,0:T(8,128)(2,1)} %broadcast_in_dim.42), calls=%async_computation.3 | async-start | bytes 524288 | tf_op jit(solution)/shard_map/all_to_all | solution.py:14
  148.6 0.7 multiply_reduce_fusion
  149.4 67.7 %psum.7 = f32[]{:T(128)} all-reduce(f32[]{:T(128)} %multiply_reduce_fusion), channel_id=1, replica_groups=mesh['y'=4,'z'=32,'tensor'=8] {'y','tensor'}, use_global_device_ids=true, to_apply=%region_4.5 | all-reduce | flops 1 | bytes 8 | tf_op jit(solution)/shard_map/psum | solution.py:63
  217.8 0.2 convolution_convert_fusion
  217.9 0.1 reshape.90
  218.0 0.1 copy.15
  218.2 0.2 fusion.13
  218.4 0.0 all-to-all-done.3
  218.4 0.7 fusion
  220.5 0.1 fusion.2
  220.7 0.1 broadcast_in_dim.43
  220.8 0.1 pad_maximum_fusion.1
  220.9 0.0 copy-start.3
  220.9 17.7 %all_to_all.26 = bf16[4,1104,128]{2,1,0:T(8,128)(2,1)S(1)} all-to-all(bf16[4,1104,128]{2,1,0:T(8,128)(2,1)S(1)} %pad_maximum_fusion.1), channel_id=1, replica_groups=mesh['y'=4,'z'=32,'tensor'=8] {'y'}, dimensions={0} | all-to-all | bytes 2260992 | tf_op jit(solution)/shard_map/all_to_all | solution.py:87
  238.7 1.6 multiply_add_fusion
  240.3 0.0 copy-done.3
  240.3 0.6 multiply_add_fusion.1
  240.9 1.0 slice.27
  (10 shorter events, 0.2 us)
Async XLA Ops:
  0.6 1.6 copy-start
  3.8 1.4 copy-start.1
  3.8 1.5 copy-start.2
  6.5 15.5 %all-to-all-start = ((bf16[4,1152,128]{2,1,0:T(8,128)(2,1)}), bf16[4,1152,128]{2,1,0:T(8,128)(2,1)S(1)}, u32[]{:S(2)}, u32[]{:S(2)}) async-start(bf16[4,1152,128]{2,1,0:T(8,128)(2,1)} %pad_maximum_fusion), calls=%async_computation | async-start | bytes 2359296 | tf_op jit(solution)/shard_map/all_to_all | solution.py:45
  95.9 44.9 %all-to-all-start.2 = ((bf16[32,32,128]{2,1,0:T(8,128)(2,1)}), bf16[32,32,128]{2,1,0:T(8,128)(2,1)S(1)}, u32[]{:S(2)}, u32[]{:S(2)}) async-start(bf16[32,32,128]{2,1,0:T(8,128)(2,1)} %broadcast_in_dim.24), calls=%async_computation.2 | async-start | bytes 524288 | tf_op jit(solution)/shard_map/all_to_all | solution.py:14
  142.9 75.5 %all-to-all-start.3 = ((bf16[32,32,128]{2,1,0:T(8,128)(2,1)}), bf16[32,32,128]{2,1,0:T(8,128)(2,1)S(1)}, u32[]{:S(2)}, u32[]{:S(2)}) async-start(bf16[32,32,128]{2,1,0:T(8,128)(2,1)} %broadcast_in_dim.42), calls=%async_computation.3 | async-start | bytes 524288 | tf_op jit(solution)/shard_map/all_to_all | solution.py:14
  220.9 19.4 %copy-start.3 = (f32[1,4,1,128]{3,2,1,0:T(1,128)S(1)}, f32[1,4,1,128]{3,2,1,0:T(1,128)}, u32[]{:S(2)}) copy-start(f32[1,4,1,128]{3,2,1,0:T(1,128)} %param.9) | copy-start | bytes 6148

commit v2 on v1

--- a/solution.py
+++ b/solution.py
@@ -19,6 +19,7 @@
 def shards(activations, cotangents, left_stats, right_stats, left_roots, right_roots):
     ny = lax.axis_size("y")
     nz = lax.axis_size("z")
+    tensors = lax.axis_size("tensor")
     y = lax.axis_index("y")
     z = lax.axis_index("z")
     features = activations.shape[1]
@@ -30,24 +31,14 @@
     partial = lax.dot_general(
         activations, cotangents, (((0,), (0,)), ((), ())), preferred_element_type=f32
     ).reshape(blocks, BLOCK, width)
-    roots = left_roots[0]
-    roots_high = roots.astype(bf16)
-    roots_low = (roots - roots_high.astype(f32)).astype(bf16)
     root_rows = mine * per_row
-    sent = jnp.concatenate(
-        [
-            partial.astype(bf16),
-            roots_high.reshape(blocks, root_rows, width),
-            roots_low.reshape(blocks, root_rows, width),
-        ],
-        axis=1,
-    )
+    roots = left_roots[0].astype(bf16).reshape(blocks, root_rows, width)
+    sent = jnp.concatenate([partial.astype(bf16), roots], axis=1)
     got = lax.all_to_all(sent, "y", 0, 0, tiled=True)
+    roots = lax.all_gather(got[:, BLOCK:].reshape(ny * mine, BLOCK), "z", axis=0, tiled=True)
     kept = lax.dynamic_index_in_dim(partial, y, 0, keepdims=False)
     others = jnp.where((jnp.arange(ny) == y)[:, None, None], 0.0, got[:, :BLOCK].astype(f32))
     column_part = kept + jnp.sum(others, axis=0)
-    roots_high = got[:, BLOCK : BLOCK + root_rows].reshape(ny * mine, BLOCK)
-    roots_low = got[:, BLOCK + root_rows :].reshape(ny * mine, BLOCK)
 
     got = lax.all_to_all(
         column_part.astype(bf16).reshape(nz, BLOCK // nz, width), "z", 0, 0, tiled=True
@@ -60,19 +51,13 @@
     )
     wide = gradient.astype(f32)
     grad_sq = jnp.sum(wide * wide)
-    layer_sq = lax.psum(grad_sq, ("y", "tensor"))
-    layer_rms = jnp.sqrt(layer_sq / (features * width * lax.axis_size("tensor")))
 
     right = lax.dynamic_index_in_dim(right_roots[0], y, 0, keepdims=False)
-    mixed = jnp.dot(roots_high, gradient, preferred_element_type=f32) + jnp.dot(
-        roots_low, gradient, preferred_element_type=f32
-    )
+    mixed = jnp.dot(roots, gradient, preferred_element_type=f32)
     direction = jnp.dot(mixed, right, precision=highest).astype(bf16)
-    direction = everyone(direction, "z", nz).reshape(nz, ny, mine, width)
     wide = direction.astype(f32)
     dir_sq = jnp.sum(wide * wide)
-    factor = jnp.sqrt(grad_sq / dir_sq) / layer_rms
-    update = (wide * factor).transpose(1, 0, 2, 3).reshape(BLOCK, width).astype(bf16)
+    direction = direction.reshape(nz, ny, mine, width).transpose(1, 0, 2, 3).reshape(BLOCK, width)
 
     rows = lax.dynamic_index_in_dim(gradient.reshape(ny, nz, mine, width), z, 1, keepdims=False)
     outer = lax.dot_general(
@@ -82,10 +67,17 @@
     inner = lax.dynamic_index_in_dim(inner.reshape(ny, nz, width), z, 1, keepdims=True).astype(bf16)
     inner = jnp.broadcast_to(inner, (ny, 16, width))
     sent = jnp.concatenate(
-        [jnp.broadcast_to(update[None], (ny, BLOCK, width)), outer, inner], axis=1
+        [jnp.broadcast_to(direction[None], (ny, BLOCK, width)), outer, inner], axis=1
     )
     got = lax.all_to_all(sent, "y", 0, 0, tiled=True)
-    update = got[:, :BLOCK].reshape(blocks * BLOCK, width)
+    norms = jnp.where((jnp.arange(8) == 0)[:, None], grad_sq, dir_sq)
+    norms = everyone(jnp.broadcast_to(norms, (8, width)), ("y", "tensor"), ny * tensors)
+    norms = norms[:, :2, 0].reshape(ny, tensors, 2)
+    layer_rms = jnp.sqrt(jnp.sum(norms[:, :, 0]) / (features * width * tensors))
+    norms = lax.dynamic_index_in_dim(norms, lax.axis_index("tensor"), 1, keepdims=False)
+    factor = jnp.sqrt(norms[:, 0] / norms[:, 1]) / layer_rms
+    update = (got[:, :BLOCK].astype(f32) * factor[:, None, None]).astype(bf16)
+    update = update.reshape(blocks * BLOCK, width)
     outer = got[:, BLOCK : BLOCK + root_rows].astype(f32).reshape(blocks, mine, BLOCK)
     inner = got[:, BLOCK + root_rows : BLOCK + root_rows + 1].astype(f32)
     left_new = stat_decay * left_stats + ((1.0 - stat_decay) / width) * outer[None]

time: 243 us -> 270 us (1.11)
  blocking collectives: 156 us -> 0 us
  waiting for transfers between devices: 44.1 us -> 156 us
  starting transfers between devices: 17.7 us -> 73.2 us
  between operations: 2.92 us -> 14.9 us
  other arithmetic: 7.49 us -> 10.6 us
  matrix products: 3.32 us -> 6.29 us
    all_to_all x2 -> x0, blocking collectives: 88.5 us -> none  [the longest x1 70.8 us: shards(): lax.all_to_all(column_part.astype(bf16).reshape(nz, BLOCK // nz, width),...]
    psum x1 -> x0, blocking collectives: 67.7 us -> none  [shards(): layer_sq = lax.psum(grad_sq, ('y', 'tensor'))]
    all_gather x0 -> x1, waiting for transfers between devices: none -> 50.6 us  [shards(): lax.all_gather(got[:, BLOCK:].reshape(ny * mine, BLOCK), 'z', axis=0, til...]
    all_to_all x0 -> x1, waiting for transfers between devices: none -> 36.5 us  [shards(): lax.all_to_all(column_part.astype(bf16).reshape(nz, BLOCK // nz, width),...]
    all_to_all x0 -> x1, starting transfers between devices: none -> 33.2 us  [shards(): lax.all_to_all(column_part.astype(bf16).reshape(nz, BLOCK // nz, width),...]
    all_to_all x2, starting transfers between devices: 12.7 us -> 31.4 us  [everyone(): lax.all_to_all(jnp.broadcast_to(piece[None], (count, *piece.shape)), axis...]
    all_to_all x1 -> x2, waiting for transfers between devices: 8.57 us -> 22.2 us  [shards(): got = lax.all_to_all(sent, 'y', 0, 0, tiled=True)]
    all_to_all x2, waiting for transfers between devices: 35.5 us -> 46.9 us  [everyone(): lax.all_to_all(jnp.broadcast_to(piece[None], (count, *piece.shape)), axis...]
  transfers between devices with their start and end apart: 3 -> 6, of which waited for: 2 -> 6; matrix products, arithmetic and copies ran while one was open for 2% -> 2% of each run, Pallas kernels for 0% -> 0%
where the time goes in v2:
time: 270 us; the launch traced here: 269 us
  waiting for transfers between devices  156 us (58%)
  starting transfers between devices  73.2 us (27%)
  between operations  14.9 us (6%)
  other arithmetic  10.6 us (4%)
  local copies, waits for them, and re-layouts  7.75 us (3%)
  matrix products  6.29 us (2%)
    all_gather x1, waiting for transfers between devices, shards(): lax.all_gather(got[:, BLOCK:].reshape(ny * mine, BLOCK), 'z', axis=0, til...  50.6 us
    all_to_all x2, waiting for transfers between devices, everyone(): lax.all_to_all(jnp.broadcast_to(piece[None], (count, *piece.shape)), axis...  46.9 us
    all_to_all x1, waiting for transfers between devices, shards(): lax.all_to_all(column_part.astype(bf16).reshape(nz, BLOCK // nz, width),...  36.5 us
    all_to_all x1, starting transfers between devices, shards(): lax.all_to_all(column_part.astype(bf16).reshape(nz, BLOCK // nz, width),...  33.2 us
    all_to_all x2, starting transfers between devices, everyone(): lax.all_to_all(jnp.broadcast_to(piece[None], (count, *piece.shape)), axis...  31.4 us
    all_to_all x2, waiting for transfers between devices, shards(): got = lax.all_to_all(sent, 'y', 0, 0, tiled=True)  22.2 us
    all_to_all x2, starting transfers between devices, shards(): got = lax.all_to_all(sent, 'y', 0, 0, tiled=True)  8.54 us
  transfers between devices with their start and end apart: 6, of which 6 were waited for; matrix products, arithmetic and copies ran while one was open for 2% of the time, Pallas kernels for 0%

profile of v2, /device:TPU:1, one launch (start us, length us, event | category | flops | bytes accessed | tf_op | source)
XLA Modules:
  0.0 269.1 jit_solution(10426144808521427111)
XLA Ops:
  7.2 0.0 copy-start
  7.2 1.6 copy-done
  8.8 1.6 fusion.7
  10.4 0.0 copy-start.1
  10.4 0.0 copy-start.2
  10.4 1.3 copy-done.1
  11.7 0.1 convert_element_type.47
  11.9 0.0 copy-done.2
  11.9 1.1 pad_maximum_fusion.1
  13.0 5.0 %all-to-all-start = ((bf16[4,1088,128]{2,1,0:T(8,128)(2,1)}), bf16[4,1088,128]{2,1,0:T(8,128)(2,1)S(1)}, u32[]{:S(2)}, u32[]{:S(2)}) async-start(bf16[4,1088,128]{2,1,0:T(8,128)(2,1)} %pad_maximum_fusion.1), calls=%async_computation | async-start | bytes 2228224 | tf_op jit(solution)/shard_map/all_to_all | solution.py:37
  18.0 1.9 constant_dynamic-slice_fusion
  19.9 8.2 %all-to-all-done = bf16[4,1088,128]{2,1,0:T(8,128)(2,1)S(1)} async-done(((bf16[4,1088,128]{2,1,0:T(8,128)(2,1)}), bf16[4,1088,128]{2,1,0:T(8,128)(2,1)S(1)}, u32[]{:S(2)}, u32[]{:S(2)}) %all-to-all-start) | async-done | bytes 1114144 | tf_op jit(solution)/shard_map/all_to_all | solution.py:37
  28.1 0.3 select_reduce_fusion
  28.4 1.9 add_convert_fusion
  30.3 33.2 %all-to-all-start.1 = ((bf16[32,32,128]{2,1,0:T(8,128)(2,1)}), bf16[32,32,128]{2,1,0:T(8,128)(2,1)S(1)}, u32[]{:S(2)}, u32[]{:S(2)}) async-start(bf16[32,32,128]{2,1,0:T(8,128)(2,1)} %add_convert_fusion), calls=%async_computation.1 | async-start | bytes 524288 | tf_op jit(solution)/shard_map/all_to_all | solution.py:43
  63.5 0.0 all-gather.2.cloned.1.call-start
  63.6 0.7 reshape.91
  64.3 0.0 all-gather.2.cloned.1.call-update
  64.3 36.5 %all-to-all-done.1 = bf16[32,32,128]{2,1,0:T(8,128)(2,1)S(1)} async-done(((bf16[32,32,128]{2,1,0:T(8,128)(2,1)}), bf16[32,32,128]{2,1,0:T(8,128)(2,1)S(1)}, u32[]{:S(2)}, u32[]{:S(2)}) %all-to-all-start.1) | async-done | bytes 262176 | tf_op jit(solution)/shard_map/all_to_all | solution.py:43
  100.8 0.1 reduce_sum.52
  100.9 0.7 broadcast_in_dim.46
  101.6 7.0 %all-to-all-start.2 = ((bf16[32,32,128]{2,1,0:T(8,128)(2,1)}), bf16[32,32,128]{2,1,0:T(8,128)(2,1)S(1)}, u32[]{:S(2)}, u32[]{:S(2)}) async-start(bf16[32,32,128]{2,1,0:T(8,128)(2,1)} %broadcast_in_dim.46), calls=%async_computation.2 | async-start | bytes 524288 | tf_op jit(solution)/shard_map/all_to_all | solution.py:14
  108.6 41.3 %all-to-all-done.2 = bf16[32,32,128]{2,1,0:T(8,128)(2,1)S(1)} async-done(((bf16[32,32,128]{2,1,0:T(8,128)(2,1)}), bf16[32,32,128]{2,1,0:T(8,128)(2,1)S(1)}, u32[]{:S(2)}, u32[]{:S(2)}) %all-to-all-start.2) | async-done | bytes 262176 | tf_op jit(solution)/shard_map/all_to_all | solution.py:14
  149.9 50.6 %all-gather.2.cloned.1.call-done = bf16[1024,1024]{1,0:T(8,128)(2,1)} async-done(((bf16[32,1024]{1,0:T(8,128)(2,1)}), bf16[1024,1024]{1,0:T(8,128)(2,1)}) %all-gather.2.cloned.1.call-update) | async-done | bytes 2097168 | tf_op jit(solution)/shard_map/all_gather | solution.py:38
  200.5 2.3 fusion.8
  202.8 2.0 multiply_reduce_fusion
  204.8 0.7 multiply_reduce_fusion.1
  205.5 1.3 compare_select_fusion
  206.8 0.7 broadcast_in_dim_broadcast_in_dim_broadcast_in_dim.2
  207.6 24.4 %all-to-all-start.4 = ((f32[32,8,128]{2,1,0:T(8,128)}), f32[32,8,128]{2,1,0:T(8,128)S(1)}, u32[]{:S(2)}, u32[]{:S(2)}) async-start(f32[32,8,128]{2,1,0:T(8,128)} %broadcast_in_dim_broadcast_in_dim_broadcast_in_dim.2), calls=%async_computation.4 | async-start | bytes 262144 | tf_op jit(solution)/shard_map/all_to_all | solution.py:14
  232.0 0.2 convolution_convert_fusion.1
  232.1 0.1 reshape.95
  232.2 0.1 copy.16
  232.4 0.2 fusion.9
  232.7 0.1 broadcast_in_dim.48
  232.8 1.1 pad_maximum_fusion
  233.9 0.0 copy-start.3
  233.9 5.7 %all-to-all-done.4 = f32[32,8,128]{2,1,0:T(8,128)S(1)} async-done(((f32[32,8,128]{2,1,0:T(8,128)}), f32[32,8,128]{2,1,0:T(8,128)S(1)}, u32[]{:S(2)}, u32[]{:S(2)}) %all-to-all-start.4) | async-done | bytes 131104 | tf_op jit(solution)/shard_map/all_to_all | solution.py:14
  239.6 3.5 %all-to-all-start.3 = ((bf16[4,1104,128]{2,1,0:T(8,128)(2,1)}), bf16[4,1104,128]{2,1,0:T(8,128)(2,1)S(1)}, u32[]{:S(2)}, u32[]{:S(2)}) async-start(bf16[4,1104,128]{2,1,0:T(8,128)(2,1)} %pad_maximum_fusion), calls=%async_computation.3 | async-start | bytes 2260992 | tf_op jit(solution)/shard_map/all_to_all | solution.py:72
  243.1 0.1 copy.17
  243.2 0.1 reshape_squeeze.3
  243.3 0.6 slice_reduce_fusion
  244.6 0.2 dynamic-slice_reduce_fusion
  244.8 14.0 %all-to-all-done.3 = bf16[4,1104,128]{2,1,0:T(8,128)(2,1)S(1)} async-done(((bf16[4,1104,128]{2,1,0:T(8,128)(2,1)}), bf16[4,1104,128]{2,1,0:T(8,128)(2,1)S(1)}, u32[]{:S(2)}, u32[]{:S(2)}) %all-to-all-start.3) | async-done | bytes 1130528 | tf_op jit(solution)/shard_map/all_to_all | solution.py:72
  258.8 1.6 multiply_add_fusion
  260.4 0.0 copy-done.3
  260.4 0.6 multiply_add_fusion.1
  261.0 1.2 multiply_convert_fusion
  (13 shorter events, 0.2 us)
Async XLA Ops:
  7.2 1.6 copy-start
  10.4 1.3 copy-start.1
  10.4 1.5 copy-start.2
  13.0 15.1 %all-to-all-start = ((bf16[4,1088,128]{2,1,0:T(8,128)(2,1)}), bf16[4,1088,128]{2,1,0:T(8,128)(2,1)S(1)}, u32[]{:S(2)}, u32[]{:S(2)}) async-start(bf16[4,1088,128]{2,1,0:T(8,128)(2,1)} %pad_maximum_fusion.1), calls=%async_computation | async-start | bytes 2228224 | tf_op jit(solution)/shard_map/all_to_all | solution.py:37
  30.3 70.5 %all-to-all-start.1 = ((bf16[32,32,128]{2,1,0:T(8,128)(2,1)}), bf16[32,32,128]{2,1,0:T(8,128)(2,1)S(1)}, u32[]{:S(2)}, u32[]{:S(2)}) async-start(bf16[32,32,128]{2,1,0:T(8,128)(2,1)} %add_convert_fusion), calls=%async_computation.1 | async-start | bytes 524288 | tf_op jit(solution)/shard_map/all_to_all | solution.py:43
  63.5 137.0 %all-gather.2.cloned.1.call-start = ((), (), s32[]{:S(2)}) async-start(), calls=%async_computation.5 | async-start | bytes 2162688 | tf_op jit(solution)/shard_map/all_gather | solution.py:38
  101.6 48.3 %all-to-all-start.2 = ((bf16[32,32,128]{2,1,0:T(8,128)(2,1)}), bf16[32,32,128]{2,1,0:T(8,128)(2,1)S(1)}, u32[]{:S(2)}, u32[]{:S(2)}) async-start(bf16[32,32,128]{2,1,0:T(8,128)(2,1)} %broadcast_in_dim.46), calls=%async_computation.2 | async-start | bytes 524288 | tf_op jit(solution)/shard_map/all_to_all | solution.py:14
  207.6 32.0 %all-to-all-start.4 = ((f32[32,8,128]{2,1,0:T(8,128)}), f32[32,8,128]{2,1,0:T(8,128)S(1)}, u32[]{:S(2)}, u32[]{:S(2)}) async-start(f32[32,8,128]{2,1,0:T(8,128)} %broadcast_in_dim_broadcast_in_dim_broadcast_in_dim.2), calls=%async_computation.4 | async-start | bytes 262144 | tf_op jit(solution)/shard_map/all_to_all | solution.py:14
  233.9 26.5 %copy-start.3 = (f32[1,4,1,128]{3,2,1,0:T(1,128)S(1)}, f32[1,4,1,128]{3,2,1,0:T(1,128)}, u32[]{:S(2)}) copy-start(f32[1,4,1,128]{3,2,1,0:T(1,128)} %param.9) | copy-start | bytes 6148
  239.6 19.2 %all-to-all-start.3 = ((bf16[4,1104,128]{2,1,0:T(8,128)(2,1)}), bf16[4,1104,128]{2,1,0:T(8,128)(2,1)S(1)}, u32[]{:S(2)}, u32[]{:S(2)}) async-start(bf16[4,1104,128]{2,1,0:T(8,128)(2,1)} %pad_maximum_fusion), calls=%async_computation.3 | async-start | bytes 2260992 | tf_op jit(solution)/shard_map/all_to_all | solution.py:72
Sparse Core Ops, SparseCore 0:
  67.6 132.8 all-gather.1

commit v3 on v2

v3 whole, which is shorter than its diff:
```python
import jax
import jax.numpy as jnp
from jax import lax
from jax.sharding import Mesh, PartitionSpec as P

BLOCK = 1024
stat_decay = 0.95
highest = lax.Precision.HIGHEST
f32 = jnp.float32
bf16 = jnp.bfloat16
Z = ("far", "near")


def swap(pieces, axis):
    return lax.all_to_all(pieces, axis, 0, 0, tiled=True)


def everyone(piece, axis):
    return swap(jnp.broadcast_to(piece[None], (lax.axis_size(axis), *piece.shape)), axis)


def thirds(value):
    parts = []
    for _ in range(3):
        part = lax.reduce_precision(value, 8, 7)
        parts.append(part.astype(bf16))
        value = value - part
    return parts


def shards(activations, cotangents, left_stats, right_stats, left_roots, right_roots):
    ny = lax.axis_size("y")
    nfar = lax.axis_size("far")
    nnear = lax.axis_size("near")
    nz = nfar * nnear
    tensors = lax.axis_size("tensor")
    y = lax.axis_index("y")
    z = lax.axis_index(Z)
    features = activations.shape[1]
    width = cotangents.shape[1]
    blocks = features // BLOCK
    mine = left_roots.shape[2]
    root_rows = mine * (BLOCK // width)

    partial = lax.dot_general(
        activations, cotangents, (((0,), (0,)), ((), ())), preferred_element_type=f32
    ).reshape(blocks, BLOCK, width)
    roots = left_roots[0].astype(bf16).reshape(blocks, root_rows, width)
    got = swap(jnp.concatenate([partial.astype(bf16), roots], axis=1), "y")
    roots = got[:, BLOCK:].reshape(ny * mine, BLOCK)
    kept = lax.dynamic_index_in_dim(partial, y, 0, keepdims=False)
    others = jnp.where((jnp.arange(ny) == y)[:, None, None], 0.0, got[:, :BLOCK].astype(f32))
    column_part = kept + jnp.sum(others, axis=0)

    got = swap(column_part.astype(bf16).reshape(nnear, BLOCK // nnear, width), "near")
    got = everyone(jnp.sum(got.astype(f32), axis=0).astype(bf16), "far")
    own = jnp.sum(got.astype(f32), axis=0).astype(bf16)
    gradient = everyone(own, "near").reshape(BLOCK, width)

    inner = lax.dot_general(
        gradient, gradient, (((0,), (0,)), ((), ())), preferred_element_type=f32
    )
    wide = gradient.astype(f32)
    grad_sq = jnp.sum(wide * wide)
    block_sq = lax.psum(grad_sq, "tensor")

    right = lax.dynamic_index_in_dim(right_roots[0], y, 0, keepdims=False)
    mixed = jnp.dot(roots, gradient, preferred_element_type=f32)
    direction = jnp.dot(mixed, right, precision=highest).astype(bf16)
    direction = everyone(direction, Z).reshape(nz, ny, mine, width)
    direction = direction.transpose(1, 0, 2, 3).reshape(BLOCK, width)
    wide = direction.astype(f32)
    dir_sq = jnp.sum(wide * wide)

    rows = lax.dynamic_index_in_dim(gradient.reshape(ny, nz, mine, width), z, 1, keepdims=False)
    outer = lax.dot_general(
        rows.reshape(ny * mine, width), gradient, (((1,), (1,)), ((), ())), preferred_element_type=f32
    )
    outer = outer.astype(bf16).reshape(ny, root_rows, width)
    inner = lax.dynamic_index_in_dim(inner.reshape(ny, nz, width), z, 1, keepdims=True).astype(bf16)
    line = jnp.arange(16)[:, None]
    scalars = thirds(jnp.sqrt(grad_sq / dir_sq)) + thirds(block_sq)
    extra = jnp.broadcast_to(inner, (ny, 16, width))
    for place, scalar in enumerate(scalars, 1):
        extra = jnp.where(line == place, scalar, extra)
    got = swap(
        jnp.concatenate(
            [jnp.broadcast_to(direction[None], (ny, BLOCK, width)), outer, extra], axis=1
        ),
        "y",
    )
    extra = got[:, BLOCK + root_rows :].astype(f32)
    ratio = jnp.sum(extra[:, 1:4, 0], axis=1)
    layer_sq = jnp.sum(extra[:, 4:7, 0])
    factor = ratio / jnp.sqrt(layer_sq / (features * width * tensors))
    update = (got[:, :BLOCK].astype(f32) * factor[:, None, None]).astype(bf16)
    update = update.reshape(blocks * BLOCK, width)
    outer = got[:, BLOCK : BLOCK + root_rows].astype(f32).reshape(blocks, mine, BLOCK)
    left_new = stat_decay * left_stats + ((1.0 - stat_decay) / width) * outer[None]
    right_new = stat_decay * right_stats + ((1.0 - stat_decay) / BLOCK) * extra[None, :, :1]
    return (update, left_new, right_new)


def solution(mesh):
    dp, tensor = mesh.devices.shape
    blocks, near = 4, 8
    fine = Mesh(
        mesh.devices.reshape(blocks, dp // (blocks * near), near, tensor),
        ("y", "far", "near", "tensor"),
    )
    dp = ("y", *Z)
    in_specs = (
        P(dp, None),
        P(dp, "tensor"),
        P("tensor", None, dp, None),
        P("tensor", None, dp, None),
        P("tensor", None, dp, None),
        P("tensor", None, None, None),
    )
    out_specs = (P(None, "tensor"), P("tensor", None, dp, None), P("tensor", None, dp, None))
    return jax.shard_map(shards, mesh=fine, in_specs=in_specs, out_specs=out_specs, check_vma=False)
```

time: 270 us -> 199 us (0.74)
  the two profiles are of different devices: /device:TPU:1 before, /device:TPU:2 now
where the time goes in v3:
time: 199 us; the launch traced here: 198 us
  blocking collectives  99 us (50%)
  waiting for transfers between devices  47.7 us (24%)
  starting transfers between devices  18.9 us (9%)
  between operations  12.7 us (6%)
  other arithmetic  9.73 us (5%)
  local copies, waits for them, and re-layouts  6.81 us (3%)
  matrix products  3.15 us (2%)
    all_to_all x3, blocking collectives, swap(): return lax.all_to_all(pieces, axis, 0, 0, tiled=True)  87.8 us
    all_to_all x3, waiting for transfers between devices, swap(): return lax.all_to_all(pieces, axis, 0, 0, tiled=True)  47.7 us
    all_to_all x3, starting transfers between devices, swap(): return lax.all_to_all(pieces, axis, 0, 0, tiled=True)  18.9 us
    psum x1, blocking collectives, shards(): block_sq = lax.psum(grad_sq, 'tensor')  11.2 us
  transfers between devices with their start and end apart: 3, of which 3 were waited for; matrix products, arithmetic and copies ran while one was open for 2% of the time, Pallas kernels for 0%

profile of v3, /device:TPU:2, one launch (start us, length us, event | category | flops | bytes accessed | tf_op | source)
XLA Modules:
  0.0 198.0 jit_solution(3255850054075953573)
XLA Ops:
  0.6 0.0 copy-start
  0.6 1.6 copy-done
  2.2 1.6 fusion.6
  3.8 0.0 copy-start.1
  3.8 0.0 copy-start.2
  3.9 1.3 copy-done.1
  5.2 0.1 convert_element_type.68
  5.3 0.0 copy-done.2
  5.4 1.1 pad_maximum_fusion.1
  6.5 4.5 %all-to-all-start = ((bf16[4,1088,128]{2,1,0:T(8,128)(2,1)}), bf16[4,1088,128]{2,1,0:T(8,128)(2,1)S(1)}, u32[]{:S(2)}, u32[]{:S(2)}) async-start(bf16[4,1088,128]{2,1,0:T(8,128)(2,1)} %pad_maximum_fusion.1), calls=%async_computation | async-start | bytes 2228224 | tf_op jit(solution)/shard_map/all_to_all | solution.py:15
  11.0 1.9 constant_dynamic-slice_fusion
  12.8 13.9 %all-to-all-done = bf16[4,1088,128]{2,1,0:T(8,128)(2,1)S(1)} async-done(((bf16[4,1088,128]{2,1,0:T(8,128)(2,1)}), bf16[4,1088,128]{2,1,0:T(8,128)(2,1)S(1)}, u32[]{:S(2)}, u32[]{:S(2)}) %all-to-all-start) | async-done | bytes 1114144 | tf_op jit(solution)/shard_map/all_to_all | solution.py:15
  26.7 0.3 select_reduce_fusion
  27.1 1.1 add_convert_fusion
  28.2 27.8 %all_to_all.30 = bf16[8,128,128]{2,1,0:T(8,128)(2,1)S(1)} all-to-all(bf16[8,128,128]{2,1,0:T(8,128)(2,1)S(1)} %add_convert_fusion), channel_id=1, replica_groups=mesh['y'=4,'far'=4,'near'=8,'tensor'=8] {'near'}, dimensions={0} | all-to-all | bytes 524288 | tf_op jit(solution)/shard_map/all_to_all | solution.py:15
  56.0 46.2 %all_to_all.31 = bf16[4,128,128]{2,1,0:T(8,128)(2,1)S(1)} all-to-all(bf16[4,128,128]{2,1,0:T(8,128)(2,1)S(1)} %broadcast_in_dim.102), channel_id=1, replica_groups=mesh['y'=4,'far'=4,'near'=8,'tensor'=8] {'far'}, dimensions={0} | all-to-all | bytes 262144 | tf_op jit(solution)/shard_map/all_to_all | solution.py:15
  102.3 0.7 broadcast_in_dim.103
  103.1 7.4 %all-to-all-start.3 = ((bf16[8,128,128]{2,1,0:T(8,128)(2,1)}), bf16[8,128,128]{2,1,0:T(8,128)(2,1)S(1)}, u32[]{:S(2)}, u32[]{:S(2)}) async-start(bf16[8,128,128]{2,1,0:T(8,128)(2,1)} %broadcast_in_dim.103), calls=%async_computation.3 | async-start | bytes 524288 | tf_op jit(solution)/shard_map/all_to_all | solution.py:15
  110.5 13.0 %all-to-all-done.3 = bf16[8,128,128]{2,1,0:T(8,128)(2,1)S(1)} async-done(((bf16[8,128,128]{2,1,0:T(8,128)(2,1)}), bf16[8,128,128]{2,1,0:T(8,128)(2,1)S(1)}, u32[]{:S(2)}, u32[]{:S(2)}) %all-to-all-start.3) | async-done | bytes 262176 | tf_op jit(solution)/shard_map/all_to_all | solution.py:15
  123.5 0.2 fusion.7
  123.7 1.0 convolution_convert_fusion.1
  124.7 0.7 broadcast_in_dim.104
  125.4 7.0 %all-to-all-start.4 = ((bf16[32,32,128]{2,1,0:T(8,128)(2,1)}), bf16[32,32,128]{2,1,0:T(8,128)(2,1)S(1)}, u32[]{:S(2)}, u32[]{:S(2)}) async-start(bf16[32,32,128]{2,1,0:T(8,128)(2,1)} %broadcast_in_dim.104), calls=%async_computation.4 | async-start | bytes 524288 | tf_op jit(solution)/shard_map/all_to_all | solution.py:15
  132.5 0.7 multiply_reduce_fusion.1
  133.2 11.2 %psum.7 = f32[]{:T(128)} all-reduce(f32[]{:T(128)} %multiply_reduce_fusion.1), channel_id=1, replica_groups=mesh['y'=4,'far'=4,'near'=8,'tensor'=8] {'tensor'}, use_global_device_ids=true, to_apply=%region_4.5 | all-reduce | flops 1 | bytes 8 | tf_op jit(solution)/shard_map/psum | solution.py:65
  150.1 0.1 copy.19
  150.2 0.2 fusion.8
  150.5 0.2 convolution_convert_fusion
  150.7 0.1 reshape.107
  150.7 20.8 %all-to-all-done.4 = bf16[32,32,128]{2,1,0:T(8,128)(2,1)S(1)} async-done(((bf16[32,32,128]{2,1,0:T(8,128)(2,1)}), bf16[32,32,128]{2,1,0:T(8,128)(2,1)S(1)}, u32[]{:S(2)}, u32[]{:S(2)}) %all-to-all-start.4) | async-done | bytes 262176 | tf_op jit(solution)/shard_map/all_to_all | solution.py:15
  171.6 0.7 multiply_reduce_fusion
  177.9 1.4 select_select_fusion
  179.3 0.1 broadcast_in_dim.106
  179.4 0.1 pad_maximum_fusion
  179.5 0.0 copy-start.3
  179.5 13.7 %all_to_all.32 = bf16[4,1104,128]{2,1,0:T(8,128)(2,1)S(1)} all-to-all(bf16[4,1104,128]{2,1,0:T(8,128)(2,1)S(1)} %pad_maximum_fusion), channel_id=1, replica_groups=mesh['y'=4,'far'=4,'near'=8,'tensor'=8] {'y'}, dimensions={0} | all-to-all | bytes 2260992 | tf_op jit(solution)/shard_map/all_to_all | solution.py:15
  193.3 0.6 slice_reduce_fusion
  194.6 1.6 multiply_add_fusion
  196.2 0.0 copy-done.3
  196.2 0.6 multiply_add_fusion.1
  196.8 1.2 multiply_convert_fusion
  (19 shorter events, 0.3 us)
Async XLA Ops:
  0.6 1.6 copy-start
  3.8 1.4 copy-start.1
  3.8 1.5 copy-start.2
  6.5 20.3 %all-to-all-start = ((bf16[4,1088,128]{2,1,0:T(8,128)(2,1)}), bf16[4,1088,128]{2,1,0:T(8,128)(2,1)S(1)}, u32[]{:S(2)}, u32[]{:S(2)}) async-start(bf16[4,1088,128]{2,1,0:T(8,128)(2,1)} %pad_maximum_fusion.1), calls=%async_computation | async-start | bytes 2228224 | tf_op jit(solution)/shard_map/all_to_all | solution.py:15
  103.1 20.4 %all-to-all-start.3 = ((bf16[8,128,128]{2,1,0:T(8,128)(2,1)}), bf16[8,128,128]{2,1,0:T(8,128)(2,1)S(1)}, u32[]{:S(2)}, u32[]{:S(2)}) async-start(bf16[8,128,128]{2,1,0:T(8,128)(2,1)} %broadcast_in_dim.103), calls=%async_computation.3 | async-start | bytes 524288 | tf_op jit(solution)/shard_map/all_to_all | solution.py:15
  125.4 46.1 %all-to-all-start.4 = ((bf16[32,32,128]{2,1,0:T(8,128)(2,1)}), bf16[32,32,128]{2,1,0:T(8,128)(2,1)S(1)}, u32[]{:S(2)}, u32[]{:S(2)}) async-start(bf16[32,32,128]{2,1,0:T(8,128)(2,1)} %broadcast_in_dim.104), calls=%async_computation.4 | async-start | bytes 524288 | tf_op jit(solution)/shard_map/all_to_all | solution.py:15
  179.5 16.7 %copy-start.3 = (f32[1,4,1,128]{3,2,1,0:T(1,128)S(1)}, f32[1,4,1,128]{3,2,1,0:T(1,128)}, u32[]{:S(2)}) copy-start(f32[1,4,1,128]{3,2,1,0:T(1,128)} %param.9) | copy-start | bytes 6148

commit v4 on v3

--- a/solution.py
+++ b/solution.py
@@ -52,25 +52,43 @@
     others = jnp.where((jnp.arange(ny) == y)[:, None, None], 0.0, got[:, :BLOCK].astype(f32))
     column_part = kept + jnp.sum(others, axis=0)
 
-    got = swap(column_part.astype(bf16).reshape(nnear, BLOCK // nnear, width), "near")
-    got = everyone(jnp.sum(got.astype(f32), axis=0).astype(bf16), "far")
+    far = lax.axis_index("far")
+    held = [roots]
+
+    def step(operand, transfer):
+        operand, block = lax.optimization_barrier((operand, roots))
+        turn = [(i, (i + len(held)) % nfar) for i in range(nfar)]
+        held.append(lax.ppermute(block, "far", turn))
+        got = transfer(operand)
+        if len(held) > 2:
+            got, held[-2] = lax.optimization_barrier((got, held[-2]))
+        return got
+
+    pieces = column_part.astype(bf16).reshape(nnear, BLOCK // nnear, width)
+    got = step(pieces, lambda pieces: swap(pieces, "near"))
+    part = jnp.sum(got.astype(f32), axis=0).astype(bf16)
+    got = step(part, lambda part: everyone(part, "far"))
     own = jnp.sum(got.astype(f32), axis=0).astype(bf16)
-    gradient = everyone(own, "near").reshape(BLOCK, width)
+    gradient = step(own, lambda own: everyone(own, "near")).reshape(BLOCK, width)
+    roots = jnp.concatenate(held, axis=0)
 
     inner = lax.dot_general(
         gradient, gradient, (((0,), (0,)), ((), ())), preferred_element_type=f32
     )
     wide = gradient.astype(f32)
-    grad_sq = jnp.sum(wide * wide)
+    grad_sq = jnp.sum(wide * wide, axis=0)
     block_sq = lax.psum(grad_sq, "tensor")
 
     right = lax.dynamic_index_in_dim(right_roots[0], y, 0, keepdims=False)
     mixed = jnp.dot(roots, gradient, preferred_element_type=f32)
-    direction = jnp.dot(mixed, right, precision=highest).astype(bf16)
-    direction = everyone(direction, Z).reshape(nz, ny, mine, width)
-    direction = direction.transpose(1, 0, 2, 3).reshape(BLOCK, width)
+    direction = jnp.dot(mixed, right, precision=highest).reshape(1, nfar, ny * mine, width)
+    steps = jnp.arange(nfar)
+    turned = (far - steps[:, None]) % nfar == steps[None, :]
+    direction = jnp.sum(jnp.where(turned[:, :, None, None], direction, 0.0), axis=1).astype(bf16)
+    direction = everyone(direction, "near").reshape(nnear, nfar, ny, mine, width)
+    direction = direction.transpose(2, 1, 0, 3, 4).reshape(BLOCK, width)
     wide = direction.astype(f32)
-    dir_sq = jnp.sum(wide * wide)
+    dir_sq = jnp.sum(wide * wide, axis=0)
 
     rows = lax.dynamic_index_in_dim(gradient.reshape(ny, nz, mine, width), z, 1, keepdims=False)
     outer = lax.dot_general(
@@ -79,10 +97,9 @@
     outer = outer.astype(bf16).reshape(ny, root_rows, width)
     inner = lax.dynamic_index_in_dim(inner.reshape(ny, nz, width), z, 1, keepdims=True).astype(bf16)
     line = jnp.arange(16)[:, None]
-    scalars = thirds(jnp.sqrt(grad_sq / dir_sq)) + thirds(block_sq)
     extra = jnp.broadcast_to(inner, (ny, 16, width))
-    for place, scalar in enumerate(scalars, 1):
-        extra = jnp.where(line == place, scalar, extra)
+    for place, values in enumerate(thirds(grad_sq) + thirds(dir_sq) + thirds(block_sq), 1):
+        extra = jnp.where(line == place, values, extra)
     got = swap(
         jnp.concatenate(
             [jnp.broadcast_to(direction[None], (ny, BLOCK, width)), outer, extra], axis=1
@@ -90,10 +107,12 @@
         "y",
     )
     extra = got[:, BLOCK + root_rows :].astype(f32)
-    ratio = jnp.sum(extra[:, 1:4, 0], axis=1)
-    layer_sq = jnp.sum(extra[:, 4:7, 0])
-    factor = ratio / jnp.sqrt(layer_sq / (features * width * tensors))
-    update = (got[:, :BLOCK].astype(f32) * factor[:, None, None]).astype(bf16)
+    grad_sq, dir_sq, block_sq = (
+        jnp.sum(extra[:, 1 + 3 * n : 4 + 3 * n], axis=(1, 2), keepdims=True) for n in range(3)
+    )
+    layer_sq = jnp.sum(block_sq, axis=0, keepdims=True)
+    factor = jnp.sqrt(grad_sq / dir_sq) / jnp.sqrt(layer_sq / (features * width * tensors))
+    update = (got[:, :BLOCK].astype(f32) * factor).astype(bf16)
     update = update.reshape(blocks * BLOCK, width)
     outer = got[:, BLOCK : BLOCK + root_rows].astype(f32).reshape(blocks, mine, BLOCK)
     left_new = stat_decay * left_stats + ((1.0 - stat_decay) / width) * outer[None]

time: 199 us -> 206 us (1.035)
  the two profiles are of different devices: /device:TPU:2 before, /device:TPU:34 now
where the time goes in v4:
time: 206 us; the launch traced here: 205 us
  starting transfers between devices  83 us (40%)
  blocking collectives  56.4 us (27%)
  waiting for transfers between devices  45.8 us (22%)
  local copies, waits for them, and re-layouts  7.48 us (4%)
  other arithmetic  7.48 us (4%)
  matrix products  3.25 us (2%)
    all_to_all x4, starting transfers between devices, swap(): return lax.all_to_all(pieces, axis, 0, 0, tiled=True)  50.8 us
    all_to_all x2, blocking collectives, swap(): return lax.all_to_all(pieces, axis, 0, 0, tiled=True)  45 us
    ppermute x3, starting transfers between devices, step(): held.append(lax.ppermute(block, 'far', turn))  32.3 us
    ppermute x3, waiting for transfers between devices, step(): held.append(lax.ppermute(block, 'far', turn))  23.5 us
    all_to_all x4, waiting for transfers between devices, swap(): return lax.all_to_all(pieces, axis, 0, 0, tiled=True)  22.3 us
    psum x1, blocking collectives, shards(): block_sq = lax.psum(grad_sq, 'tensor')  11.4 us
  transfers between devices with their start and end apart: 7, of which 6 were waited for; matrix products, arithmetic and copies ran while one was open for 1% of the time, Pallas kernels for 0%

profile of v4, /device:TPU:34, one launch (start us, length us, event | category | flops | bytes accessed | tf_op | source)
XLA Modules:
  0.0 205.0 jit_solution(7878566363909936348)
XLA Ops:
  0.6 0.0 copy-start
  0.6 1.6 copy-done
  2.2 1.6 fusion.14
  3.8 0.0 copy-start.1
  3.8 0.0 copy-start.2
  3.9 1.3 copy-done.1
  5.2 0.1 convert_element_type.81
  5.3 0.0 copy-done.2
  5.4 1.1 pad_maximum_fusion.1
  6.5 4.5 %all-to-all-start = ((bf16[4,1088,128]{2,1,0:T(8,128)(2,1)}), bf16[4,1088,128]{2,1,0:T(8,128)(2,1)S(1)}, u32[]{:S(2)}, u32[]{:S(2)}) async-start(bf16[4,1088,128]{2,1,0:T(8,128)(2,1)} %pad_maximum_fusion.1), calls=%async_computation | async-start | bytes 2228224 | tf_op jit(solution)/shard_map/all_to_all | solution.py:15
  11.0 1.9 constant_dynamic-slice_fusion
  12.8 13.9 %all-to-all-done = bf16[4,1088,128]{2,1,0:T(8,128)(2,1)S(1)} async-done(((bf16[4,1088,128]{2,1,0:T(8,128)(2,1)}), bf16[4,1088,128]{2,1,0:T(8,128)(2,1)S(1)}, u32[]{:S(2)}, u32[]{:S(2)}) %all-to-all-start) | async-done | bytes 1114144 | tf_op jit(solution)/shard_map/all_to_all | solution.py:15
  26.8 0.3 select_reduce_fusion
  27.1 1.1 add_convert_fusion
  28.2 27.5 %all_to_all.30 = bf16[8,128,128]{2,1,0:T(8,128)(2,1)S(1)} all-to-all(bf16[8,128,128]{2,1,0:T(8,128)(2,1)S(1)} %add_convert_fusion), channel_id=1, replica_groups=mesh['y'=4,'far'=4,'near'=8,'tensor'=8] {'near'}, dimensions={0} | all-to-all | bytes 524288 | tf_op jit(solution)/shard_map/all_to_all | solution.py:15
  55.8 0.7 broadcast_in_dim.153
  56.4 20.8 %all-to-all-start.2 = ((bf16[4,128,128]{2,1,0:T(8,128)(2,1)}), bf16[4,128,128]{2,1,0:T(8,128)(2,1)S(1)}, u32[]{:S(2)}, u32[]{:S(2)}) async-start(bf16[4,128,128]{2,1,0:T(8,128)(2,1)} %broadcast_in_dim.153), calls=%async_computation.2 | async-start | bytes 262144 | tf_op jit(solution)/shard_map/all_to_all | solution.py:15
  77.3 12.6 %collective-permute-start = (bf16[32,1024]{1,0:T(8,128)(2,1)S(1)}, bf16[32,1024]{1,0:T(8,128)(2,1)S(1)}, u32[]{:S(2)}, u32[]{:S(2)}) collective-permute-start(bf16[32,1024]{1,0:T(8,128)(2,1)S(1)} %reshape.181), channel_id=1, source_target_pairs={{0,64},{64,128},{128,192},{192,0},{1,65},{65,129},{129,193},{193,1... | collective-permute-start | bytes 196616 | tf_op jit(solution)/shard_map/ppermute | solution.py:61
  89.9 9.2 %collective-permute-done = bf16[32,1024]{1,0:T(8,128)(2,1)S(1)} collective-permute-done((bf16[32,1024]{1,0:T(8,128)(2,1)S(1)}, bf16[32,1024]{1,0:T(8,128)(2,1)S(1)}, u32[]{:S(2)}, u32[]{:S(2)}) %collective-permute-start) | collective-permute-done | bytes 65568 | tf_op jit(solution)/shard_map/ppermute | solution.py:61
  99.1 4.0 %all-to-all-done.2 = bf16[4,128,128]{2,1,0:T(8,128)(2,1)S(1)} async-done(((bf16[4,128,128]{2,1,0:T(8,128)(2,1)}), bf16[4,128,128]{2,1,0:T(8,128)(2,1)S(1)}, u32[]{:S(2)}, u32[]{:S(2)}) %all-to-all-start.2) | async-done | bytes 131104 | tf_op jit(solution)/shard_map/all_to_all | solution.py:15
  103.2 0.7 broadcast_in_dim.154
  104.0 10.3 %all-to-all-start.3 = ((bf16[8,128,128]{2,1,0:T(8,128)(2,1)}), bf16[8,128,128]{2,1,0:T(8,128)(2,1)S(1)}, u32[]{:S(2)}, u32[]{:S(2)}) async-start(bf16[8,128,128]{2,1,0:T(8,128)(2,1)} %broadcast_in_dim.154), calls=%async_computation.3 | async-start | bytes 524288 | tf_op jit(solution)/shard_map/all_to_all | solution.py:15
  114.2 11.8 %collective-permute-start.1 = (bf16[32,1024]{1,0:T(8,128)(2,1)S(1)}, bf16[32,1024]{1,0:T(8,128)(2,1)S(1)}, u32[]{:S(2)}, u32[]{:S(2)}) collective-permute-start(bf16[32,1024]{1,0:T(8,128)(2,1)S(1)} %reshape.181), channel_id=1, source_target_pairs={{0,128},{64,192},{128,0},{192,64},{1,129},{65,193},{129,1},{193,65... | collective-permute-start | bytes 196616 | tf_op jit(solution)/shard_map/ppermute | solution.py:61
  126.1 7.8 %collective-permute-start.2 = (bf16[32,1024]{1,0:T(8,128)(2,1)S(1)}, bf16[32,1024]{1,0:T(8,128)(2,1)S(1)}, u32[]{:S(2)}, u32[]{:S(2)}) collective-permute-start(bf16[32,1024]{1,0:T(8,128)(2,1)S(1)} %reshape.181), channel_id=1, source_target_pairs={{0,192},{64,0},{128,64},{192,128},{1,193},{65,1},{129,65},{193,129... | collective-permute-start | bytes 196616 | tf_op jit(solution)/shard_map/ppermute | solution.py:61
  133.9 0.1 iota_compare_fusion
  134.0 5.6 %collective-permute-done.1 = bf16[32,1024]{1,0:T(8,128)(2,1)S(1)} collective-permute-done((bf16[32,1024]{1,0:T(8,128)(2,1)S(1)}, bf16[32,1024]{1,0:T(8,128)(2,1)S(1)}, u32[]{:S(2)}, u32[]{:S(2)}) %collective-permute-start.1) | collective-permute-done | bytes 65568 | tf_op jit(solution)/shard_map/ppermute | solution.py:61
  139.5 0.0 all-to-all-done.3
  139.5 8.7 %collective-permute-done.2 = bf16[32,1024]{1,0:T(8,128)(2,1)S(1)} collective-permute-done((bf16[32,1024]{1,0:T(8,128)(2,1)S(1)}, bf16[32,1024]{1,0:T(8,128)(2,1)S(1)}, u32[]{:S(2)}, u32[]{:S(2)}) %collective-permute-start.2) | collective-permute-done | bytes 65568 | tf_op jit(solution)/shard_map/ppermute | solution.py:61
  148.3 0.2 fusion.15
  148.5 1.0 fusion
  149.6 0.1 select_reduce_fusion.1
  149.7 0.7 broadcast_in_dim.157
  150.4 15.2 %all-to-all-start.4 = ((bf16[8,4,32,128]{3,2,1,0:T(8,128)(2,1)}), bf16[8,4,32,128]{3,2,1,0:T(8,128)(2,1)S(1)}, u32[]{:S(2)}, u32[]{:S(2)}) async-start(bf16[8,4,32,128]{3,2,1,0:T(8,128)(2,1)} %broadcast_in_dim.157), calls=%async_computation.4 | async-start | bytes 524288 | tf_op jit(solution)/shard_map/all_to_all | solution.py:15
  165.7 0.2 convolution_convert_fusion
  165.8 0.1 reshape.185
  165.9 0.1 copy.19
  166.1 0.2 fusion.16
  166.3 0.2 multiply_reduce_fusion.1
  166.5 11.4 %psum.7 = f32[128]{0:T(128)S(1)} all-reduce(f32[128]{0:T(128)S(1)} %multiply_reduce_fusion.1), channel_id=1, replica_groups=mesh['y'=4,'far'=4,'near'=8,'tensor'=8] {'tensor'}, use_global_device_ids=true, to_apply=%region_5.6 | all-reduce | flops 128 | bytes 1024 | tf_op jit(solution)/shard_map/psum | solution.py:80
  177.9 4.3 %all-to-all-done.4 = bf16[8,4,32,128]{3,2,1,0:T(8,128)(2,1)S(1)} async-done(((bf16[8,4,32,128]{3,2,1,0:T(8,128)(2,1)}), bf16[8,4,32,128]{3,2,1,0:T(8,128)(2,1)S(1)}, u32[]{:S(2)}, u32[]{:S(2)}) %all-to-all-start.4) | async-done | bytes 262176 | tf_op jit(solution)/shard_map/all_to_all | solution.py:15
  182.1 0.1 copy.18
  182.2 0.2 multiply_reduce_fusion
  182.4 0.1 select_select_fusion
  182.5 0.1 broadcast_in_dim.159
  182.6 0.1 pad_maximum_fusion
  182.7 0.0 copy-start.3
  182.7 17.5 %all_to_all.31 = bf16[4,1104,128]{2,1,0:T(8,128)(2,1)S(1)} all-to-all(bf16[4,1104,128]{2,1,0:T(8,128)(2,1)S(1)} %pad_maximum_fusion), channel_id=1, replica_groups=mesh['y'=4,'far'=4,'near'=8,'tensor'=8] {'y'}, dimensions={0} | all-to-all | bytes 2260992 | tf_op jit(solution)/shard_map/all_to_all | solution.py:15
  200.2 0.6 slice_reduce_fusion
  201.6 1.6 multiply_add_fusion
  203.2 0.0 copy-done.3
  203.2 0.6 multiply_add_fusion.1
  203.8 1.3 multiply_convert_fusion
  (24 shorter events, 0.3 us)
Async XLA Ops:
  0.6 1.6 copy-start
  3.8 1.4 copy-start.1
  3.8 1.5 copy-start.2
  6.5 20.3 %all-to-all-start = ((bf16[4,1088,128]{2,1,0:T(8,128)(2,1)}), bf16[4,1088,128]{2,1,0:T(8,128)(2,1)S(1)}, u32[]{:S(2)}, u32[]{:S(2)}) async-start(bf16[4,1088,128]{2,1,0:T(8,128)(2,1)} %pad_maximum_fusion.1), calls=%async_computation | async-start | bytes 2228224 | tf_op jit(solution)/shard_map/all_to_all | solution.py:15
  56.4 46.8 %all-to-all-start.2 = ((bf16[4,128,128]{2,1,0:T(8,128)(2,1)}), bf16[4,128,128]{2,1,0:T(8,128)(2,1)S(1)}, u32[]{:S(2)}, u32[]{:S(2)}) async-start(bf16[4,128,128]{2,1,0:T(8,128)(2,1)} %broadcast_in_dim.153), calls=%async_computation.2 | async-start | bytes 262144 | tf_op jit(solution)/shard_map/all_to_all | solution.py:15
  77.3 21.9 %collective-permute-start = (bf16[32,1024]{1,0:T(8,128)(2,1)S(1)}, bf16[32,1024]{1,0:T(8,128)(2,1)S(1)}, u32[]{:S(2)}, u32[]{:S(2)}) collective-permute-start(bf16[32,1024]{1,0:T(8,128)(2,1)S(1)} %reshape.181), channel_id=1, source_target_pairs={{0,64},{64,128},{128,192},{192,0},{1,65},{65,129},{129,193},{193,1... | collective-permute-start | bytes 196616 | tf_op jit(solution)/shard_map/ppermute | solution.py:61
  104.0 35.6 %all-to-all-start.3 = ((bf16[8,128,128]{2,1,0:T(8,128)(2,1)}), bf16[8,128,128]{2,1,0:T(8,128)(2,1)S(1)}, u32[]{:S(2)}, u32[]{:S(2)}) async-start(bf16[8,128,128]{2,1,0:T(8,128)(2,1)} %broadcast_in_dim.154), calls=%async_computation.3 | async-start | bytes 524288 | tf_op jit(solution)/shard_map/all_to_all | solution.py:15
  114.2 25.3 %collective-permute-start.1 = (bf16[32,1024]{1,0:T(8,128)(2,1)S(1)}, bf16[32,1024]{1,0:T(8,128)(2,1)S(1)}, u32[]{:S(2)}, u32[]{:S(2)}) collective-permute-start(bf16[32,1024]{1,0:T(8,128)(2,1)S(1)} %reshape.181), channel_id=1, source_target_pairs={{0,128},{64,192},{128,0},{192,64},{1,129},{65,193},{129,1},{193,65... | collective-permute-start | bytes 196616 | tf_op jit(solution)/shard_map/ppermute | solution.py:61
  126.1 22.2 %collective-permute-start.2 = (bf16[32,1024]{1,0:T(8,128)(2,1)S(1)}, bf16[32,1024]{1,0:T(8,128)(2,1)S(1)}, u32[]{:S(2)}, u32[]{:S(2)}) collective-permute-start(bf16[32,1024]{1,0:T(8,128)(2,1)S(1)} %reshape.181), channel_id=1, source_target_pairs={{0,192},{64,0},{128,64},{192,128},{1,193},{65,1},{129,65},{193,129... | collective-permute-start | bytes 196616 | tf_op jit(solution)/shard_map/ppermute | solution.py:61
  150.4 31.7 %all-to-all-start.4 = ((bf16[8,4,32,128]{3,2,1,0:T(8,128)(2,1)}), bf16[8,4,32,128]{3,2,1,0:T(8,128)(2,1)S(1)}, u32[]{:S(2)}, u32[]{:S(2)}) async-start(bf16[8,4,32,128]{3,2,1,0:T(8,128)(2,1)} %broadcast_in_dim.157), calls=%async_computation.4 | async-start | bytes 524288 | tf_op jit(solution)/shard_map/all_to_all | solution.py:15
  182.7 20.5 %copy-start.3 = (f32[1,4,1,128]{3,2,1,0:T(1,128)S(1)}, f32[1,4,1,128]{3,2,1,0:T(1,128)}, u32[]{:S(2)}) copy-start(f32[1,4,1,128]{3,2,1,0:T(1,128)} %param.9) | copy-start | bytes 6148

commit v5 on v4

--- a/solution.py
+++ b/solution.py
@@ -52,25 +52,13 @@
     others = jnp.where((jnp.arange(ny) == y)[:, None, None], 0.0, got[:, :BLOCK].astype(f32))
     column_part = kept + jnp.sum(others, axis=0)
 
-    far = lax.axis_index("far")
-    held = [roots]
-
-    def step(operand, transfer):
-        operand, block = lax.optimization_barrier((operand, roots))
-        turn = [(i, (i + len(held)) % nfar) for i in range(nfar)]
-        held.append(lax.ppermute(block, "far", turn))
-        got = transfer(operand)
-        if len(held) > 2:
-            got, held[-2] = lax.optimization_barrier((got, held[-2]))
-        return got
-
-    pieces = column_part.astype(bf16).reshape(nnear, BLOCK // nnear, width)
-    got = step(pieces, lambda pieces: swap(pieces, "near"))
+    got = swap(column_part.astype(bf16).reshape(nnear, BLOCK // nnear, width), "near")
     part = jnp.sum(got.astype(f32), axis=0).astype(bf16)
-    got = step(part, lambda part: everyone(part, "far"))
+    part, roots = lax.optimization_barrier((part, roots))
+    roots = lax.all_gather(roots, "far", axis=0, tiled=True)
+    got, roots = lax.optimization_barrier((everyone(part, "far"), roots))
     own = jnp.sum(got.astype(f32), axis=0).astype(bf16)
-    gradient = step(own, lambda own: everyone(own, "near")).reshape(BLOCK, width)
-    roots = jnp.concatenate(held, axis=0)
+    gradient = everyone(own, "near").reshape(BLOCK, width)
 
     inner = lax.dot_general(
         gradient, gradient, (((0,), (0,)), ((), ())), preferred_element_type=f32
@@ -81,10 +69,7 @@
 
     right = lax.dynamic_index_in_dim(right_roots[0], y, 0, keepdims=False)
     mixed = jnp.dot(roots, gradient, preferred_element_type=f32)
-    direction = jnp.dot(mixed, right, precision=highest).reshape(1, nfar, ny * mine, width)
-    steps = jnp.arange(nfar)
-    turned = (far - steps[:, None]) % nfar == steps[None, :]
-    direction = jnp.sum(jnp.where(turned[:, :, None, None], direction, 0.0), axis=1).astype(bf16)
+    direction = jnp.dot(mixed, right, precision=highest).astype(bf16)
     direction = everyone(direction, "near").reshape(nnear, nfar, ny, mine, width)
     direction = direction.transpose(2, 1, 0, 3, 4).reshape(BLOCK, width)
     wide = direction.astype(f32)

time: 206 us -> 191 us (0.927)
  the two profiles are of different devices: /device:TPU:34 before, /device:TPU:1 now
where the time goes in v5:
time: 191 us; the launch traced here: 187 us
  blocking collectives  95.5 us (50%)
  starting transfers between devices  51.8 us (27%)
  waiting for transfers between devices  20.1 us (11%)
  other arithmetic  7.98 us (4%)
  local copies, waits for them, and re-layouts  6.76 us (4%)
  matrix products  3.26 us (2%)
    all_to_all x4, starting transfers between devices, swap(): return lax.all_to_all(pieces, axis, 0, 0, tiled=True)  51.8 us
    all_gather x1, blocking collectives, shards(): roots = lax.all_gather(roots, 'far', axis=0, tiled=True)  44.6 us
    all_to_all x2, blocking collectives, swap(): return lax.all_to_all(pieces, axis, 0, 0, tiled=True)  37.5 us
    all_to_all x4, waiting for transfers between devices, swap(): return lax.all_to_all(pieces, axis, 0, 0, tiled=True)  20.1 us
    psum x1, blocking collectives, shards(): block_sq = lax.psum(grad_sq, 'tensor')  13.5 us
  transfers between devices with their start and end apart: 4, of which 2 were waited for; matrix products, arithmetic and copies ran while one was open for 1% of the time, Pallas kernels for 0%

profile of v5, /device:TPU:1, one launch (start us, length us, event | category | flops | bytes accessed | tf_op | source)
XLA Modules:
  0.0 186.9 jit_solution(13006236952369247086)
XLA Ops:
  0.6 0.0 copy-start
  0.6 1.6 copy-done
  2.2 1.6 fusion.12
  3.8 0.0 copy-start.1
  3.8 0.0 copy-start.2
  3.9 1.3 copy-done.1
  5.2 0.1 convert_element_type.77
  5.3 0.0 copy-done.2
  5.4 1.1 pad_maximum_fusion.1
  6.5 5.0 %all-to-all-start = ((bf16[4,1088,128]{2,1,0:T(8,128)(2,1)}), bf16[4,1088,128]{2,1,0:T(8,128)(2,1)S(1)}, u32[]{:S(2)}, u32[]{:S(2)}) async-start(bf16[4,1088,128]{2,1,0:T(8,128)(2,1)} %pad_maximum_fusion.1), calls=%async_computation | async-start | bytes 2228224 | tf_op jit(solution)/shard_map/all_to_all | solution.py:15
  11.5 1.9 constant_dynamic-slice_fusion
  13.4 8.2 %all-to-all-done = bf16[4,1088,128]{2,1,0:T(8,128)(2,1)S(1)} async-done(((bf16[4,1088,128]{2,1,0:T(8,128)(2,1)}), bf16[4,1088,128]{2,1,0:T(8,128)(2,1)S(1)}, u32[]{:S(2)}, u32[]{:S(2)}) %all-to-all-start) | async-done | bytes 1114144 | tf_op jit(solution)/shard_map/all_to_all | solution.py:15
  21.6 0.3 select_reduce_fusion
  21.9 1.8 add_convert_fusion
  23.7 17.0 %all-to-all-start.1 = ((bf16[8,128,128]{2,1,0:T(8,128)(2,1)}), bf16[8,128,128]{2,1,0:T(8,128)(2,1)S(1)}, u32[]{:S(2)}, u32[]{:S(2)}) async-start(bf16[8,128,128]{2,1,0:T(8,128)(2,1)} %add_convert_fusion), calls=%async_computation.1 | async-start | bytes 524288 | tf_op jit(solution)/shard_map/all_to_all | solution.py:15
  40.8 11.9 %all-to-all-done.1 = bf16[8,128,128]{2,1,0:T(8,128)(2,1)S(1)} async-done(((bf16[8,128,128]{2,1,0:T(8,128)(2,1)}), bf16[8,128,128]{2,1,0:T(8,128)(2,1)S(1)}, u32[]{:S(2)}, u32[]{:S(2)}) %all-to-all-start.1) | async-done | bytes 262176 | tf_op jit(solution)/shard_map/all_to_all | solution.py:15
  52.7 0.7 broadcast_in_dim.129
  53.4 20.6 %all-to-all-start.2 = ((bf16[4,128,128]{2,1,0:T(8,128)(2,1)}), bf16[4,128,128]{2,1,0:T(8,128)(2,1)S(1)}, u32[]{:S(2)}, u32[]{:S(2)}) async-start(bf16[4,128,128]{2,1,0:T(8,128)(2,1)} %broadcast_in_dim.129), calls=%async_computation.2 | async-start | bytes 262144 | tf_op jit(solution)/shard_map/all_to_all | solution.py:15
  73.9 44.6 %all_gather.3 = bf16[128,1024]{1,0:T(8,128)(2,1)S(1)} all-gather(bf16[32,1024]{1,0:T(8,128)(2,1)S(1)} %reshape.130), channel_id=1, replica_groups=mesh['y'=4,'far'=4,'near'=8,'tensor'=8] {'far'}, dimensions={0}, use_global_device_ids=true | all-gather | bytes 327680 | tf_op jit(solution)/shard_map/all_gather | solution.py:58
  118.5 0.0 all-to-all-done.2
  118.6 22.6 %all_to_all.30 = bf16[8,128,128]{2,1,0:T(8,128)(2,1)S(1)} all-to-all(bf16[8,128,128]{2,1,0:T(8,128)(2,1)S(1)} %broadcast_in_dim.130), channel_id=1, replica_groups=mesh['y'=4,'far'=4,'near'=8,'tensor'=8] {'near'}, dimensions={0} | all-to-all | bytes 524288 | tf_op jit(solution)/shard_map/all_to_all | solution.py:15
  141.2 0.2 fusion.13
  141.4 1.0 convolution_convert_fusion.1
  142.4 0.7 broadcast_in_dim.131
  143.2 9.2 %all-to-all-start.4 = ((bf16[8,128,128]{2,1,0:T(8,128)(2,1)}), bf16[8,128,128]{2,1,0:T(8,128)(2,1)S(1)}, u32[]{:S(2)}, u32[]{:S(2)}) async-start(bf16[8,128,128]{2,1,0:T(8,128)(2,1)} %broadcast_in_dim.131), calls=%async_computation.4 | async-start | bytes 524288 | tf_op jit(solution)/shard_map/all_to_all | solution.py:15
  152.4 0.1 copy.15
  152.5 0.2 fusion.14
  152.8 0.2 convolution_convert_fusion
  153.0 0.1 reshape.134
  153.0 0.2 multiply_reduce_fusion.1
  153.2 13.5 %psum.7 = f32[128]{0:T(128)S(1)} all-reduce(f32[128]{0:T(128)S(1)} %multiply_reduce_fusion.1), channel_id=1, replica_groups=mesh['y'=4,'far'=4,'near'=8,'tensor'=8] {'tensor'}, use_global_device_ids=true, to_apply=%region_4.5 | all-reduce | flops 128 | bytes 1024 | tf_op jit(solution)/shard_map/psum | solution.py:68
  166.6 0.0 all-to-all-done.4
  166.7 0.2 multiply_reduce_fusion
  166.8 0.1 copy.14
  166.9 0.1 select_select_fusion
  167.0 0.1 broadcast_in_dim.133
  167.1 0.1 pad_maximum_fusion
  167.2 0.0 copy-start.3
  167.2 14.9 %all_to_all.31 = bf16[4,1104,128]{2,1,0:T(8,128)(2,1)S(1)} all-to-all(bf16[4,1104,128]{2,1,0:T(8,128)(2,1)S(1)} %pad_maximum_fusion), channel_id=1, replica_groups=mesh['y'=4,'far'=4,'near'=8,'tensor'=8] {'y'}, dimensions={0} | all-to-all | bytes 2260992 | tf_op jit(solution)/shard_map/all_to_all | solution.py:15
  182.1 0.6 slice_reduce_fusion
  183.5 1.6 multiply_add_fusion
  185.1 0.0 copy-done.3
  185.1 0.6 multiply_add_fusion.1
  185.7 1.3 multiply_convert_fusion
  (22 shorter events, 0.3 us)
Async XLA Ops:
  0.6 1.6 copy-start
  3.8 1.4 copy-start.1
  3.8 1.5 copy-start.2
  6.5 15.1 %all-to-all-start = ((bf16[4,1088,128]{2,1,0:T(8,128)(2,1)}), bf16[4,1088,128]{2,1,0:T(8,128)(2,1)S(1)}, u32[]{:S(2)}, u32[]{:S(2)}) async-start(bf16[4,1088,128]{2,1,0:T(8,128)(2,1)} %pad_maximum_fusion.1), calls=%async_computation | async-start | bytes 2228224 | tf_op jit(solution)/shard_map/all_to_all | solution.py:15
  23.7 29.0 %all-to-all-start.1 = ((bf16[8,128,128]{2,1,0:T(8,128)(2,1)}), bf16[8,128,128]{2,1,0:T(8,128)(2,1)S(1)}, u32[]{:S(2)}, u32[]{:S(2)}) async-start(bf16[8,128,128]{2,1,0:T(8,128)(2,1)} %add_convert_fusion), calls=%async_computation.1 | async-start | bytes 524288 | tf_op jit(solution)/shard_map/all_to_all | solution.py:15
  53.4 65.1 %all-to-all-start.2 = ((bf16[4,128,128]{2,1,0:T(8,128)(2,1)}), bf16[4,128,128]{2,1,0:T(8,128)(2,1)S(1)}, u32[]{:S(2)}, u32[]{:S(2)}) async-start(bf16[4,128,128]{2,1,0:T(8,128)(2,1)} %broadcast_in_dim.129), calls=%async_computation.2 | async-start | bytes 262144 | tf_op jit(solution)/shard_map/all_to_all | solution.py:15
  143.2 23.5 %all-to-all-start.4 = ((bf16[8,128,128]{2,1,0:T(8,128)(2,1)}), bf16[8,128,128]{2,1,0:T(8,128)(2,1)S(1)}, u32[]{:S(2)}, u32[]{:S(2)}) async-start(bf16[8,128,128]{2,1,0:T(8,128)(2,1)} %broadcast_in_dim.131), calls=%async_computation.4 | async-start | bytes 524288 | tf_op jit(solution)/shard_map/all_to_all | solution.py:15
  167.2 17.8 %copy-start.3 = (f32[1,4,1,128]{3,2,1,0:T(1,128)S(1)}, f32[1,4,1,128]{3,2,1,0:T(1,128)}, u32[]{:S(2)}) copy-start(f32[1,4,1,128]{3,2,1,0:T(1,128)} %param.9) | copy-start | bytes 6148

commit v6 on v5

--- a/solution.py
+++ b/solution.py
@@ -28,6 +28,13 @@
     return parts
 
 
+def lines(block, values):
+    row = jnp.arange(block.shape[-2])[:, None]
+    for place, value in enumerate(values, 1):
+        block = jnp.where(row == place, value, block)
+    return block
+
+
 def shards(activations, cotangents, left_stats, right_stats, left_roots, right_roots):
     ny = lax.axis_size("y")
     nfar = lax.axis_size("far")
@@ -52,25 +59,32 @@
     others = jnp.where((jnp.arange(ny) == y)[:, None, None], 0.0, got[:, :BLOCK].astype(f32))
     column_part = kept + jnp.sum(others, axis=0)
 
-    got = swap(column_part.astype(bf16).reshape(nnear, BLOCK // nnear, width), "near")
+    pieces = column_part.astype(bf16).reshape(nnear, BLOCK // nnear, width)
+    pieces, roots = lax.optimization_barrier((pieces, roots))
+    roots = lax.all_gather(roots, "far", axis=0, tiled=True)
+    got, roots = lax.optimization_barrier((swap(pieces, "near"), roots))
     part = jnp.sum(got.astype(f32), axis=0).astype(bf16)
-    part, roots = lax.optimization_barrier((part, roots))
-    roots = lax.all_gather(roots, "far", axis=0, tiled=True)
-    got, roots = lax.optimization_barrier((everyone(part, "far"), roots))
-    own = jnp.sum(got.astype(f32), axis=0).astype(bf16)
-    gradient = everyone(own, "near").reshape(BLOCK, width)
+    got = everyone(part, "far")
+    own = jnp.sum(got.astype(f32), axis=0)
+    own_sq = lax.psum(jnp.sum(own * own, axis=0), "tensor")
+    own = own.astype(bf16)
+    gradient, own_sq = lax.optimization_barrier((everyone(own, "near"), own_sq))
+    gradient = gradient.reshape(BLOCK, width)
 
     inner = lax.dot_general(
         gradient, gradient, (((0,), (0,)), ((), ())), preferred_element_type=f32
     )
     wide = gradient.astype(f32)
     grad_sq = jnp.sum(wide * wide, axis=0)
-    block_sq = lax.psum(grad_sq, "tensor")
 
     right = lax.dynamic_index_in_dim(right_roots[0], y, 0, keepdims=False)
     mixed = jnp.dot(roots, gradient, preferred_element_type=f32)
     direction = jnp.dot(mixed, right, precision=highest).astype(bf16)
-    direction = everyone(direction, "near").reshape(nnear, nfar, ny, mine, width)
+    got = everyone(
+        jnp.concatenate([direction, lines(jnp.zeros((16, width), bf16), thirds(own_sq))], axis=0), "near"
+    )
+    block_sq = jnp.sum(got[:, nfar * ny * mine :].astype(f32), axis=(0, 1))
+    direction = got[:, : nfar * ny * mine].reshape(nnear, nfar, ny, mine, width)
     direction = direction.transpose(2, 1, 0, 3, 4).reshape(BLOCK, width)
     wide = direction.astype(f32)
     dir_sq = jnp.sum(wide * wide, axis=0)
@@ -81,10 +95,9 @@
     )
     outer = outer.astype(bf16).reshape(ny, root_rows, width)
     inner = lax.dynamic_index_in_dim(inner.reshape(ny, nz, width), z, 1, keepdims=True).astype(bf16)
-    line = jnp.arange(16)[:, None]
-    extra = jnp.broadcast_to(inner, (ny, 16, width))
-    for place, values in enumerate(thirds(grad_sq) + thirds(dir_sq) + thirds(block_sq), 1):
-        extra = jnp.where(line == place, values, extra)
+    extra = lines(
+        jnp.broadcast_to(inner, (ny, 16, width)), thirds(grad_sq) + thirds(dir_sq) + thirds(block_sq)
+    )
     got = swap(
         jnp.concatenate(
             [jnp.broadcast_to(direction[None], (ny, BLOCK, width)), outer, extra], axis=1

time: 191 us -> 199 us (1.042)
  the two profiles are of different devices: /device:TPU:1 before, /device:TPU:32 now
where the time goes in v6:
time: 199 us; the launch traced here: 198 us
  blocking collectives  104 us (52%)
  starting transfers between devices  43.5 us (22%)
  waiting for transfers between devices  30.7 us (15%)
  other arithmetic  8.15 us (4%)
  local copies, waits for them, and re-layouts  6.85 us (3%)
  matrix products  3.26 us (2%)
    all_to_all x2, blocking collectives, swap(): return lax.all_to_all(pieces, axis, 0, 0, tiled=True)  52.8 us
    all_to_all x4, starting transfers between devices, swap(): return lax.all_to_all(pieces, axis, 0, 0, tiled=True)  43.5 us
    all_gather x1, blocking collectives, shards(): roots = lax.all_gather(roots, 'far', axis=0, tiled=True)  38.8 us
    all_to_all x4, waiting for transfers between devices, swap(): return lax.all_to_all(pieces, axis, 0, 0, tiled=True)  30.7 us
    psum x1, blocking collectives, shards(): own_sq = lax.psum(jnp.sum(own * own, axis=0), 'tensor')  12.7 us
  transfers between devices with their start and end apart: 4, of which 2 were waited for; matrix products, arithmetic and copies ran while one was open for 1% of the time, Pallas kernels for 0%

profile of v6, /device:TPU:32, one launch (start us, length us, event | category | flops | bytes accessed | tf_op | source)
XLA Modules:
  0.0 198.3 jit_solution(3502702372017688535)
XLA Ops:
  0.6 0.0 copy-start
  0.6 1.6 copy-done
  2.2 1.6 fusion.14
  3.8 0.0 copy-start.1
  3.8 0.0 copy-start.2
  3.9 1.3 copy-done.1
  5.2 0.1 convert_element_type.97
  5.3 0.0 copy-done.2
  5.4 1.1 pad_maximum_fusion.1
  6.5 4.5 %all-to-all-start = ((bf16[4,1088,128]{2,1,0:T(8,128)(2,1)}), bf16[4,1088,128]{2,1,0:T(8,128)(2,1)S(1)}, u32[]{:S(2)}, u32[]{:S(2)}) async-start(bf16[4,1088,128]{2,1,0:T(8,128)(2,1)} %pad_maximum_fusion.1), calls=%async_computation | async-start | bytes 2228224 | tf_op jit(solution)/shard_map/all_to_all | solution.py:15
  11.0 1.9 constant_dynamic-slice_fusion
  12.8 13.9 %all-to-all-done = bf16[4,1088,128]{2,1,0:T(8,128)(2,1)S(1)} async-done(((bf16[4,1088,128]{2,1,0:T(8,128)(2,1)}), bf16[4,1088,128]{2,1,0:T(8,128)(2,1)S(1)}, u32[]{:S(2)}, u32[]{:S(2)}) %all-to-all-start) | async-done | bytes 1114144 | tf_op jit(solution)/shard_map/all_to_all | solution.py:15
  26.8 0.3 select_reduce_fusion
  27.1 1.8 add_convert_fusion
  28.9 12.6 %all-to-all-start.1 = ((bf16[8,128,128]{2,1,0:T(8,128)(2,1)}), bf16[8,128,128]{2,1,0:T(8,128)(2,1)S(1)}, u32[]{:S(2)}, u32[]{:S(2)}) async-start(bf16[8,128,128]{2,1,0:T(8,128)(2,1)} %add_convert_fusion), calls=%async_computation.1 | async-start | bytes 524288 | tf_op jit(solution)/shard_map/all_to_all | solution.py:15
  41.5 38.8 %all_gather.3 = bf16[128,1024]{1,0:T(8,128)(2,1)S(1)} all-gather(bf16[32,1024]{1,0:T(8,128)(2,1)S(1)} %reshape.141), channel_id=1, replica_groups=mesh['y'=4,'far'=4,'near'=8,'tensor'=8] {'far'}, dimensions={0}, use_global_device_ids=true | all-gather | bytes 327680 | tf_op jit(solution)/shard_map/all_gather | solution.py:64
  80.3 0.0 all-to-all-done.1
  80.4 35.6 %all_to_all.30 = bf16[4,128,128]{2,1,0:T(8,128)(2,1)S(1)} all-to-all(bf16[4,128,128]{2,1,0:T(8,128)(2,1)S(1)} %broadcast_in_dim.161), channel_id=1, replica_groups=mesh['y'=4,'far'=4,'near'=8,'tensor'=8] {'far'}, dimensions={0} | all-to-all | bytes 262144 | tf_op jit(solution)/shard_map/all_to_all | solution.py:15
  116.0 0.7 broadcast_in_dim.162
  116.8 16.5 %all-to-all-start.3 = ((bf16[8,128,128]{2,1,0:T(8,128)(2,1)}), bf16[8,128,128]{2,1,0:T(8,128)(2,1)S(1)}, u32[]{:S(2)}, u32[]{:S(2)}) async-start(bf16[8,128,128]{2,1,0:T(8,128)(2,1)} %broadcast_in_dim.162), calls=%async_computation.3 | async-start | bytes 524288 | tf_op jit(solution)/shard_map/all_to_all | solution.py:15
  133.3 12.7 %psum.7 = f32[128]{0:T(128)S(1)} all-reduce(f32[128]{0:T(128)S(1)} %get-tuple-element.27), channel_id=1, replica_groups=mesh['y'=4,'far'=4,'near'=8,'tensor'=8] {'tensor'}, use_global_device_ids=true, to_apply=%region_4.5 | all-reduce | flops 128 | bytes 1024 | tf_op jit(solution)/shard_map/psum | solution.py:69
  146.0 0.0 all-to-all-done.3
  146.0 0.2 fusion.15
  146.2 1.0 convolution_convert_fusion.1
  147.3 0.1 select_select_fusion.1
  147.4 0.8 broadcast_in_dim.170
  148.1 9.9 %all-to-all-start.4 = ((bf16[8,144,128]{2,1,0:T(8,128)(2,1)}), bf16[8,144,128]{2,1,0:T(8,128)(2,1)S(1)}, u32[]{:S(2)}, u32[]{:S(2)}) async-start(bf16[8,144,128]{2,1,0:T(8,128)(2,1)} %broadcast_in_dim.170), calls=%async_computation.4 | async-start | bytes 589824 | tf_op jit(solution)/shard_map/all_to_all | solution.py:15
  158.1 0.2 convolution_convert_fusion
  158.2 0.1 reshape.145
  158.3 0.1 copy.19
  158.5 0.2 fusion.16
  158.7 0.2 multiply_reduce_fusion
  158.9 16.8 %all-to-all-done.4 = bf16[8,144,128]{2,1,0:T(8,128)(2,1)S(1)} async-done(((bf16[8,144,128]{2,1,0:T(8,128)(2,1)}), bf16[8,144,128]{2,1,0:T(8,128)(2,1)S(1)}, u32[]{:S(2)}, u32[]{:S(2)}) %all-to-all-start.4) | async-done | bytes 294944 | tf_op jit(solution)/shard_map/all_to_all | solution.py:15
  175.7 0.1 copy.18
  175.7 0.2 multiply_reduce_fusion.1
  175.9 0.1 select_select_fusion
  176.0 0.1 broadcast_in_dim.172
  176.2 0.1 pad_maximum_fusion
  176.3 0.0 copy-start.3
  176.3 17.2 %all_to_all.31 = bf16[4,1104,128]{2,1,0:T(8,128)(2,1)S(1)} all-to-all(bf16[4,1104,128]{2,1,0:T(8,128)(2,1)S(1)} %pad_maximum_fusion), channel_id=1, replica_groups=mesh['y'=4,'far'=4,'near'=8,'tensor'=8] {'y'}, dimensions={0} | all-to-all | bytes 2260992 | tf_op jit(solution)/shard_map/all_to_all | solution.py:15
  193.5 0.6 slice_reduce_fusion
  194.9 1.6 multiply_add_fusion
  196.5 0.0 copy-done.3
  196.5 0.6 multiply_add_fusion.1
  197.1 1.3 multiply_convert_fusion
  (28 shorter events, 0.4 us)
Async XLA Ops:
  0.6 1.6 copy-start
  3.8 1.4 copy-start.1
  3.8 1.5 copy-start.2
  6.5 20.3 %all-to-all-start = ((bf16[4,1088,128]{2,1,0:T(8,128)(2,1)}), bf16[4,1088,128]{2,1,0:T(8,128)(2,1)S(1)}, u32[]{:S(2)}, u32[]{:S(2)}) async-start(bf16[4,1088,128]{2,1,0:T(8,128)(2,1)} %pad_maximum_fusion.1), calls=%async_computation | async-start | bytes 2228224 | tf_op jit(solution)/shard_map/all_to_all | solution.py:15
  28.9 51.4 %all-to-all-start.1 = ((bf16[8,128,128]{2,1,0:T(8,128)(2,1)}), bf16[8,128,128]{2,1,0:T(8,128)(2,1)S(1)}, u32[]{:S(2)}, u32[]{:S(2)}) async-start(bf16[8,128,128]{2,1,0:T(8,128)(2,1)} %add_convert_fusion), calls=%async_computation.1 | async-start | bytes 524288 | tf_op jit(solution)/shard_map/all_to_all | solution.py:15
  116.8 29.3 %all-to-all-start.3 = ((bf16[8,128,128]{2,1,0:T(8,128)(2,1)}), bf16[8,128,128]{2,1,0:T(8,128)(2,1)S(1)}, u32[]{:S(2)}, u32[]{:S(2)}) async-start(bf16[8,128,128]{2,1,0:T(8,128)(2,1)} %broadcast_in_dim.162), calls=%async_computation.3 | async-start | bytes 524288 | tf_op jit(solution)/shard_map/all_to_all | solution.py:15
  148.1 27.5 %all-to-all-start.4 = ((bf16[8,144,128]{2,1,0:T(8,128)(2,1)}), bf16[8,144,128]{2,1,0:T(8,128)(2,1)S(1)}, u32[]{:S(2)}, u32[]{:S(2)}) async-start(bf16[8,144,128]{2,1,0:T(8,128)(2,1)} %broadcast_in_dim.170), calls=%async_computation.4 | async-start | bytes 589824 | tf_op jit(solution)/shard_map/all_to_all | solution.py:15
  176.3 20.2 %copy-start.3 = (f32[1,4,1,128]{3,2,1,0:T(1,128)S(1)}, f32[1,4,1,128]{3,2,1,0:T(1,128)}, u32[]{:S(2)}) copy-start(f32[1,4,1,128]{3,2,1,0:T(1,128)} %param.9) | copy-start | bytes 6148

commit v7 on v5

--- a/solution.py
+++ b/solution.py
@@ -28,6 +28,10 @@
     return parts
 
 
+def sum_tokens(rows, columns):
+    return lax.dot_general(rows, columns, (((0,), (0,)), ((), ())), preferred_element_type=f32)
+
+
 def shards(activations, cotangents, left_stats, right_stats, left_roots, right_roots):
     ny = lax.axis_size("y")
     nfar = lax.axis_size("far")
@@ -42,21 +46,20 @@
     mine = left_roots.shape[2]
     root_rows = mine * (BLOCK // width)
 
-    partial = lax.dot_general(
-        activations, cotangents, (((0,), (0,)), ((), ())), preferred_element_type=f32
-    ).reshape(blocks, BLOCK, width)
+    partial = sum_tokens(activations, cotangents).astype(bf16).reshape(blocks, BLOCK, width)
     roots = left_roots[0].astype(bf16).reshape(blocks, root_rows, width)
-    got = swap(jnp.concatenate([partial.astype(bf16), roots], axis=1), "y")
+    got = swap(jnp.concatenate([partial, roots], axis=1), "y")
     roots = got[:, BLOCK:].reshape(ny * mine, BLOCK)
-    kept = lax.dynamic_index_in_dim(partial, y, 0, keepdims=False)
+    kept = sum_tokens(lax.dynamic_slice_in_dim(activations, y * BLOCK, BLOCK, 1), cotangents)
     others = jnp.where((jnp.arange(ny) == y)[:, None, None], 0.0, got[:, :BLOCK].astype(f32))
     column_part = kept + jnp.sum(others, axis=0)
 
-    got = swap(column_part.astype(bf16).reshape(nnear, BLOCK // nnear, width), "near")
+    pieces = column_part.astype(bf16).reshape(nnear, BLOCK // nnear, width)
+    pieces, roots = lax.optimization_barrier((pieces, roots))
+    roots = lax.all_gather(roots, "far", axis=0, tiled=True)
+    got, roots = lax.optimization_barrier((swap(pieces, "near"), roots))
     part = jnp.sum(got.astype(f32), axis=0).astype(bf16)
-    part, roots = lax.optimization_barrier((part, roots))
-    roots = lax.all_gather(roots, "far", axis=0, tiled=True)
-    got, roots = lax.optimization_barrier((everyone(part, "far"), roots))
+    got = everyone(part, "far")
     own = jnp.sum(got.astype(f32), axis=0).astype(bf16)
     gradient = everyone(own, "near").reshape(BLOCK, width)
 

time: 191 us -> 189 us (0.990); the launches traced: 187 us -> 188 us
  blocking collectives: 95.5 us -> 108 us
  starting transfers between devices: 51.8 us -> 42.9 us
  local copies, waits for them, and re-layouts: 6.76 us -> 2.58 us
  waiting for transfers between devices: 20.1 us -> 22.1 us
    all_to_all x2, blocking collectives: 37.5 us -> 50.4 us  [swap(): return lax.all_to_all(pieces, axis, 0, 0, tiled=True)]
    all_gather x1, blocking collectives: 44.6 us -> 35.2 us  [shards(): roots = lax.all_gather(roots, 'far', axis=0, tiled=True)]
    all_to_all x4, starting transfers between devices: 51.8 us -> 42.9 us  [swap(): return lax.all_to_all(pieces, axis, 0, 0, tiled=True)]
    psum x1, blocking collectives: 13.5 us -> 22 us  [shards(): block_sq = lax.psum(grad_sq, 'tensor')]
    unnamed x9 -> x7, local copies, waits for them, and re-layouts: 2.94 us -> 0.57 us
    all_to_all x4, waiting for transfers between devices: 20.1 us -> 22.1 us  [swap(): return lax.all_to_all(pieces, axis, 0, 0, tiled=True)]
    convert_element_type x2 -> x0, other arithmetic: 1.93 us -> none  [the longest x1 1.79 us: shards(): column_part.astype(bf16).reshape(nnear, BLOCK // nnear, width)]
  transfers between devices with their start and end apart: 4 -> 4, of which waited for: 2 -> 2; matrix products, arithmetic and copies ran while one was open for 1% -> 0% of each run, Pallas kernels for 0% -> 0%
where the time goes in v7:
time: 189 us; the launch traced here: 188 us
  blocking collectives  108 us (57%)
  starting transfers between devices  42.9 us (23%)
  waiting for transfers between devices  22.1 us (12%)
  other arithmetic  7.07 us (4%)
  matrix products  4.32 us (2%)
  local copies, waits for them, and re-layouts  2.58 us (1%)
    all_to_all x2, blocking collectives, swap(): return lax.all_to_all(pieces, axis, 0, 0, tiled=True)  50.4 us
    all_to_all x4, starting transfers between devices, swap(): return lax.all_to_all(pieces, axis, 0, 0, tiled=True)  42.9 us
    all_gather x1, blocking collectives, shards(): roots = lax.all_gather(roots, 'far', axis=0, tiled=True)  35.2 us
    all_to_all x4, waiting for transfers between devices, swap(): return lax.all_to_all(pieces, axis, 0, 0, tiled=True)  22.1 us
    psum x1, blocking collectives, shards(): block_sq = lax.psum(grad_sq, 'tensor')  22 us
  transfers between devices with their start and end apart: 4, of which 2 were waited for; matrix products, arithmetic and copies ran while one was open for 0% of the time, Pallas kernels for 0%

profile of v7, /device:TPU:1, one launch (start us, length us, event | category | flops | bytes accessed | tf_op | source)
XLA Modules:
  0.0 188.1 jit_solution(15681542344479993086)
XLA Ops:
  0.6 0.0 copy-start
  0.6 1.1 convert_element_type.77
  1.7 0.5 copy-done
  2.3 1.6 convolution_convert_fusion
  3.9 1.1 pad_maximum_fusion.1
  5.0 0.0 copy-start.1
  5.0 5.1 %all-to-all-start = ((bf16[4,1088,128]{2,1,0:T(8,128)(2,1)}), bf16[4,1088,128]{2,1,0:T(8,128)(2,1)S(1)}, u32[]{:S(2)}, u32[]{:S(2)}) async-start(bf16[4,1088,128]{2,1,0:T(8,128)(2,1)} %pad_maximum_fusion.1), calls=%async_computation | async-start | bytes 2228224 | tf_op jit(solution)/shard_map/all_to_all | solution.py:15
  10.1 10.1 %all-to-all-done = bf16[4,1088,128]{2,1,0:T(8,128)(2,1)S(1)} async-done(((bf16[4,1088,128]{2,1,0:T(8,128)(2,1)}), bf16[4,1088,128]{2,1,0:T(8,128)(2,1)S(1)}, u32[]{:S(2)}, u32[]{:S(2)}) %all-to-all-start) | async-done | bytes 1114144 | tf_op jit(solution)/shard_map/all_to_all | solution.py:15
  20.2 0.3 select_reduce_fusion
  20.6 0.0 copy-done.1
  20.6 1.1 fusion
  21.6 17.0 %all-to-all-start.1 = ((bf16[8,128,128]{2,1,0:T(8,128)(2,1)}), bf16[8,128,128]{2,1,0:T(8,128)(2,1)S(1)}, u32[]{:S(2)}, u32[]{:S(2)}) async-start(bf16[8,128,128]{2,1,0:T(8,128)(2,1)} %bitcast.1), calls=%async_computation.1 | async-start | bytes 524288 | tf_op jit(solution)/shard_map/all_to_all | solution.py:15
  38.7 35.2 %all_gather.3 = bf16[128,1024]{1,0:T(8,128)(2,1)S(1)} all-gather(bf16[32,1024]{1,0:T(8,128)(2,1)S(1)} %reshape.131), channel_id=1, replica_groups=mesh['y'=4,'far'=4,'near'=8,'tensor'=8] {'far'}, dimensions={0}, use_global_device_ids=true | all-gather | bytes 327680 | tf_op jit(solution)/shard_map/all_gather | solution.py:59
  73.9 0.0 all-to-all-done.1
  73.9 32.7 %all_to_all.30 = bf16[4,128,128]{2,1,0:T(8,128)(2,1)S(1)} all-to-all(bf16[4,128,128]{2,1,0:T(8,128)(2,1)S(1)} %broadcast_in_dim.129), channel_id=1, replica_groups=mesh['y'=4,'far'=4,'near'=8,'tensor'=8] {'far'}, dimensions={0} | all-to-all | bytes 262144 | tf_op jit(solution)/shard_map/all_to_all | solution.py:15
  106.6 0.7 broadcast_in_dim.130
  107.4 16.6 %all-to-all-start.3 = ((bf16[8,128,128]{2,1,0:T(8,128)(2,1)}), bf16[8,128,128]{2,1,0:T(8,128)(2,1)S(1)}, u32[]{:S(2)}, u32[]{:S(2)}) async-start(bf16[8,128,128]{2,1,0:T(8,128)(2,1)} %broadcast_in_dim.130), calls=%async_computation.3 | async-start | bytes 524288 | tf_op jit(solution)/shard_map/all_to_all | solution.py:15
  124.0 12.0 %all-to-all-done.3 = bf16[8,128,128]{2,1,0:T(8,128)(2,1)S(1)} async-done(((bf16[8,128,128]{2,1,0:T(8,128)(2,1)}), bf16[8,128,128]{2,1,0:T(8,128)(2,1)S(1)}, u32[]{:S(2)}, u32[]{:S(2)}) %all-to-all-start.3) | async-done | bytes 262176 | tf_op jit(solution)/shard_map/all_to_all | solution.py:15
  136.0 0.2 fusion.15
  136.2 1.0 convolution_convert_fusion.2
  137.3 0.7 broadcast_in_dim.131
  138.0 4.1 %all-to-all-start.4 = ((bf16[8,128,128]{2,1,0:T(8,128)(2,1)}), bf16[8,128,128]{2,1,0:T(8,128)(2,1)S(1)}, u32[]{:S(2)}, u32[]{:S(2)}) async-start(bf16[8,128,128]{2,1,0:T(8,128)(2,1)} %broadcast_in_dim.131), calls=%async_computation.4 | async-start | bytes 524288 | tf_op jit(solution)/shard_map/all_to_all | solution.py:15
  142.2 0.2 convolution_convert_fusion.1
  142.4 0.1 reshape.135
  142.4 0.1 copy.19
  142.6 0.2 fusion.16
  142.8 0.2 multiply_reduce_fusion.1
  143.0 22.0 %psum.7 = f32[128]{0:T(128)S(1)} all-reduce(f32[128]{0:T(128)S(1)} %multiply_reduce_fusion.1), channel_id=1, replica_groups=mesh['y'=4,'far'=4,'near'=8,'tensor'=8] {'tensor'}, use_global_device_ids=true, to_apply=%region_4.5 | all-reduce | flops 128 | bytes 1024 | tf_op jit(solution)/shard_map/psum | solution.py:71
  165.0 0.0 all-to-all-done.4
  165.0 0.2 multiply_reduce_fusion
  165.1 0.1 copy.18
  165.2 0.1 select_select_fusion
  165.3 0.1 broadcast_in_dim.133
  165.4 0.0 copy-start.2
  165.5 0.1 pad_maximum_fusion
  165.5 17.8 %all_to_all.31 = bf16[4,1104,128]{2,1,0:T(8,128)(2,1)S(1)} all-to-all(bf16[4,1104,128]{2,1,0:T(8,128)(2,1)S(1)} %pad_maximum_fusion), channel_id=1, replica_groups=mesh['y'=4,'far'=4,'near'=8,'tensor'=8] {'y'}, dimensions={0} | all-to-all | bytes 2260992 | tf_op jit(solution)/shard_map/all_to_all | solution.py:15
  183.3 0.6 slice_reduce_fusion
  184.7 0.0 copy-done.2
  184.7 0.6 multiply_add_fusion.1
  185.3 1.6 multiply_add_fusion
  186.9 1.3 multiply_convert_fusion
  (21 shorter events, 0.3 us)
Async XLA Ops:
  0.6 1.7 copy-start
  5.0 15.6 %copy-start.1 = (bf16[256,128]{1,0:T(8,128)(2,1)S(1)}, bf16[256,128]{1,0:T(8,128)(2,1)}, u32[]{:S(2)}) copy-start(bf16[256,128]{1,0:T(8,128)(2,1)} %param.7) | copy-start | bytes 196612
  5.0 15.2 %all-to-all-start = ((bf16[4,1088,128]{2,1,0:T(8,128)(2,1)}), bf16[4,1088,128]{2,1,0:T(8,128)(2,1)S(1)}, u32[]{:S(2)}, u32[]{:S(2)}) async-start(bf16[4,1088,128]{2,1,0:T(8,128)(2,1)} %pad_maximum_fusion.1), calls=%async_computation | async-start | bytes 2228224 | tf_op jit(solution)/shard_map/all_to_all | solution.py:15
  21.6 52.2 %all-to-all-start.1 = ((bf16[8,128,128]{2,1,0:T(8,128)(2,1)}), bf16[8,128,128]{2,1,0:T(8,128)(2,1)S(1)}, u32[]{:S(2)}, u32[]{:S(2)}) async-start(bf16[8,128,128]{2,1,0:T(8,128)(2,1)} %bitcast.1), calls=%async_computation.1 | async-start | bytes 524288 | tf_op jit(solution)/shard_map/all_to_all | solution.py:15
  107.4 28.7 %all-to-all-start.3 = ((bf16[8,128,128]{2,1,0:T(8,128)(2,1)}), bf16[8,128,128]{2,1,0:T(8,128)(2,1)S(1)}, u32[]{:S(2)}, u32[]{:S(2)}) async-start(bf16[8,128,128]{2,1,0:T(8,128)(2,1)} %broadcast_in_dim.130), calls=%async_computation.3 | async-start | bytes 524288 | tf_op jit(solution)/shard_map/all_to_all | solution.py:15
  138.0 26.9 %all-to-all-start.4 = ((bf16[8,128,128]{2,1,0:T(8,128)(2,1)}), bf16[8,128,128]{2,1,0:T(8,128)(2,1)S(1)}, u32[]{:S(2)}, u32[]{:S(2)}) async-start(bf16[8,128,128]{2,1,0:T(8,128)(2,1)} %broadcast_in_dim.131), calls=%async_computation.4 | async-start | bytes 524288 | tf_op jit(solution)/shard_map/all_to_all | solution.py:15
  165.4 19.2 %copy-start.2 = (f32[1,4,1,128]{3,2,1,0:T(1,128)S(1)}, f32[1,4,1,128]{3,2,1,0:T(1,128)}, u32[]{:S(2)}) copy-start(f32[1,4,1,128]{3,2,1,0:T(1,128)} %param.9) | copy-start | bytes 6148

commit v8 on v7

v8 whole, which is shorter than its diff:
```python
import jax
import jax.numpy as jnp
from jax import lax
from jax.sharding import Mesh, PartitionSpec as P

BLOCK = 1024
stat_decay = 0.95
highest = lax.Precision.HIGHEST
f32 = jnp.float32
bf16 = jnp.bfloat16
Z = ("far", "mid", "pair")


def swap(pieces, axis):
    return lax.all_to_all(pieces, axis, 0, 0, tiled=True)


def everyone(piece, axis):
    return swap(jnp.broadcast_to(piece[None], (lax.axis_size(axis), *piece.shape)), axis)


def thirds(value):
    parts = []
    for _ in range(3):
        part = lax.reduce_precision(value, 8, 7)
        parts.append(part.astype(bf16))
        value = value - part
    return parts


def sum_tokens(rows, columns):
    return lax.dot_general(rows, columns, (((0,), (0,)), ((), ())), preferred_element_type=f32)


def shards(activations, cotangents, left_stats, right_stats, left_roots, right_roots):
    ny = lax.axis_size("y")
    nfar = lax.axis_size("far")
    nmid = lax.axis_size("mid")
    npair = lax.axis_size("pair")
    nz = nfar * nmid * npair
    tensors = lax.axis_size("tensor")
    y = lax.axis_index("y")
    pair = lax.axis_index("pair")
    place = y * npair + pair
    features = activations.shape[1]
    width = cotangents.shape[1]
    blocks = features // BLOCK
    mine = left_roots.shape[2]
    root_rows = mine * (BLOCK // width)

    half = BLOCK // npair
    partial = sum_tokens(activations, cotangents).astype(bf16)
    partial = partial.reshape(blocks * npair, half, width)
    roots = left_roots[0].astype(bf16).reshape(blocks, 1, root_rows, width)
    roots = jnp.broadcast_to(roots, (blocks, npair, root_rows, width))
    roots = roots.reshape(blocks * npair, root_rows, width)
    got = swap(jnp.concatenate([partial, roots], axis=1), ("y", "pair"))
    roots = got[:, half:].reshape(ny, npair, root_rows, width)
    roots = lax.dynamic_index_in_dim(roots, pair, 1, keepdims=False).reshape(ny * mine, BLOCK)
    kept = sum_tokens(lax.dynamic_slice_in_dim(activations, place * half, half, 1), cotangents)
    others = jnp.arange(ny * npair) == place
    others = jnp.where(others[:, None, None], 0.0, got[:, :half].astype(f32))
    column_part = kept + jnp.sum(others, axis=0)

    pieces = column_part.astype(bf16).reshape(nmid, half // nmid, width)
    pieces, roots = lax.optimization_barrier((pieces, roots))
    roots = lax.all_gather(roots, "far", axis=0, tiled=True)
    got, roots = lax.optimization_barrier((swap(pieces, "mid"), roots))
    part = jnp.sum(got.astype(f32), axis=0).astype(bf16)
    got = everyone(part, "far")
    own = jnp.sum(got.astype(f32), axis=0).astype(bf16)
    gradient = everyone(own, ("pair", "mid")).reshape(BLOCK, width)

    inner = lax.dot_general(
        gradient, gradient, (((0,), (0,)), ((), ())), preferred_element_type=f32
    )
    wide = gradient.astype(f32)
    grad_sq = jnp.sum(wide * wide, axis=0)
    block_sq = lax.psum(grad_sq, "tensor")

    right = lax.dynamic_index_in_dim(right_roots[0], y, 0, keepdims=False)
    mixed = jnp.dot(roots, gradient, preferred_element_type=f32)
    direction = jnp.dot(mixed, right, precision=highest).astype(bf16)
    direction = everyone(direction, "mid").reshape(nmid, nfar, ny, mine, width)
    direction = direction.transpose(2, 1, 0, 3, 4).reshape(half, width)
    wide = direction.astype(f32)
    dir_sq = jnp.sum(wide * wide, axis=0)

    spot = lax.axis_index("far") * nmid + lax.axis_index("mid")
    rows = gradient.reshape(ny, nz // npair, npair * mine, width)
    rows = lax.dynamic_index_in_dim(rows, spot, 1, keepdims=False).reshape(ny * npair * mine, width)
    outer = lax.dot_general(
        rows,
        lax.dynamic_slice_in_dim(gradient, pair * half, half, 0),
        (((1,), (1,)), ((), ())),
        preferred_element_type=f32,
    )
    outer_rows = root_rows // npair
    outer = outer.astype(bf16).reshape(ny * npair, outer_rows, width)
    inner = inner.reshape(ny, nz // npair, npair, width)
    inner = lax.dynamic_index_in_dim(inner, spot, 1, keepdims=False).astype(bf16)
    inner = inner.reshape(ny * npair, 1, width)
    line = jnp.arange(16)[:, None]
    extra = jnp.broadcast_to(inner, (ny * npair, 16, width))
    for number, values in enumerate(thirds(grad_sq) + thirds(dir_sq) + thirds(block_sq), 1):
        extra = jnp.where(line == number, values, extra)
    got = swap(
        jnp.concatenate(
            [jnp.broadcast_to(direction[None], (ny * npair, half, width)), outer, extra], axis=1
        ),
        ("y", "pair"),
    )
    got = got.reshape(blocks, npair, half + outer_rows + 16, width)
    extra = got[:, :, half + outer_rows :].astype(f32)
    grad_sq = jnp.sum(extra[:, :1, 1:4], axis=(1, 2, 3), keepdims=True)
    dir_sq = jnp.sum(extra[:, :, 4:7], axis=(1, 2, 3), keepdims=True)
    layer_sq = jnp.sum(extra[:, :1, 7:10], keepdims=True)
    factor = jnp.sqrt(grad_sq / dir_sq) / jnp.sqrt(layer_sq / (features * width * tensors))
    update = (got[:, :, :half].astype(f32) * factor).astype(bf16)
    update = update.reshape(blocks, npair, half // mine, mine, width).transpose(0, 2, 1, 3, 4)
    update = update.reshape(blocks * BLOCK, width)
    outer = got[:, :, half : half + outer_rows].astype(f32)
    outer = outer.reshape(blocks, npair, mine, half).transpose(0, 2, 1, 3)
    outer = outer.reshape(blocks, mine, BLOCK)
    left_new = stat_decay * left_stats + ((1.0 - stat_decay) / width) * outer[None]
    right_new = stat_decay * right_stats + ((1.0 - stat_decay) / BLOCK) * extra[None, :, 0, :1]
    return (update, left_new, right_new)


def solution(mesh):
    dp, tensor = mesh.devices.shape
    blocks, mid, pair = 4, 4, 2
    fine = Mesh(
        mesh.devices.reshape(blocks, dp // (blocks * mid * pair), mid, pair, tensor),
        ("y", "far", "mid", "pair", "tensor"),
    )
    dp = ("y", *Z)
    in_specs = (
        P(dp, None),
        P(dp, "tensor"),
        P("tensor", None, dp, None),
        P("tensor", None, dp, None),
        P("tensor", None, dp, None),
        P("tensor", None, None, None),
    )
    out_specs = (P(None, "tensor"), P("tensor", None, dp, None), P("tensor", None, dp, None))
    return jax.shard_map(shards, mesh=fine, in_specs=in_specs, out_specs=out_specs, check_vma=False)
```

time: 189 us -> 186 us (0.984)
  starting transfers between devices: 42.9 us -> 34.9 us
  blocking collectives: 108 us -> 112 us
    all_to_all x4, starting transfers between devices: 42.9 us -> 34.9 us  [swap(): return lax.all_to_all(pieces, axis, 0, 0, tiled=True)]
    all_to_all x2, blocking collectives: 50.4 us -> 55.6 us  [swap(): return lax.all_to_all(pieces, axis, 0, 0, tiled=True)]
  transfers between devices with their start and end apart: 4 -> 4, of which waited for: 2 -> 2; matrix products, arithmetic and copies ran while one was open for 0% -> 1% of each run, Pallas kernels for 0% -> 0%
where the time goes in v8:
time: 186 us; the launch traced here: 185 us
  blocking collectives  112 us (60%)
  starting transfers between devices  34.9 us (19%)
  waiting for transfers between devices  23.4 us (13%)
  other arithmetic  5.24 us (3%)
  matrix products  4.2 us (2%)
  local copies, waits for them, and re-layouts  3.77 us (2%)
    all_to_all x2, blocking collectives, swap(): return lax.all_to_all(pieces, axis, 0, 0, tiled=True)  55.6 us
    all_gather x1, blocking collectives, shards(): roots = lax.all_gather(roots, 'far', axis=0, tiled=True)  36.3 us
    all_to_all x4, starting transfers between devices, swap(): return lax.all_to_all(pieces, axis, 0, 0, tiled=True)  34.9 us
    all_to_all x4, waiting for transfers between devices, swap(): return lax.all_to_all(pieces, axis, 0, 0, tiled=True)  23.4 us
    psum x1, blocking collectives, shards(): block_sq = lax.psum(grad_sq, 'tensor')  20.2 us
  transfers between devices with their start and end apart: 4, of which 2 were waited for; matrix products, arithmetic and copies ran while one was open for 1% of the time, Pallas kernels for 0%

profile of v8, /device:TPU:1, one launch (start us, length us, event | category | flops | bytes accessed | tf_op | source)
XLA Modules:
  0.0 185.1 jit_solution(1841180905332530922)
XLA Ops:
  0.6 0.0 copy-start
  0.6 1.1 convert_element_type.87
  1.7 0.5 copy-done
  2.3 1.6 convolution_convert_fusion
  3.9 1.1 pad_maximum_fusion
  5.0 0.0 copy-start.1
  5.0 6.5 %all-to-all-start = ((bf16[8,576,128]{2,1,0:T(8,128)(2,1)}), bf16[8,576,128]{2,1,0:T(8,128)(2,1)S(1)}, u32[]{:S(2)}, u32[]{:S(2)}) async-start(bf16[8,576,128]{2,1,0:T(8,128)(2,1)} %pad_maximum_fusion), calls=%async_computation | async-start | bytes 2359296 | tf_op jit(solution)/shard_map/all_to_all | solution.py:15
  11.5 11.1 %all-to-all-done = bf16[8,576,128]{2,1,0:T(8,128)(2,1)S(1)} async-done(((bf16[8,576,128]{2,1,0:T(8,128)(2,1)}), bf16[8,576,128]{2,1,0:T(8,128)(2,1)S(1)}, u32[]{:S(2)}, u32[]{:S(2)}) %all-to-all-start) | async-done | bytes 1179680 | tf_op jit(solution)/shard_map/all_to_all | solution.py:15
  22.7 0.3 select_reduce_fusion
  23.0 0.0 copy-done.1
  23.0 0.9 fusion
  23.9 16.0 %all-to-all-start.1 = ((bf16[4,128,128]{2,1,0:T(8,128)(2,1)}), bf16[4,128,128]{2,1,0:T(8,128)(2,1)S(1)}, u32[]{:S(2)}, u32[]{:S(2)}) async-start(bf16[4,128,128]{2,1,0:T(8,128)(2,1)} %bitcast.2), calls=%async_computation.1 | async-start | bytes 262144 | tf_op jit(solution)/shard_map/all_to_all | solution.py:15
  40.0 36.3 %all_gather.3 = bf16[128,1024]{1,0:T(8,128)(2,1)S(1)} all-gather(bf16[32,1024]{1,0:T(8,128)(2,1)S(1)} %reshape.158), channel_id=1, replica_groups=mesh['y'=4,'far'=4,'mid'=4,'pair'=2,'tensor'=8] {'far'}, dimensions={0}, use_global_device_ids=true | all-gather | bytes 327680 | tf_op jit(solution)/shard_map/all_gather | solution.py:67
  76.2 0.0 all-to-all-done.1
  76.3 34.9 %all_to_all.30 = bf16[4,128,128]{2,1,0:T(8,128)(2,1)S(1)} all-to-all(bf16[4,128,128]{2,1,0:T(8,128)(2,1)S(1)} %broadcast_in_dim.131), channel_id=1, replica_groups=mesh['y'=4,'far'=4,'mid'=4,'pair'=2,'tensor'=8] {'far'}, dimensions={0} | all-to-all | bytes 262144 | tf_op jit(solution)/shard_map/all_to_all | solution.py:15
  111.2 0.7 broadcast_in_dim.132
  112.0 9.0 %all-to-all-start.3 = ((bf16[8,128,128]{2,1,0:T(8,128)(2,1)}), bf16[8,128,128]{2,1,0:T(8,128)(2,1)S(1)}, u32[]{:S(2)}, u32[]{:S(2)}) async-start(bf16[8,128,128]{2,1,0:T(8,128)(2,1)} %broadcast_in_dim.132), calls=%async_computation.3 | async-start | bytes 524288 | tf_op jit(solution)/shard_map/all_to_all | solution.py:15
  121.1 12.3 %all-to-all-done.3 = bf16[8,128,128]{2,1,0:T(8,128)(2,1)S(1)} async-done(((bf16[8,128,128]{2,1,0:T(8,128)(2,1)}), bf16[8,128,128]{2,1,0:T(8,128)(2,1)S(1)}, u32[]{:S(2)}, u32[]{:S(2)}) %all-to-all-start.3) | async-done | bytes 262176 | tf_op jit(solution)/shard_map/all_to_all | solution.py:15
  133.3 0.2 fusion.17
  133.6 1.0 convolution_convert_fusion.2
  134.6 0.7 broadcast_in_dim.133
  135.3 3.3 %all-to-all-start.4 = ((bf16[4,128,128]{2,1,0:T(8,128)(2,1)}), bf16[4,128,128]{2,1,0:T(8,128)(2,1)S(1)}, u32[]{:S(2)}, u32[]{:S(2)}) async-start(bf16[4,128,128]{2,1,0:T(8,128)(2,1)} %broadcast_in_dim.133), calls=%async_computation.4 | async-start | bytes 262144 | tf_op jit(solution)/shard_map/all_to_all | solution.py:15
  138.6 0.2 convolution_convert_fusion.1
  138.8 0.1 reshape.162
  138.9 0.1 copy.23
  139.0 0.1 dot_general.28
  139.1 0.2 fusion.2
  139.4 0.2 multiply_reduce_fusion
  139.6 20.2 %psum.7 = f32[128]{0:T(128)S(1)} all-reduce(f32[128]{0:T(128)S(1)} %multiply_reduce_fusion), channel_id=1, replica_groups=mesh['y'=4,'far'=4,'mid'=4,'pair'=2,'tensor'=8] {'tensor'}, use_global_device_ids=true, to_apply=%region_4.5 | all-reduce | flops 128 | bytes 1024 | tf_op jit(solution)/shard_map/psum | solution.py:79
  159.7 0.0 all-to-all-done.4
  159.7 0.1 multiply_reduce_fusion.1
  159.9 0.1 select_select_fusion
  160.0 0.1 broadcast_in_dim.135
  160.1 0.1 pad_maximum_fusion.1
  160.2 20.7 %all_to_all.31 = bf16[8,560,128]{2,1,0:T(8,128)(2,1)S(1)} all-to-all(bf16[8,560,128]{2,1,0:T(8,128)(2,1)S(1)} %pad_maximum_fusion.1), channel_id=1, replica_groups=mesh['y'=4,'far'=4,'mid'=4,'pair'=2,'tensor'=8] {'y','pair'}, dimensions={0} | all-to-all | bytes 2293760 | tf_op jit(solution)/shard_map/all_to_all | solution.py:15
  180.9 0.1 slice_reduce_fusion
  181.0 0.6 slice_reduce_fusion.1
  182.3 0.0 copy-start.3
  182.3 0.0 copy-start.2
  182.3 0.3 fusion.1
  182.6 1.2 copy.25
  183.8 0.0 copy-done.3
  183.8 0.6 multiply_add_fusion
  184.4 0.0 copy-done.2
  184.4 0.7 bitcast_add_fusion
  (25 shorter events, 0.3 us)
Async XLA Ops:
  0.6 1.7 copy-start
  5.0 18.0 %copy-start.1 = (bf16[256,128]{1,0:T(8,128)(2,1)S(1)}, bf16[256,128]{1,0:T(8,128)(2,1)}, u32[]{:S(2)}) copy-start(bf16[256,128]{1,0:T(8,128)(2,1)} %param.7) | copy-start | bytes 196612
  5.0 17.6 %all-to-all-start = ((bf16[8,576,128]{2,1,0:T(8,128)(2,1)}), bf16[8,576,128]{2,1,0:T(8,128)(2,1)S(1)}, u32[]{:S(2)}, u32[]{:S(2)}) async-start(bf16[8,576,128]{2,1,0:T(8,128)(2,1)} %pad_maximum_fusion), calls=%async_computation | async-start | bytes 2359296 | tf_op jit(solution)/shard_map/all_to_all | solution.py:15
  23.9 52.3 %all-to-all-start.1 = ((bf16[4,128,128]{2,1,0:T(8,128)(2,1)}), bf16[4,128,128]{2,1,0:T(8,128)(2,1)S(1)}, u32[]{:S(2)}, u32[]{:S(2)}) async-start(bf16[4,128,128]{2,1,0:T(8,128)(2,1)} %bitcast.2), calls=%async_computation.1 | async-start | bytes 262144 | tf_op jit(solution)/shard_map/all_to_all | solution.py:15
  112.0 21.4 %all-to-all-start.3 = ((bf16[8,128,128]{2,1,0:T(8,128)(2,1)}), bf16[8,128,128]{2,1,0:T(8,128)(2,1)S(1)}, u32[]{:S(2)}, u32[]{:S(2)}) async-start(bf16[8,128,128]{2,1,0:T(8,128)(2,1)} %broadcast_in_dim.132), calls=%async_computation.3 | async-start | bytes 524288 | tf_op jit(solution)/shard_map/all_to_all | solution.py:15
  135.3 24.4 %all-to-all-start.4 = ((bf16[4,128,128]{2,1,0:T(8,128)(2,1)}), bf16[4,128,128]{2,1,0:T(8,128)(2,1)S(1)}, u32[]{:S(2)}, u32[]{:S(2)}) async-start(bf16[4,128,128]{2,1,0:T(8,128)(2,1)} %broadcast_in_dim.133), calls=%async_computation.4 | async-start | bytes 262144 | tf_op jit(solution)/shard_map/all_to_all | solution.py:15
  182.3 1.5 copy-start.3
  182.3 2.1 %copy-start.2 = (f32[1,4,8,1024]{3,2,1,0:T(8,128)S(1)}, f32[1,4,8,1024]{3,2,1,0:T(8,128)}, u32[]{:S(2)}) copy-start(f32[1,4,8,1024]{3,2,1,0:T(8,128)} %param.8) | copy-start | bytes 393220

commit v9 on v7

--- a/solution.py
+++ b/solution.py
@@ -8,7 +8,7 @@
 highest = lax.Precision.HIGHEST
 f32 = jnp.float32
 bf16 = jnp.bfloat16
-Z = ("far", "near")
+Z = ("far", "mid", "pair")
 
 
 def swap(pieces, axis):
@@ -35,33 +35,42 @@
 def shards(activations, cotangents, left_stats, right_stats, left_roots, right_roots):
     ny = lax.axis_size("y")
     nfar = lax.axis_size("far")
-    nnear = lax.axis_size("near")
-    nz = nfar * nnear
+    nmid = lax.axis_size("mid")
+    npair = lax.axis_size("pair")
+    nz = nfar * nmid * npair
     tensors = lax.axis_size("tensor")
     y = lax.axis_index("y")
     z = lax.axis_index(Z)
+    pair = lax.axis_index("pair")
+    place = y * npair + pair
     features = activations.shape[1]
     width = cotangents.shape[1]
     blocks = features // BLOCK
     mine = left_roots.shape[2]
     root_rows = mine * (BLOCK // width)
 
-    partial = sum_tokens(activations, cotangents).astype(bf16).reshape(blocks, BLOCK, width)
-    roots = left_roots[0].astype(bf16).reshape(blocks, root_rows, width)
-    got = swap(jnp.concatenate([partial, roots], axis=1), "y")
-    roots = got[:, BLOCK:].reshape(ny * mine, BLOCK)
-    kept = sum_tokens(lax.dynamic_slice_in_dim(activations, y * BLOCK, BLOCK, 1), cotangents)
-    others = jnp.where((jnp.arange(ny) == y)[:, None, None], 0.0, got[:, :BLOCK].astype(f32))
+    half = BLOCK // npair
+    partial = sum_tokens(activations, cotangents).astype(bf16)
+    partial = partial.reshape(blocks * npair, half, width)
+    roots = left_roots[0].astype(bf16).reshape(blocks, 1, root_rows, width)
+    roots = jnp.broadcast_to(roots, (blocks, npair, root_rows, width))
+    roots = roots.reshape(blocks * npair, root_rows, width)
+    got = swap(jnp.concatenate([partial, roots], axis=1), ("y", "pair"))
+    roots = got[:, half:].reshape(ny, npair, root_rows, width)
+    roots = lax.dynamic_index_in_dim(roots, pair, 1, keepdims=False).reshape(ny * mine, BLOCK)
+    kept = sum_tokens(lax.dynamic_slice_in_dim(activations, place * half, half, 1), cotangents)
+    others = jnp.arange(ny * npair) == place
+    others = jnp.where(others[:, None, None], 0.0, got[:, :half].astype(f32))
     column_part = kept + jnp.sum(others, axis=0)
 
-    pieces = column_part.astype(bf16).reshape(nnear, BLOCK // nnear, width)
+    pieces = column_part.astype(bf16).reshape(nmid, half // nmid, width)
     pieces, roots = lax.optimization_barrier((pieces, roots))
     roots = lax.all_gather(roots, "far", axis=0, tiled=True)
-    got, roots = lax.optimization_barrier((swap(pieces, "near"), roots))
+    got, roots = lax.optimization_barrier((swap(pieces, "mid"), roots))
     part = jnp.sum(got.astype(f32), axis=0).astype(bf16)
     got = everyone(part, "far")
     own = jnp.sum(got.astype(f32), axis=0).astype(bf16)
-    gradient = everyone(own, "near").reshape(BLOCK, width)
+    gradient = everyone(own, ("pair", "mid")).reshape(BLOCK, width)
 
     inner = lax.dot_general(
         gradient, gradient, (((0,), (0,)), ((), ())), preferred_element_type=f32
@@ -73,7 +82,7 @@
     right = lax.dynamic_index_in_dim(right_roots[0], y, 0, keepdims=False)
     mixed = jnp.dot(roots, gradient, preferred_element_type=f32)
     direction = jnp.dot(mixed, right, precision=highest).astype(bf16)
-    direction = everyone(direction, "near").reshape(nnear, nfar, ny, mine, width)
+    direction = everyone(direction, ("mid", "pair")).reshape(nmid * npair, nfar, ny, mine, width)
     direction = direction.transpose(2, 1, 0, 3, 4).reshape(BLOCK, width)
     wide = direction.astype(f32)
     dir_sq = jnp.sum(wide * wide, axis=0)
@@ -110,10 +119,10 @@
 
 def solution(mesh):
     dp, tensor = mesh.devices.shape
-    blocks, near = 4, 8
+    blocks, mid, pair = 4, 4, 2
     fine = Mesh(
-        mesh.devices.reshape(blocks, dp // (blocks * near), near, tensor),
-        ("y", "far", "near", "tensor"),
+        mesh.devices.reshape(blocks, dp // (blocks * mid * pair), mid, pair, tensor),
+        ("y", "far", "mid", "pair", "tensor"),
     )
     dp = ("y", *Z)
     in_specs = (

time: 189 us -> 186 us (0.984); the launches traced: 188 us -> 183 us
  starting transfers between devices: 42.9 us -> 35 us
    all_to_all x4, starting transfers between devices: 42.9 us -> 35 us  [swap(): return lax.all_to_all(pieces, axis, 0, 0, tiled=True)]
where the time goes in v9:
time: 186 us; the launch traced here: 183 us
  blocking collectives  109 us (59%)
  starting transfers between devices  35 us (19%)
  waiting for transfers between devices  23.4 us (13%)
  other arithmetic  7.06 us (4%)
  matrix products  4.2 us (2%)
  local copies, waits for them, and re-layouts  2.61 us (1%)
    all_to_all x2, blocking collectives, swap(): return lax.all_to_all(pieces, axis, 0, 0, tiled=True)  52.3 us
    all_gather x1, blocking collectives, shards(): roots = lax.all_gather(roots, 'far', axis=0, tiled=True)  36.3 us
    all_to_all x4, starting transfers between devices, swap(): return lax.all_to_all(pieces, axis, 0, 0, tiled=True)  35 us
    all_to_all x4, waiting for transfers between devices, swap(): return lax.all_to_all(pieces, axis, 0, 0, tiled=True)  23.4 us
    psum x1, blocking collectives, shards(): block_sq = lax.psum(grad_sq, 'tensor')  20.2 us
  transfers between devices with their start and end apart: 4, of which 2 were waited for; matrix products, arithmetic and copies ran while one was open for 0% of the time, Pallas kernels for 0%

profile of v9, /device:TPU:1, one launch (start us, length us, event | category | flops | bytes accessed | tf_op | source)
XLA Modules:
  0.0 182.5 jit_solution(1503559569913805424)
XLA Ops:
  0.6 0.0 copy-start
  0.6 1.1 convert_element_type.80
  1.7 0.5 copy-done
  2.3 1.6 convolution_convert_fusion
  3.9 1.1 pad_maximum_fusion
  5.0 0.0 copy-start.1
  5.0 6.5 %all-to-all-start = ((bf16[8,576,128]{2,1,0:T(8,128)(2,1)}), bf16[8,576,128]{2,1,0:T(8,128)(2,1)S(1)}, u32[]{:S(2)}, u32[]{:S(2)}) async-start(bf16[8,576,128]{2,1,0:T(8,128)(2,1)} %pad_maximum_fusion), calls=%async_computation | async-start | bytes 2359296 | tf_op jit(solution)/shard_map/all_to_all | solution.py:15
  11.5 11.1 %all-to-all-done = bf16[8,576,128]{2,1,0:T(8,128)(2,1)S(1)} async-done(((bf16[8,576,128]{2,1,0:T(8,128)(2,1)}), bf16[8,576,128]{2,1,0:T(8,128)(2,1)S(1)}, u32[]{:S(2)}, u32[]{:S(2)}) %all-to-all-start) | async-done | bytes 1179680 | tf_op jit(solution)/shard_map/all_to_all | solution.py:15
  22.7 0.3 select_reduce_fusion
  23.0 0.0 copy-done.1
  23.0 0.9 fusion
  23.9 16.0 %all-to-all-start.1 = ((bf16[4,128,128]{2,1,0:T(8,128)(2,1)}), bf16[4,128,128]{2,1,0:T(8,128)(2,1)S(1)}, u32[]{:S(2)}, u32[]{:S(2)}) async-start(bf16[4,128,128]{2,1,0:T(8,128)(2,1)} %bitcast.2), calls=%async_computation.1 | async-start | bytes 262144 | tf_op jit(solution)/shard_map/all_to_all | solution.py:15
  40.0 36.3 %all_gather.3 = bf16[128,1024]{1,0:T(8,128)(2,1)S(1)} all-gather(bf16[32,1024]{1,0:T(8,128)(2,1)S(1)} %reshape.144), channel_id=1, replica_groups=mesh['y'=4,'far'=4,'mid'=4,'pair'=2,'tensor'=8] {'far'}, dimensions={0}, use_global_device_ids=true | all-gather | bytes 327680 | tf_op jit(solution)/shard_map/all_gather | solution.py:68
  76.2 0.0 all-to-all-done.1
  76.3 34.9 %all_to_all.30 = bf16[4,128,128]{2,1,0:T(8,128)(2,1)S(1)} all-to-all(bf16[4,128,128]{2,1,0:T(8,128)(2,1)S(1)} %broadcast_in_dim.135), channel_id=1, replica_groups=mesh['y'=4,'far'=4,'mid'=4,'pair'=2,'tensor'=8] {'far'}, dimensions={0} | all-to-all | bytes 262144 | tf_op jit(solution)/shard_map/all_to_all | solution.py:15
  111.2 0.7 broadcast_in_dim.136
  112.0 9.0 %all-to-all-start.3 = ((bf16[8,128,128]{2,1,0:T(8,128)(2,1)}), bf16[8,128,128]{2,1,0:T(8,128)(2,1)S(1)}, u32[]{:S(2)}, u32[]{:S(2)}) async-start(bf16[8,128,128]{2,1,0:T(8,128)(2,1)} %broadcast_in_dim.136), calls=%async_computation.3 | async-start | bytes 524288 | tf_op jit(solution)/shard_map/all_to_all | solution.py:15
  121.0 12.3 %all-to-all-done.3 = bf16[8,128,128]{2,1,0:T(8,128)(2,1)S(1)} async-done(((bf16[8,128,128]{2,1,0:T(8,128)(2,1)}), bf16[8,128,128]{2,1,0:T(8,128)(2,1)S(1)}, u32[]{:S(2)}, u32[]{:S(2)}) %all-to-all-start.3) | async-done | bytes 262176 | tf_op jit(solution)/shard_map/all_to_all | solution.py:15
  133.3 0.2 fusion.15
  133.6 1.0 convolution_convert_fusion.2
  134.6 0.7 broadcast_in_dim.137
  135.4 3.4 %all-to-all-start.4 = ((bf16[8,128,128]{2,1,0:T(8,128)(2,1)}), bf16[8,128,128]{2,1,0:T(8,128)(2,1)S(1)}, u32[]{:S(2)}, u32[]{:S(2)}) async-start(bf16[8,128,128]{2,1,0:T(8,128)(2,1)} %broadcast_in_dim.137), calls=%async_computation.4 | async-start | bytes 524288 | tf_op jit(solution)/shard_map/all_to_all | solution.py:15
  138.8 0.2 convolution_convert_fusion.1
  139.0 0.1 reshape.148
  139.1 0.1 copy.19
  139.2 0.2 fusion.16
  139.5 0.2 multiply_reduce_fusion.1
  139.7 20.2 %psum.7 = f32[128]{0:T(128)S(1)} all-reduce(f32[128]{0:T(128)S(1)} %multiply_reduce_fusion.1), channel_id=1, replica_groups=mesh['y'=4,'far'=4,'mid'=4,'pair'=2,'tensor'=8] {'tensor'}, use_global_device_ids=true, to_apply=%region_4.5 | all-reduce | flops 128 | bytes 1024 | tf_op jit(solution)/shard_map/psum | solution.py:80
  159.8 0.0 all-to-all-done.4
  159.8 0.1 copy.18
  159.9 0.2 multiply_reduce_fusion
  160.1 0.1 select_select_fusion
  160.1 0.1 broadcast_in_dim.139
  160.3 0.1 pad_maximum_fusion.1
  160.4 0.0 copy-start.2
  160.4 17.4 %all_to_all.31 = bf16[4,1104,128]{2,1,0:T(8,128)(2,1)S(1)} all-to-all(bf16[4,1104,128]{2,1,0:T(8,128)(2,1)S(1)} %pad_maximum_fusion.1), channel_id=1, replica_groups=mesh['y'=4,'far'=4,'mid'=4,'pair'=2,'tensor'=8] {'y'}, dimensions={0} | all-to-all | bytes 2260992 | tf_op jit(solution)/shard_map/all_to_all | solution.py:15
  177.7 0.6 slice_reduce_fusion
  179.1 1.6 multiply_add_fusion
  180.7 0.0 copy-done.2
  180.7 0.6 multiply_add_fusion.1
  181.3 1.3 multiply_convert_fusion
  (23 shorter events, 0.3 us)
Async XLA Ops:
  0.6 1.7 copy-start
  5.0 18.0 %copy-start.1 = (bf16[256,128]{1,0:T(8,128)(2,1)S(1)}, bf16[256,128]{1,0:T(8,128)(2,1)}, u32[]{:S(2)}) copy-start(bf16[256,128]{1,0:T(8,128)(2,1)} %param.7) | copy-start | bytes 196612
  5.0 17.6 %all-to-all-start = ((bf16[8,576,128]{2,1,0:T(8,128)(2,1)}), bf16[8,576,128]{2,1,0:T(8,128)(2,1)S(1)}, u32[]{:S(2)}, u32[]{:S(2)}) async-start(bf16[8,576,128]{2,1,0:T(8,128)(2,1)} %pad_maximum_fusion), calls=%async_computation | async-start | bytes 2359296 | tf_op jit(solution)/shard_map/all_to_all | solution.py:15
  23.9 52.3 %all-to-all-start.1 = ((bf16[4,128,128]{2,1,0:T(8,128)(2,1)}), bf16[4,128,128]{2,1,0:T(8,128)(2,1)S(1)}, u32[]{:S(2)}, u32[]{:S(2)}) async-start(bf16[4,128,128]{2,1,0:T(8,128)(2,1)} %bitcast.2), calls=%async_computation.1 | async-start | bytes 262144 | tf_op jit(solution)/shard_map/all_to_all | solution.py:15
  112.0 21.4 %all-to-all-start.3 = ((bf16[8,128,128]{2,1,0:T(8,128)(2,1)}), bf16[8,128,128]{2,1,0:T(8,128)(2,1)S(1)}, u32[]{:S(2)}, u32[]{:S(2)}) async-start(bf16[8,128,128]{2,1,0:T(8,128)(2,1)} %broadcast_in_dim.136), calls=%async_computation.3 | async-start | bytes 524288 | tf_op jit(solution)/shard_map/all_to_all | solution.py:15
  135.4 24.5 %all-to-all-start.4 = ((bf16[8,128,128]{2,1,0:T(8,128)(2,1)}), bf16[8,128,128]{2,1,0:T(8,128)(2,1)S(1)}, u32[]{:S(2)}, u32[]{:S(2)}) async-start(bf16[8,128,128]{2,1,0:T(8,128)(2,1)} %broadcast_in_dim.137), calls=%async_computation.4 | async-start | bytes 524288 | tf_op jit(solution)/shard_map/all_to_all | solution.py:15
  160.4 20.3 %copy-start.2 = (f32[1,4,1,128]{3,2,1,0:T(1,128)S(1)}, f32[1,4,1,128]{3,2,1,0:T(1,128)}, u32[]{:S(2)}) copy-start(f32[1,4,1,128]{3,2,1,0:T(1,128)} %param.9) | copy-start | bytes 6148

commit v10 on v9

--- a/solution.py
+++ b/solution.py
@@ -52,23 +52,25 @@
     half = BLOCK // npair
     partial = sum_tokens(activations, cotangents).astype(bf16)
     partial = partial.reshape(blocks * npair, half, width)
-    roots = left_roots[0].astype(bf16).reshape(blocks, 1, root_rows, width)
-    roots = jnp.broadcast_to(roots, (blocks, npair, root_rows, width))
-    roots = roots.reshape(blocks * npair, root_rows, width)
-    got = swap(jnp.concatenate([partial, roots], axis=1), ("y", "pair"))
-    roots = got[:, half:].reshape(ny, npair, root_rows, width)
-    roots = lax.dynamic_index_in_dim(roots, pair, 1, keepdims=False).reshape(ny * mine, BLOCK)
+    partial, roots = lax.optimization_barrier((partial, left_roots[0].astype(bf16)))
+    roots = lax.all_gather(roots, "far")
+    got, roots = lax.optimization_barrier((swap(partial, ("y", "pair")), roots))
     kept = sum_tokens(lax.dynamic_slice_in_dim(activations, place * half, half, 1), cotangents)
     others = jnp.arange(ny * npair) == place
-    others = jnp.where(others[:, None, None], 0.0, got[:, :half].astype(f32))
+    others = jnp.where(others[:, None, None], 0.0, got.astype(f32))
     column_part = kept + jnp.sum(others, axis=0)
 
-    pieces = column_part.astype(bf16).reshape(nmid, half // nmid, width)
-    pieces, roots = lax.optimization_barrier((pieces, roots))
-    roots = lax.all_gather(roots, "far", axis=0, tiled=True)
-    got, roots = lax.optimization_barrier((swap(pieces, "mid"), roots))
+    got = swap(column_part.astype(bf16).reshape(nmid, half // nmid, width), "mid")
     part = jnp.sum(got.astype(f32), axis=0).astype(bf16)
-    got = everyone(part, "far")
+    part, roots = lax.optimization_barrier((part, roots))
+    held = [lax.dynamic_index_in_dim(roots, y, 1, keepdims=False)]
+    for step in range(1, ny):
+        turn = [(i, (i - step) % ny) for i in range(ny)]
+        block = lax.dynamic_index_in_dim(roots, (y - step) % ny, 1, keepdims=False)
+        held.append(lax.ppermute(block, "y", turn))
+    roots = lax.dynamic_slice_in_dim(jnp.stack(held + held), (ny - y) % ny, ny, 0)
+    roots = roots.reshape(ny * nfar * mine, BLOCK)
+    got, roots = lax.optimization_barrier((everyone(part, "far"), roots))
     own = jnp.sum(got.astype(f32), axis=0).astype(bf16)
     gradient = everyone(own, ("pair", "mid")).reshape(BLOCK, width)
 
@@ -77,13 +79,13 @@
     )
     wide = gradient.astype(f32)
     grad_sq = jnp.sum(wide * wide, axis=0)
-    block_sq = lax.psum(grad_sq, "tensor")
+    block_sq = jnp.sum(lax.all_gather(grad_sq, "tensor"), axis=0)
 
     right = lax.dynamic_index_in_dim(right_roots[0], y, 0, keepdims=False)
     mixed = jnp.dot(roots, gradient, preferred_element_type=f32)
     direction = jnp.dot(mixed, right, precision=highest).astype(bf16)
-    direction = everyone(direction, ("mid", "pair")).reshape(nmid * npair, nfar, ny, mine, width)
-    direction = direction.transpose(2, 1, 0, 3, 4).reshape(BLOCK, width)
+    direction = everyone(direction, ("mid", "pair")).reshape(nmid * npair, ny, nfar, mine, width)
+    direction = direction.transpose(1, 2, 0, 3, 4).reshape(BLOCK, width)
     wide = direction.astype(f32)
     dir_sq = jnp.sum(wide * wide, axis=0)
 

time: 186 us -> 180 us (0.968)
  blocking collectives: 109 us -> 107 us
    all_gather x1 -> x2, blocking collectives: 36.3 us -> 72.1 us  [the longest x1 51.4 us: shards(): roots = lax.all_gather(roots, 'far')]
    psum x1 -> x0, blocking collectives: 20.2 us -> none  [shards(): block_sq = lax.psum(grad_sq, 'tensor')]
    all_to_all x2, blocking collectives: 52.3 us -> 34.6 us  [swap(): return lax.all_to_all(pieces, axis, 0, 0, tiled=True)]
    all_to_all x4, starting transfers between devices: 35 us -> 24.5 us  [swap(): return lax.all_to_all(pieces, axis, 0, 0, tiled=True)]
    ppermute x0 -> x3, starting transfers between devices: none -> 8.68 us  [shards(): held.append(lax.ppermute(block, 'y', turn))]
    all_to_all x4, waiting for transfers between devices: 23.4 us -> 20.1 us  [swap(): return lax.all_to_all(pieces, axis, 0, 0, tiled=True)]
    ppermute x0 -> x3, waiting for transfers between devices: none -> 1.92 us  [shards(): held.append(lax.ppermute(block, 'y', turn))]
  transfers between devices with their start and end apart: 4 -> 7, of which waited for: 2 -> 3; matrix products, arithmetic and copies ran while one was open for 0% -> 1% of each run, Pallas kernels for 0% -> 0%
where the time goes in v10:
time: 180 us; the launch traced here: 177 us
  blocking collectives  107 us (59%)
  starting transfers between devices  33.2 us (18%)
  waiting for transfers between devices  22 us (12%)
  other arithmetic  6 us (3%)
  matrix products  5.16 us (3%)
  local copies, waits for them, and re-layouts  2.6 us (1%)
    all_gather x1, blocking collectives, shards(): roots = lax.all_gather(roots, 'far')  51.4 us
    all_to_all x2, blocking collectives, swap(): return lax.all_to_all(pieces, axis, 0, 0, tiled=True)  34.6 us
    all_to_all x4, starting transfers between devices, swap(): return lax.all_to_all(pieces, axis, 0, 0, tiled=True)  24.5 us
    all_gather x1, blocking collectives, shards(): block_sq = jnp.sum(lax.all_gather(grad_sq, 'tensor'), axis=0)  20.7 us
    all_to_all x4, waiting for transfers between devices, swap(): return lax.all_to_all(pieces, axis, 0, 0, tiled=True)  20.1 us
    ppermute x3, starting transfers between devices, shards(): held.append(lax.ppermute(block, 'y', turn))  8.68 us
  transfers between devices with their start and end apart: 7, of which 3 were waited for; matrix products, arithmetic and copies ran while one was open for 1% of the time, Pallas kernels for 0%

profile of v10, /device:TPU:1, one launch (start us, length us, event | category | flops | bytes accessed | tf_op | source)
XLA Modules:
  0.0 177.5 jit_solution(7079507965718111533)
XLA Ops:
  0.6 0.0 copy-start
  0.6 1.1 convert_bitcast_fusion
  1.7 0.6 copy-done
  2.3 2.6 %convolution_convert_fusion = bf16[4096,128]{1,0:T(8,128)(2,1)} fusion(bf16[256,4096]{1,0:T(8,128)(2,1)S(1)} %copy-done, bf16[256,128]{1,0:T(8,128)(2,1)} %param.7), kind=kOutput, calls=%fused_computation | convolution fusion | flops 268959744 | bytes 3211264 | tf_op jit(solution)/shard_map/dot_general | solution.py:32
  4.9 0.0 copy-start.1
  4.9 6.5 %all-to-all-start = ((bf16[8,512,128]{2,1,0:T(8,128)(2,1)}), bf16[8,512,128]{2,1,0:T(8,128)(2,1)S(1)}, u32[]{:S(2)}, u32[]{:S(2)}) async-start(bf16[8,512,128]{2,1,0:T(8,128)(2,1)} %bitcast), calls=%async_computation | async-start | bytes 2097152 | tf_op jit(solution)/shard_map/all_to_all | solution.py:15
  11.4 51.4 %all-gather = bf16[16,8,1024]{2,1,0:T(8,128)(2,1)S(1)} all-gather(bf16[4,8,1024]{2,1,0:T(8,128)(2,1)S(1)} %convert_bitcast_fusion), channel_id=2, replica_groups=mesh['y'=4,'far'=4,'mid'=4,'pair'=2,'tensor'=8] {'far'}, dimensions={0}, use_global_device_ids=true | all-gather | bytes 327680 | tf_op jit(solution)/shard_map/all_gather | solution.py:56
  62.8 0.0 all-to-all-done
  62.8 0.3 select_reduce_fusion
  63.1 0.0 copy-done.1
  63.1 0.9 fusion
  64.1 3.3 %all-to-all-start.1 = ((bf16[4,128,128]{2,1,0:T(8,128)(2,1)}), bf16[4,128,128]{2,1,0:T(8,128)(2,1)S(1)}, u32[]{:S(2)}, u32[]{:S(2)}) async-start(bf16[4,128,128]{2,1,0:T(8,128)(2,1)} %bitcast.3), calls=%async_computation.1 | async-start | bytes 262144 | tf_op jit(solution)/shard_map/all_to_all | solution.py:15
  67.5 8.6 %all-to-all-done.1 = bf16[4,128,128]{2,1,0:T(8,128)(2,1)S(1)} async-done(((bf16[4,128,128]{2,1,0:T(8,128)(2,1)}), bf16[4,128,128]{2,1,0:T(8,128)(2,1)S(1)}, u32[]{:S(2)}, u32[]{:S(2)}) %all-to-all-start.1) | async-done | bytes 131104 | tf_op jit(solution)/shard_map/all_to_all | solution.py:15
  76.1 0.7 broadcast_in_dim.129
  76.7 11.3 %all-to-all-start.2 = ((bf16[4,128,128]{2,1,0:T(8,128)(2,1)}), bf16[4,128,128]{2,1,0:T(8,128)(2,1)S(1)}, u32[]{:S(2)}, u32[]{:S(2)}) async-start(bf16[4,128,128]{2,1,0:T(8,128)(2,1)} %broadcast_in_dim.129), calls=%async_computation.2 | async-start | bytes 262144 | tf_op jit(solution)/shard_map/all_to_all | solution.py:15
  88.0 1.9 %collective-permute-start.2 = (bf16[4,8,1024]{2,1,0:T(8,128)(2,1)S(1)}, bf16[4,8,1024]{2,1,0:T(8,128)(2,1)S(1)}, u32[]{:S(2)}, u32[]{:S(2)}) collective-permute-start(bf16[4,8,1024]{2,1,0:T(8,128)(2,1)S(1)} %get-tuple-element.31), channel_id=1, source_target_pairs={{0,256},{256,512},{512,768},{768,0},{1,257},{257,513},{513,769},{7... | collective-permute-start | bytes 196616 | tf_op jit(solution)/shard_map/ppermute | solution.py:70
  89.9 3.7 %collective-permute-start.1 = (bf16[4,8,1024]{2,1,0:T(8,128)(2,1)S(1)}, bf16[4,8,1024]{2,1,0:T(8,128)(2,1)S(1)}, u32[]{:S(2)}, u32[]{:S(2)}) collective-permute-start(bf16[4,8,1024]{2,1,0:T(8,128)(2,1)S(1)} %get-tuple-element.32), channel_id=1, source_target_pairs={{0,512},{256,768},{512,0},{768,256},{1,513},{257,769},{513,1},{769... | collective-permute-start | bytes 196616 | tf_op jit(solution)/shard_map/ppermute | solution.py:70
  93.6 3.1 %collective-permute-start = (bf16[4,8,1024]{2,1,0:T(8,128)(2,1)S(1)}, bf16[4,8,1024]{2,1,0:T(8,128)(2,1)S(1)}, u32[]{:S(2)}, u32[]{:S(2)}) collective-permute-start(bf16[4,8,1024]{2,1,0:T(8,128)(2,1)S(1)} %get-tuple-element.33), channel_id=1, source_target_pairs={{0,768},{256,0},{512,256},{768,512},{1,769},{257,1},{513,257},{769... | collective-permute-start | bytes 196616 | tf_op jit(solution)/shard_map/ppermute | solution.py:70
  96.7 1.9 %collective-permute-done = bf16[4,8,1024]{2,1,0:T(8,128)(2,1)S(1)} collective-permute-done((bf16[4,8,1024]{2,1,0:T(8,128)(2,1)S(1)}, bf16[4,8,1024]{2,1,0:T(8,128)(2,1)S(1)}, u32[]{:S(2)}, u32[]{:S(2)}) %collective-permute-start) | collective-permute-done | bytes 65568 | tf_op jit(solution)/shard_map/ppermute | solution.py:70
  98.7 0.0 collective-permute-done.1
  98.7 0.0 collective-permute-done.2
  98.8 11.5 %all-to-all-done.2 = bf16[4,128,128]{2,1,0:T(8,128)(2,1)S(1)} async-done(((bf16[4,128,128]{2,1,0:T(8,128)(2,1)}), bf16[4,128,128]{2,1,0:T(8,128)(2,1)S(1)}, u32[]{:S(2)}, u32[]{:S(2)}) %all-to-all-start.2) | async-done | bytes 131104 | tf_op jit(solution)/shard_map/all_to_all | solution.py:15
  110.4 16.8 %all_to_all.30 = bf16[8,128,128]{2,1,0:T(8,128)(2,1)S(1)} all-to-all(bf16[8,128,128]{2,1,0:T(8,128)(2,1)S(1)} %broadcast_in_dim.130), channel_id=1, replica_groups=mesh['y'=4,'far'=4,'mid'=4,'pair'=2,'tensor'=8] {'pair','mid'}, dimensions={0} | all-to-all | bytes 524288 | tf_op jit(solution)/shard_map/all_to_all | solution.py:15
  127.3 0.2 fusion.16
  127.5 1.0 convolution_convert_fusion.2
  128.5 0.7 broadcast_in_dim.131
  129.3 3.4 %all-to-all-start.4 = ((bf16[8,128,128]{2,1,0:T(8,128)(2,1)}), bf16[8,128,128]{2,1,0:T(8,128)(2,1)S(1)}, u32[]{:S(2)}, u32[]{:S(2)}) async-start(bf16[8,128,128]{2,1,0:T(8,128)(2,1)} %broadcast_in_dim.131), calls=%async_computation.4 | async-start | bytes 524288 | tf_op jit(solution)/shard_map/all_to_all | solution.py:15
  132.8 0.2 convolution_convert_fusion.1
  132.9 0.1 reshape.134
  133.0 0.1 copy.19
  133.1 0.2 fusion.17
  133.4 0.2 multiply_reduce_fusion.1
  133.6 20.7 %all-gather.2 = f32[8,1,128]{2,1,0:T(1,128)S(1)} all-gather(f32[1,1,128]{2,1,0:T(1,128)S(1)} %bitcast.73), channel_id=3, replica_groups=mesh['y'=4,'far'=4,'mid'=4,'pair'=2,'tensor'=8] {'tensor'}, dimensions={0}, use_global_device_ids=true | all-gather | bytes 4608 | tf_op jit(solution)/shard_map/all_gather | solution.py:82
  154.3 0.0 all-to-all-done.4
  154.3 0.2 multiply_reduce_fusion
  154.4 0.1 copy.18
  154.5 0.1 select_select_fusion
  154.6 0.1 broadcast_in_dim.133
  154.8 0.0 copy-start.2
  154.8 0.1 pad_maximum_fusion
  154.9 17.8 %all_to_all.31 = bf16[4,1104,128]{2,1,0:T(8,128)(2,1)S(1)} all-to-all(bf16[4,1104,128]{2,1,0:T(8,128)(2,1)S(1)} %pad_maximum_fusion), channel_id=1, replica_groups=mesh['y'=4,'far'=4,'mid'=4,'pair'=2,'tensor'=8] {'y'}, dimensions={0} | all-to-all | bytes 2260992 | tf_op jit(solution)/shard_map/all_to_all | solution.py:15
  172.7 0.6 slice_reduce_fusion
  174.0 0.0 copy-done.2
  174.0 0.6 multiply_add_fusion.1
  174.6 1.6 multiply_add_fusion
  176.2 1.3 multiply_convert_fusion
  (29 shorter events, 0.3 us)
Async XLA Ops:
  0.6 1.7 copy-start
  4.9 58.2 %copy-start.1 = (bf16[256,128]{1,0:T(8,128)(2,1)S(1)}, bf16[256,128]{1,0:T(8,128)(2,1)}, u32[]{:S(2)}) copy-start(bf16[256,128]{1,0:T(8,128)(2,1)} %param.7) | copy-start | bytes 196612
  4.9 57.9 %all-to-all-start = ((bf16[8,512,128]{2,1,0:T(8,128)(2,1)}), bf16[8,512,128]{2,1,0:T(8,128)(2,1)S(1)}, u32[]{:S(2)}, u32[]{:S(2)}) async-start(bf16[8,512,128]{2,1,0:T(8,128)(2,1)} %bitcast), calls=%async_computation | async-start | bytes 2097152 | tf_op jit(solution)/shard_map/all_to_all | solution.py:15
  64.1 12.0 %all-to-all-start.1 = ((bf16[4,128,128]{2,1,0:T(8,128)(2,1)}), bf16[4,128,128]{2,1,0:T(8,128)(2,1)S(1)}, u32[]{:S(2)}, u32[]{:S(2)}) async-start(bf16[4,128,128]{2,1,0:T(8,128)(2,1)} %bitcast.3), calls=%async_computation.1 | async-start | bytes 262144 | tf_op jit(solution)/shard_map/all_to_all | solution.py:15
  76.7 33.6 %all-to-all-start.2 = ((bf16[4,128,128]{2,1,0:T(8,128)(2,1)}), bf16[4,128,128]{2,1,0:T(8,128)(2,1)S(1)}, u32[]{:S(2)}, u32[]{:S(2)}) async-start(bf16[4,128,128]{2,1,0:T(8,128)(2,1)} %broadcast_in_dim.129), calls=%async_computation.2 | async-start | bytes 262144 | tf_op jit(solution)/shard_map/all_to_all | solution.py:15
  88.0 10.7 %collective-permute-start.2 = (bf16[4,8,1024]{2,1,0:T(8,128)(2,1)S(1)}, bf16[4,8,1024]{2,1,0:T(8,128)(2,1)S(1)}, u32[]{:S(2)}, u32[]{:S(2)}) collective-permute-start(bf16[4,8,1024]{2,1,0:T(8,128)(2,1)S(1)} %get-tuple-element.31), channel_id=1, source_target_pairs={{0,256},{256,512},{512,768},{768,0},{1,257},{257,513},{513,769},{7... | collective-permute-start | bytes 196616 | tf_op jit(solution)/shard_map/ppermute | solution.py:70
  89.9 8.7 %collective-permute-start.1 = (bf16[4,8,1024]{2,1,0:T(8,128)(2,1)S(1)}, bf16[4,8,1024]{2,1,0:T(8,128)(2,1)S(1)}, u32[]{:S(2)}, u32[]{:S(2)}) collective-permute-start(bf16[4,8,1024]{2,1,0:T(8,128)(2,1)S(1)} %get-tuple-element.32), channel_id=1, source_target_pairs={{0,512},{256,768},{512,0},{768,256},{1,513},{257,769},{513,1},{769... | collective-permute-start | bytes 196616 | tf_op jit(solution)/shard_map/ppermute | solution.py:70
  93.6 5.0 %collective-permute-start = (bf16[4,8,1024]{2,1,0:T(8,128)(2,1)S(1)}, bf16[4,8,1024]{2,1,0:T(8,128)(2,1)S(1)}, u32[]{:S(2)}, u32[]{:S(2)}) collective-permute-start(bf16[4,8,1024]{2,1,0:T(8,128)(2,1)S(1)} %get-tuple-element.33), channel_id=1, source_target_pairs={{0,768},{256,0},{512,256},{768,512},{1,769},{257,1},{513,257},{769... | collective-permute-start | bytes 196616 | tf_op jit(solution)/shard_map/ppermute | solution.py:70
  129.3 25.0 %all-to-all-start.4 = ((bf16[8,128,128]{2,1,0:T(8,128)(2,1)}), bf16[8,128,128]{2,1,0:T(8,128)(2,1)S(1)}, u32[]{:S(2)}, u32[]{:S(2)}) async-start(bf16[8,128,128]{2,1,0:T(8,128)(2,1)} %broadcast_in_dim.131), calls=%async_computation.4 | async-start | bytes 524288 | tf_op jit(solution)/shard_map/all_to_all | solution.py:15
  154.8 19.3 %copy-start.2 = (f32[1,4,1,128]{3,2,1,0:T(1,128)S(1)}, f32[1,4,1,128]{3,2,1,0:T(1,128)}, u32[]{:S(2)}) copy-start(f32[1,4,1,128]{3,2,1,0:T(1,128)} %param.9) | copy-start | bytes 6148

commit v11 on v7

--- a/solution.py
+++ b/solution.py
@@ -47,19 +47,24 @@
     root_rows = mine * (BLOCK // width)
 
     partial = sum_tokens(activations, cotangents).astype(bf16).reshape(blocks, BLOCK, width)
-    roots = left_roots[0].astype(bf16).reshape(blocks, root_rows, width)
-    got = swap(jnp.concatenate([partial, roots], axis=1), "y")
-    roots = got[:, BLOCK:].reshape(ny * mine, BLOCK)
+    partial, roots = lax.optimization_barrier((partial, left_roots[0].astype(bf16)))
+    roots = lax.all_gather(roots, "far")
+    got, roots = lax.optimization_barrier((swap(partial, "y"), roots))
     kept = sum_tokens(lax.dynamic_slice_in_dim(activations, y * BLOCK, BLOCK, 1), cotangents)
-    others = jnp.where((jnp.arange(ny) == y)[:, None, None], 0.0, got[:, :BLOCK].astype(f32))
+    others = jnp.where((jnp.arange(ny) == y)[:, None, None], 0.0, got.astype(f32))
     column_part = kept + jnp.sum(others, axis=0)
 
-    pieces = column_part.astype(bf16).reshape(nnear, BLOCK // nnear, width)
-    pieces, roots = lax.optimization_barrier((pieces, roots))
-    roots = lax.all_gather(roots, "far", axis=0, tiled=True)
-    got, roots = lax.optimization_barrier((swap(pieces, "near"), roots))
+    got = swap(column_part.astype(bf16).reshape(nnear, BLOCK // nnear, width), "near")
     part = jnp.sum(got.astype(f32), axis=0).astype(bf16)
-    got = everyone(part, "far")
+    part, roots = lax.optimization_barrier((part, roots))
+    held = [lax.dynamic_index_in_dim(roots, y, 1, keepdims=False)]
+    for step in range(1, ny):
+        turn = [(i, (i - step) % ny) for i in range(ny)]
+        block = lax.dynamic_index_in_dim(roots, (y - step) % ny, 1, keepdims=False)
+        held.append(lax.ppermute(block, "y", turn))
+    roots = lax.dynamic_slice_in_dim(jnp.stack(held + held), (ny - y) % ny, ny, 0)
+    roots = roots.reshape(ny * nfar * mine, BLOCK)
+    got, roots = lax.optimization_barrier((everyone(part, "far"), roots))
     own = jnp.sum(got.astype(f32), axis=0).astype(bf16)
     gradient = everyone(own, "near").reshape(BLOCK, width)
 
@@ -68,13 +73,13 @@
     )
     wide = gradient.astype(f32)
     grad_sq = jnp.sum(wide * wide, axis=0)
-    block_sq = lax.psum(grad_sq, "tensor")
+    block_sq = jnp.sum(lax.all_gather(grad_sq, "tensor"), axis=0)
 
     right = lax.dynamic_index_in_dim(right_roots[0], y, 0, keepdims=False)
     mixed = jnp.dot(roots, gradient, preferred_element_type=f32)
     direction = jnp.dot(mixed, right, precision=highest).astype(bf16)
-    direction = everyone(direction, "near").reshape(nnear, nfar, ny, mine, width)
-    direction = direction.transpose(2, 1, 0, 3, 4).reshape(BLOCK, width)
+    direction = everyone(direction, "near").reshape(nnear, ny, nfar, mine, width)
+    direction = direction.transpose(1, 2, 0, 3, 4).reshape(BLOCK, width)
     wide = direction.astype(f32)
     dir_sq = jnp.sum(wide * wide, axis=0)
 

time: 189 us -> 183 us (0.968)
  the two profiles are of different devices: /device:TPU:1 before, /device:TPU:32 now
where the time goes in v11:
time: 183 us; the launch traced here: 182 us
  blocking collectives  98.1 us (54%)
  starting transfers between devices  35.9 us (20%)
  waiting for transfers between devices  32.4 us (18%)
  other arithmetic  6.03 us (3%)
  matrix products  5.29 us (3%)
  local copies, waits for them, and re-layouts  2.6 us (1%)
    all_gather x1, blocking collectives, shards(): roots = lax.all_gather(roots, 'far')  50.6 us
    all_to_all x2, blocking collectives, swap(): return lax.all_to_all(pieces, axis, 0, 0, tiled=True)  36.7 us
    all_to_all x4, waiting for transfers between devices, swap(): return lax.all_to_all(pieces, axis, 0, 0, tiled=True)  29.6 us
    all_to_all x4, starting transfers between devices, swap(): return lax.all_to_all(pieces, axis, 0, 0, tiled=True)  24.9 us
    ppermute x3, starting transfers between devices, shards(): held.append(lax.ppermute(block, 'y', turn))  10.9 us
    all_gather x1, blocking collectives, shards(): block_sq = jnp.sum(lax.all_gather(grad_sq, 'tensor'), axis=0)  10.7 us
  transfers between devices with their start and end apart: 7, of which 4 were waited for; matrix products, arithmetic and copies ran while one was open for 1% of the time, Pallas kernels for 0%

profile of v11, /device:TPU:32, one launch (start us, length us, event | category | flops | bytes accessed | tf_op | source)
XLA Modules:
  0.0 181.8 jit_solution(855533485696381724)
XLA Ops:
  0.6 0.0 copy-start
  0.6 1.1 convert_bitcast_fusion
  1.7 0.6 copy-done
  2.3 2.6 %convolution_convert_fusion = bf16[4096,128]{1,0:T(8,128)(2,1)} fusion(bf16[256,4096]{1,0:T(8,128)(2,1)S(1)} %copy-done, bf16[256,128]{1,0:T(8,128)(2,1)} %param.7), kind=kOutput, calls=%fused_computation | convolution fusion | flops 268959744 | bytes 3211264 | tf_op jit(solution)/shard_map/dot_general | solution.py:32
  4.9 0.0 copy-start.1
  4.9 4.6 %all-to-all-start = ((bf16[4,1024,128]{2,1,0:T(8,128)(2,1)}), bf16[4,1024,128]{2,1,0:T(8,128)(2,1)S(1)}, u32[]{:S(2)}, u32[]{:S(2)}) async-start(bf16[4,1024,128]{2,1,0:T(8,128)(2,1)} %bitcast), calls=%async_computation | async-start | bytes 2097152 | tf_op jit(solution)/shard_map/all_to_all | solution.py:15
  9.5 50.6 %all-gather = bf16[16,8,1024]{2,1,0:T(8,128)(2,1)S(1)} all-gather(bf16[4,8,1024]{2,1,0:T(8,128)(2,1)S(1)} %convert_bitcast_fusion), channel_id=2, replica_groups=mesh['y'=4,'far'=4,'near'=8,'tensor'=8] {'far'}, dimensions={0}, use_global_device_ids=true | all-gather | bytes 327680 | tf_op jit(solution)/shard_map/all_gather | solution.py:51
  60.1 0.0 all-to-all-done
  60.1 0.3 select_reduce_fusion
  60.4 0.0 copy-done.1
  60.4 1.1 fusion
  61.5 3.7 %all-to-all-start.1 = ((bf16[8,128,128]{2,1,0:T(8,128)(2,1)}), bf16[8,128,128]{2,1,0:T(8,128)(2,1)S(1)}, u32[]{:S(2)}, u32[]{:S(2)}) async-start(bf16[8,128,128]{2,1,0:T(8,128)(2,1)} %bitcast.3), calls=%async_computation.1 | async-start | bytes 524288 | tf_op jit(solution)/shard_map/all_to_all | solution.py:15
  65.1 15.8 %all-to-all-done.1 = bf16[8,128,128]{2,1,0:T(8,128)(2,1)S(1)} async-done(((bf16[8,128,128]{2,1,0:T(8,128)(2,1)}), bf16[8,128,128]{2,1,0:T(8,128)(2,1)S(1)}, u32[]{:S(2)}, u32[]{:S(2)}) %all-to-all-start.1) | async-done | bytes 262176 | tf_op jit(solution)/shard_map/all_to_all | solution.py:15
  80.9 0.7 broadcast_in_dim.129
  81.6 11.4 %all-to-all-start.2 = ((bf16[4,128,128]{2,1,0:T(8,128)(2,1)}), bf16[4,128,128]{2,1,0:T(8,128)(2,1)S(1)}, u32[]{:S(2)}, u32[]{:S(2)}) async-start(bf16[4,128,128]{2,1,0:T(8,128)(2,1)} %broadcast_in_dim.129), calls=%async_computation.2 | async-start | bytes 262144 | tf_op jit(solution)/shard_map/all_to_all | solution.py:15
  93.1 3.0 %collective-permute-start.2 = (bf16[4,8,1024]{2,1,0:T(8,128)(2,1)S(1)}, bf16[4,8,1024]{2,1,0:T(8,128)(2,1)S(1)}, u32[]{:S(2)}, u32[]{:S(2)}) collective-permute-start(bf16[4,8,1024]{2,1,0:T(8,128)(2,1)S(1)} %get-tuple-element.31), channel_id=1, source_target_pairs={{0,256},{256,512},{512,768},{768,0},{1,257},{257,513},{513,769},{7... | collective-permute-start | bytes 196616 | tf_op jit(solution)/shard_map/ppermute | solution.py:64
  96.0 4.6 %collective-permute-start.1 = (bf16[4,8,1024]{2,1,0:T(8,128)(2,1)S(1)}, bf16[4,8,1024]{2,1,0:T(8,128)(2,1)S(1)}, u32[]{:S(2)}, u32[]{:S(2)}) collective-permute-start(bf16[4,8,1024]{2,1,0:T(8,128)(2,1)S(1)} %get-tuple-element.32), channel_id=1, source_target_pairs={{0,512},{256,768},{512,0},{768,256},{1,513},{257,769},{513,1},{769... | collective-permute-start | bytes 196616 | tf_op jit(solution)/shard_map/ppermute | solution.py:64
  100.6 3.4 %collective-permute-start = (bf16[4,8,1024]{2,1,0:T(8,128)(2,1)S(1)}, bf16[4,8,1024]{2,1,0:T(8,128)(2,1)S(1)}, u32[]{:S(2)}, u32[]{:S(2)}) collective-permute-start(bf16[4,8,1024]{2,1,0:T(8,128)(2,1)S(1)} %get-tuple-element.33), channel_id=1, source_target_pairs={{0,768},{256,0},{512,256},{768,512},{1,769},{257,1},{513,257},{769... | collective-permute-start | bytes 196616 | tf_op jit(solution)/shard_map/ppermute | solution.py:64
  104.0 2.8 %collective-permute-done = bf16[4,8,1024]{2,1,0:T(8,128)(2,1)S(1)} collective-permute-done((bf16[4,8,1024]{2,1,0:T(8,128)(2,1)S(1)}, bf16[4,8,1024]{2,1,0:T(8,128)(2,1)S(1)}, u32[]{:S(2)}, u32[]{:S(2)}) %collective-permute-start) | collective-permute-done | bytes 65568 | tf_op jit(solution)/shard_map/ppermute | solution.py:64
  106.8 0.0 collective-permute-done.1
  106.8 0.0 collective-permute-done.2
  106.9 12.1 %all-to-all-done.2 = bf16[4,128,128]{2,1,0:T(8,128)(2,1)S(1)} async-done(((bf16[4,128,128]{2,1,0:T(8,128)(2,1)}), bf16[4,128,128]{2,1,0:T(8,128)(2,1)S(1)}, u32[]{:S(2)}, u32[]{:S(2)}) %all-to-all-start.2) | async-done | bytes 131104 | tf_op jit(solution)/shard_map/all_to_all | solution.py:15
  119.1 19.3 %all_to_all.30 = bf16[8,128,128]{2,1,0:T(8,128)(2,1)S(1)} all-to-all(bf16[8,128,128]{2,1,0:T(8,128)(2,1)S(1)} %broadcast_in_dim.130), channel_id=1, replica_groups=mesh['y'=4,'far'=4,'near'=8,'tensor'=8] {'near'}, dimensions={0} | all-to-all | bytes 524288 | tf_op jit(solution)/shard_map/all_to_all | solution.py:15
  138.4 0.2 fusion.16
  138.6 1.0 convolution_convert_fusion.2
  139.7 0.7 broadcast_in_dim.131
  140.4 5.3 %all-to-all-start.4 = ((bf16[8,128,128]{2,1,0:T(8,128)(2,1)}), bf16[8,128,128]{2,1,0:T(8,128)(2,1)S(1)}, u32[]{:S(2)}, u32[]{:S(2)}) async-start(bf16[8,128,128]{2,1,0:T(8,128)(2,1)} %broadcast_in_dim.131), calls=%async_computation.4 | async-start | bytes 524288 | tf_op jit(solution)/shard_map/all_to_all | solution.py:15
  145.7 0.2 convolution_convert_fusion.1
  145.9 0.1 reshape.134
  146.0 0.1 copy.19
  146.1 0.2 fusion.17
  146.4 0.2 multiply_reduce_fusion.1
  146.5 10.7 %all-gather.2 = f32[8,1,128]{2,1,0:T(1,128)S(1)} all-gather(f32[1,1,128]{2,1,0:T(1,128)S(1)} %bitcast.73), channel_id=3, replica_groups=mesh['y'=4,'far'=4,'near'=8,'tensor'=8] {'tensor'}, dimensions={0}, use_global_device_ids=true | all-gather | bytes 4608 | tf_op jit(solution)/shard_map/all_gather | solution.py:76
  157.3 1.8 all-to-all-done.4
  159.1 0.2 multiply_reduce_fusion
  159.2 0.1 copy.18
  159.3 0.1 select_select_fusion
  159.4 0.1 broadcast_in_dim.133
  159.6 0.0 copy-start.2
  159.6 0.1 pad_maximum_fusion
  159.7 17.4 %all_to_all.31 = bf16[4,1104,128]{2,1,0:T(8,128)(2,1)S(1)} all-to-all(bf16[4,1104,128]{2,1,0:T(8,128)(2,1)S(1)} %pad_maximum_fusion), channel_id=1, replica_groups=mesh['y'=4,'far'=4,'near'=8,'tensor'=8] {'y'}, dimensions={0} | all-to-all | bytes 2260992 | tf_op jit(solution)/shard_map/all_to_all | solution.py:15
  177.0 0.6 slice_reduce_fusion
  178.4 0.0 copy-done.2
  178.4 0.6 multiply_add_fusion.1
  179.0 1.6 multiply_add_fusion
  180.6 1.3 multiply_convert_fusion
  (29 shorter events, 0.4 us)
Async XLA Ops:
  0.6 1.7 copy-start
  4.9 55.5 %copy-start.1 = (bf16[256,128]{1,0:T(8,128)(2,1)S(1)}, bf16[256,128]{1,0:T(8,128)(2,1)}, u32[]{:S(2)}) copy-start(bf16[256,128]{1,0:T(8,128)(2,1)} %param.7) | copy-start | bytes 196612
  4.9 55.2 %all-to-all-start = ((bf16[4,1024,128]{2,1,0:T(8,128)(2,1)}), bf16[4,1024,128]{2,1,0:T(8,128)(2,1)S(1)}, u32[]{:S(2)}, u32[]{:S(2)}) async-start(bf16[4,1024,128]{2,1,0:T(8,128)(2,1)} %bitcast), calls=%async_computation | async-start | bytes 2097152 | tf_op jit(solution)/shard_map/all_to_all | solution.py:15
  61.5 19.4 %all-to-all-start.1 = ((bf16[8,128,128]{2,1,0:T(8,128)(2,1)}), bf16[8,128,128]{2,1,0:T(8,128)(2,1)S(1)}, u32[]{:S(2)}, u32[]{:S(2)}) async-start(bf16[8,128,128]{2,1,0:T(8,128)(2,1)} %bitcast.3), calls=%async_computation.1 | async-start | bytes 524288 | tf_op jit(solution)/shard_map/all_to_all | solution.py:15
  81.6 37.4 %all-to-all-start.2 = ((bf16[4,128,128]{2,1,0:T(8,128)(2,1)}), bf16[4,128,128]{2,1,0:T(8,128)(2,1)S(1)}, u32[]{:S(2)}, u32[]{:S(2)}) async-start(bf16[4,128,128]{2,1,0:T(8,128)(2,1)} %broadcast_in_dim.129), calls=%async_computation.2 | async-start | bytes 262144 | tf_op jit(solution)/shard_map/all_to_all | solution.py:15
  93.1 13.8 %collective-permute-start.2 = (bf16[4,8,1024]{2,1,0:T(8,128)(2,1)S(1)}, bf16[4,8,1024]{2,1,0:T(8,128)(2,1)S(1)}, u32[]{:S(2)}, u32[]{:S(2)}) collective-permute-start(bf16[4,8,1024]{2,1,0:T(8,128)(2,1)S(1)} %get-tuple-element.31), channel_id=1, source_target_pairs={{0,256},{256,512},{512,768},{768,0},{1,257},{257,513},{513,769},{7... | collective-permute-start | bytes 196616 | tf_op jit(solution)/shard_map/ppermute | solution.py:64
  96.0 10.8 %collective-permute-start.1 = (bf16[4,8,1024]{2,1,0:T(8,128)(2,1)S(1)}, bf16[4,8,1024]{2,1,0:T(8,128)(2,1)S(1)}, u32[]{:S(2)}, u32[]{:S(2)}) collective-permute-start(bf16[4,8,1024]{2,1,0:T(8,128)(2,1)S(1)} %get-tuple-element.32), channel_id=1, source_target_pairs={{0,512},{256,768},{512,0},{768,256},{1,513},{257,769},{513,1},{769... | collective-permute-start | bytes 196616 | tf_op jit(solution)/shard_map/ppermute | solution.py:64
  100.6 6.2 %collective-permute-start = (bf16[4,8,1024]{2,1,0:T(8,128)(2,1)S(1)}, bf16[4,8,1024]{2,1,0:T(8,128)(2,1)S(1)}, u32[]{:S(2)}, u32[]{:S(2)}) collective-permute-start(bf16[4,8,1024]{2,1,0:T(8,128)(2,1)S(1)} %get-tuple-element.33), channel_id=1, source_target_pairs={{0,768},{256,0},{512,256},{768,512},{1,769},{257,1},{513,257},{769... | collective-permute-start | bytes 196616 | tf_op jit(solution)/shard_map/ppermute | solution.py:64
  140.4 18.6 %all-to-all-start.4 = ((bf16[8,128,128]{2,1,0:T(8,128)(2,1)}), bf16[8,128,128]{2,1,0:T(8,128)(2,1)S(1)}, u32[]{:S(2)}, u32[]{:S(2)}) async-start(bf16[8,128,128]{2,1,0:T(8,128)(2,1)} %broadcast_in_dim.131), calls=%async_computation.4 | async-start | bytes 524288 | tf_op jit(solution)/shard_map/all_to_all | solution.py:15
  159.6 18.8 %copy-start.2 = (f32[1,4,1,128]{3,2,1,0:T(1,128)S(1)}, f32[1,4,1,128]{3,2,1,0:T(1,128)}, u32[]{:S(2)}) copy-start(f32[1,4,1,128]{3,2,1,0:T(1,128)} %param.9) | copy-start | bytes 6148

commit v12 on v10

--- a/solution.py
+++ b/solution.py
@@ -1,6 +1,8 @@
 import jax
 import jax.numpy as jnp
 from jax import lax
+from jax.experimental import pallas as pl
+from jax.experimental.pallas import tpu as pltpu
 from jax.sharding import Mesh, PartitionSpec as P
 
 BLOCK = 1024
@@ -30,6 +32,51 @@
 
 def sum_tokens(rows, columns):
     return lax.dot_general(rows, columns, (((0,), (0,)), ((), ())), preferred_element_type=f32)
+
+
+def finish_kernel(size, got, extras, left_stats, right_stats, update, left_new, right_new):
+    width = got.shape[2]
+    mine = left_stats.shape[1]
+    extra = got[0, -16:, :].astype(f32)
+    grad_sq = jnp.sum(extra[1:4], keepdims=True)
+    dir_sq = jnp.sum(extra[4:7], keepdims=True)
+    layer_sq = jnp.sum(extras[...].astype(f32)[:, 7:10], axis=(0, 1), keepdims=True)[0]
+    layer_sq = jnp.sum(layer_sq, keepdims=True)
+    factor = jnp.sqrt(grad_sq / dir_sq) / jnp.sqrt(layer_sq / size)
+    update[0] = (got[0, :BLOCK, :].astype(f32) * factor).astype(bf16)
+    outer = got[0, BLOCK:-16, :].astype(f32) * ((1.0 - stat_decay) / width)
+    for piece in range(BLOCK // width):
+        columns = pl.ds(piece * width, width)
+        left_new[0, :, columns] = (
+            stat_decay * left_stats[0, :, columns] + outer[piece * mine : (piece + 1) * mine]
+        )
+    right_new[0] = stat_decay * right_stats[0] + ((1.0 - stat_decay) / BLOCK) * extra[:1]
+
+
+def finish(got, left_stats, right_stats, size):
+    blocks, rows, width = got.shape
+
+    def whole(shape):
+        return pl.BlockSpec((1, *shape[1:]), lambda block: (block, 0, 0))
+
+    shapes = (
+        jax.ShapeDtypeStruct((blocks, BLOCK, width), bf16),
+        jax.ShapeDtypeStruct(left_stats.shape, f32),
+        jax.ShapeDtypeStruct(right_stats.shape, f32),
+    )
+    return pl.pallas_call(
+        lambda *refs: finish_kernel(float(size), *refs),
+        grid=(blocks,),
+        in_specs=[
+            whole(got.shape),
+            pl.BlockSpec((blocks, 16, width), lambda block: (0, rows // 16 - 1, 0)),
+            whole(left_stats.shape),
+            whole(right_stats.shape),
+        ],
+        out_specs=[whole(shape.shape) for shape in shapes],
+        out_shape=shapes,
+        name="finish",
+    )(got, got, left_stats, right_stats)
 
 
 def shards(activations, cotangents, left_stats, right_stats, left_roots, right_roots):
@@ -93,7 +140,8 @@
     outer = lax.dot_general(
         rows.reshape(ny * mine, width), gradient, (((1,), (1,)), ((), ())), preferred_element_type=f32
     )
-    outer = outer.astype(bf16).reshape(ny, root_rows, width)
+    outer = outer.astype(bf16).reshape(ny, mine, BLOCK // width, width)
+    outer = outer.transpose(0, 2, 1, 3).reshape(ny, root_rows, width)
     inner = lax.dynamic_index_in_dim(inner.reshape(ny, nz, width), z, 1, keepdims=True).astype(bf16)
     line = jnp.arange(16)[:, None]
     extra = jnp.broadcast_to(inner, (ny, 16, width))
@@ -105,18 +153,10 @@
         ),
         "y",
     )
-    extra = got[:, BLOCK + root_rows :].astype(f32)
-    grad_sq, dir_sq, block_sq = (
-        jnp.sum(extra[:, 1 + 3 * n : 4 + 3 * n], axis=(1, 2), keepdims=True) for n in range(3)
+    update, left_new, right_new = finish(
+        got, left_stats[0], right_stats[0], features * width * tensors
     )
-    layer_sq = jnp.sum(block_sq, axis=0, keepdims=True)
-    factor = jnp.sqrt(grad_sq / dir_sq) / jnp.sqrt(layer_sq / (features * width * tensors))
-    update = (got[:, :BLOCK].astype(f32) * factor).astype(bf16)
-    update = update.reshape(blocks * BLOCK, width)
-    outer = got[:, BLOCK : BLOCK + root_rows].astype(f32).reshape(blocks, mine, BLOCK)
-    left_new = stat_decay * left_stats + ((1.0 - stat_decay) / width) * outer[None]
-    right_new = stat_decay * right_stats + ((1.0 - stat_decay) / BLOCK) * extra[None, :, :1]
-    return (update, left_new, right_new)
+    return (update.reshape(blocks * BLOCK, width), left_new[None], right_new[None])
 
 
 def solution(mesh):

time: 180 us -> 179 us (level)
  other arithmetic: 6 us -> 1.96 us
  Pallas kernels: 0 us -> 3.8 us
    pallas_call x0 -> x1, Pallas kernels: none -> 3.8 us  [finish(): pl.pallas_call(lambda *refs: finish_kernel(float(size), *refs), grid=(blo...]
    add x2 -> x0, other arithmetic: 2.16 us -> none  [the longest x1 1.58 us: shards(): stat_decay * left_stats + (1.0 - stat_decay) / width * outer[None]]
where the time goes in v12:
time: 179 us; the launch traced here: 176 us
  blocking collectives  107 us (60%)
  starting transfers between devices  33.2 us (19%)
  waiting for transfers between devices  22 us (12%)
  matrix products  5.16 us (3%)
  Pallas kernels  3.8 us (2%)
  local copies, waits for them, and re-layouts  2.51 us (1%)
  other arithmetic  1.96 us (1%)
    all_gather x1, blocking collectives, shards(): roots = lax.all_gather(roots, 'far')  51.4 us
    all_to_all x2, blocking collectives, swap(): return lax.all_to_all(pieces, axis, 0, 0, tiled=True)  34.7 us
    all_to_all x4, starting transfers between devices, swap(): return lax.all_to_all(pieces, axis, 0, 0, tiled=True)  24.5 us
    all_gather x1, blocking collectives, shards(): block_sq = jnp.sum(lax.all_gather(grad_sq, 'tensor'), axis=0)  20.7 us
    all_to_all x4, waiting for transfers between devices, swap(): return lax.all_to_all(pieces, axis, 0, 0, tiled=True)  20.1 us
    ppermute x3, starting transfers between devices, shards(): held.append(lax.ppermute(block, 'y', turn))  8.68 us
    pallas_call x1, Pallas kernels, finish(): pl.pallas_call(lambda *refs: finish_kernel(float(size), *refs), grid=(blo...  3.8 us
  transfers between devices with their start and end apart: 7, of which 3 were waited for; matrix products, arithmetic and copies ran while one was open for 1% of the time, Pallas kernels for 0%

profile of v12, /device:TPU:1, one launch (start us, length us, event | category | flops | bytes accessed | tf_op | source)
XLA Modules:
  0.0 176.5 jit_solution(13438984868826720162)
XLA Ops:
  0.6 0.0 copy-start
  0.6 1.1 convert_bitcast_fusion
  1.7 0.6 copy-done
  2.3 2.6 %convolution_convert_fusion = bf16[4096,128]{1,0:T(8,128)(2,1)} fusion(bf16[256,4096]{1,0:T(8,128)(2,1)S(1)} %copy-done, bf16[256,128]{1,0:T(8,128)(2,1)} %param.7), kind=kOutput, calls=%fused_computation | convolution fusion | flops 268959744 | bytes 3211264 | tf_op jit(solution)/shard_map/dot_general | solution.py:34
  4.9 0.0 copy-start.1
  4.9 6.5 %all-to-all-start = ((bf16[8,512,128]{2,1,0:T(8,128)(2,1)}), bf16[8,512,128]{2,1,0:T(8,128)(2,1)S(1)}, u32[]{:S(2)}, u32[]{:S(2)}) async-start(bf16[8,512,128]{2,1,0:T(8,128)(2,1)} %bitcast), calls=%async_computation | async-start | bytes 2097152 | tf_op jit(solution)/shard_map/all_to_all | solution.py:17
  11.4 51.4 %all-gather = bf16[16,8,1024]{2,1,0:T(8,128)(2,1)S(1)} all-gather(bf16[4,8,1024]{2,1,0:T(8,128)(2,1)S(1)} %convert_bitcast_fusion), channel_id=2, replica_groups=mesh['y'=4,'far'=4,'mid'=4,'pair'=2,'tensor'=8] {'far'}, dimensions={0}, use_global_device_ids=true | all-gather | bytes 327680 | tf_op jit(solution)/shard_map/all_gather | solution.py:103
  62.8 0.0 all-to-all-done
  62.8 0.3 select_reduce_fusion
  63.1 0.0 copy-done.1
  63.1 0.9 fusion
  64.1 3.3 %all-to-all-start.1 = ((bf16[4,128,128]{2,1,0:T(8,128)(2,1)}), bf16[4,128,128]{2,1,0:T(8,128)(2,1)S(1)}, u32[]{:S(2)}, u32[]{:S(2)}) async-start(bf16[4,128,128]{2,1,0:T(8,128)(2,1)} %bitcast.3), calls=%async_computation.1 | async-start | bytes 262144 | tf_op jit(solution)/shard_map/all_to_all | solution.py:17
  67.5 8.6 %all-to-all-done.1 = bf16[4,128,128]{2,1,0:T(8,128)(2,1)S(1)} async-done(((bf16[4,128,128]{2,1,0:T(8,128)(2,1)}), bf16[4,128,128]{2,1,0:T(8,128)(2,1)S(1)}, u32[]{:S(2)}, u32[]{:S(2)}) %all-to-all-start.1) | async-done | bytes 131104 | tf_op jit(solution)/shard_map/all_to_all | solution.py:17
  76.1 0.7 broadcast_in_dim.130
  76.7 11.3 %all-to-all-start.2 = ((bf16[4,128,128]{2,1,0:T(8,128)(2,1)}), bf16[4,128,128]{2,1,0:T(8,128)(2,1)S(1)}, u32[]{:S(2)}, u32[]{:S(2)}) async-start(bf16[4,128,128]{2,1,0:T(8,128)(2,1)} %broadcast_in_dim.130), calls=%async_computation.2 | async-start | bytes 262144 | tf_op jit(solution)/shard_map/all_to_all | solution.py:17
  88.0 1.9 %collective-permute-start.2 = (bf16[4,8,1024]{2,1,0:T(8,128)(2,1)S(1)}, bf16[4,8,1024]{2,1,0:T(8,128)(2,1)S(1)}, u32[]{:S(2)}, u32[]{:S(2)}) collective-permute-start(bf16[4,8,1024]{2,1,0:T(8,128)(2,1)S(1)} %get-tuple-element.37), channel_id=1, source_target_pairs={{0,256},{256,512},{512,768},{768,0},{1,257},{257,513},{513,769},{7... | collective-permute-start | bytes 196616 | tf_op jit(solution)/shard_map/ppermute | solution.py:117
  89.9 3.7 %collective-permute-start.1 = (bf16[4,8,1024]{2,1,0:T(8,128)(2,1)S(1)}, bf16[4,8,1024]{2,1,0:T(8,128)(2,1)S(1)}, u32[]{:S(2)}, u32[]{:S(2)}) collective-permute-start(bf16[4,8,1024]{2,1,0:T(8,128)(2,1)S(1)} %get-tuple-element.38), channel_id=1, source_target_pairs={{0,512},{256,768},{512,0},{768,256},{1,513},{257,769},{513,1},{769... | collective-permute-start | bytes 196616 | tf_op jit(solution)/shard_map/ppermute | solution.py:117
  93.6 3.1 %collective-permute-start = (bf16[4,8,1024]{2,1,0:T(8,128)(2,1)S(1)}, bf16[4,8,1024]{2,1,0:T(8,128)(2,1)S(1)}, u32[]{:S(2)}, u32[]{:S(2)}) collective-permute-start(bf16[4,8,1024]{2,1,0:T(8,128)(2,1)S(1)} %get-tuple-element.39), channel_id=1, source_target_pairs={{0,768},{256,0},{512,256},{768,512},{1,769},{257,1},{513,257},{769... | collective-permute-start | bytes 196616 | tf_op jit(solution)/shard_map/ppermute | solution.py:117
  96.7 1.9 %collective-permute-done = bf16[4,8,1024]{2,1,0:T(8,128)(2,1)S(1)} collective-permute-done((bf16[4,8,1024]{2,1,0:T(8,128)(2,1)S(1)}, bf16[4,8,1024]{2,1,0:T(8,128)(2,1)S(1)}, u32[]{:S(2)}, u32[]{:S(2)}) %collective-permute-start) | collective-permute-done | bytes 65568 | tf_op jit(solution)/shard_map/ppermute | solution.py:117
  98.7 0.0 collective-permute-done.1
  98.7 0.0 collective-permute-done.2
  98.8 11.5 %all-to-all-done.2 = bf16[4,128,128]{2,1,0:T(8,128)(2,1)S(1)} async-done(((bf16[4,128,128]{2,1,0:T(8,128)(2,1)}), bf16[4,128,128]{2,1,0:T(8,128)(2,1)S(1)}, u32[]{:S(2)}, u32[]{:S(2)}) %all-to-all-start.2) | async-done | bytes 131104 | tf_op jit(solution)/shard_map/all_to_all | solution.py:17
  110.4 16.8 %all_to_all.30 = bf16[8,128,128]{2,1,0:T(8,128)(2,1)S(1)} all-to-all(bf16[8,128,128]{2,1,0:T(8,128)(2,1)S(1)} %broadcast_in_dim.131), channel_id=1, replica_groups=mesh['y'=4,'far'=4,'mid'=4,'pair'=2,'tensor'=8] {'pair','mid'}, dimensions={0} | all-to-all | bytes 524288 | tf_op jit(solution)/shard_map/all_to_all | solution.py:17
  127.3 0.2 fusion.17
  127.5 1.0 convolution_convert_fusion.2
  128.5 0.7 broadcast_in_dim.132
  129.3 3.4 %all-to-all-start.4 = ((bf16[8,128,128]{2,1,0:T(8,128)(2,1)}), bf16[8,128,128]{2,1,0:T(8,128)(2,1)S(1)}, u32[]{:S(2)}, u32[]{:S(2)}) async-start(bf16[8,128,128]{2,1,0:T(8,128)(2,1)} %broadcast_in_dim.132), calls=%async_computation.4 | async-start | bytes 524288 | tf_op jit(solution)/shard_map/all_to_all | solution.py:17
  132.8 0.1 copy.17
  132.9 0.2 fusion.18
  133.2 0.2 multiply_reduce_fusion.1
  133.3 20.7 %all-gather.2 = f32[8,1,128]{2,1,0:T(1,128)S(1)} all-gather(f32[1,1,128]{2,1,0:T(1,128)S(1)} %bitcast.81), channel_id=3, replica_groups=mesh['y'=4,'far'=4,'mid'=4,'pair'=2,'tensor'=8] {'tensor'}, dimensions={0}, use_global_device_ids=true | all-gather | bytes 4608 | tf_op jit(solution)/shard_map/all_gather | solution.py:129
  154.0 0.2 fusion.1
  154.2 0.0 all-to-all-done.4
  154.3 0.2 multiply_reduce_fusion
  154.4 0.1 copy.16
  154.5 0.1 select_select_fusion
  154.6 0.1 broadcast_in_dim.134
  154.7 0.1 pad_maximum_fusion
  154.8 17.9 %all_to_all.31.refs_0_.refs_1_ = bf16[4,1104,128]{2,1,0:T(8,128)(2,1)} all-to-all(bf16[4,1104,128]{2,1,0:T(8,128)(2,1)S(1)} %pad_maximum_fusion), channel_id=1, replica_groups=mesh['y'=4,'far'=4,'mid'=4,'pair'=2,'tensor'=8] {'y'}, dimensions={0} | all-to-all | bytes 2260992 | tf_op jit(solution)/shard_map/all_to_all | solution.py:17
  172.7 3.8 %finish.1 = (bf16[4,1024,128]{2,1,0:T(8,128)(2,1)}, f32[4,8,1024]{2,1,0:T(8,128)}, f32[4,1,128]{2,1,0:T(1,128)}) custom-call(bf16[4,1104,128]{2,1,0:T(8,128)(2,1)} %all_to_all.31.refs_0_.refs_1_, bf16[4,1104,128]{2,1,0:T(8,128)(2,1)} %all_to_all.31.refs_0_.refs_1_, f32[4,8,1024]{2,1,0:T(8,128)} %bitcast.80, f32[4,1,128]{2,1,0:T(1,128)} %bitcast.83), custom_call_target="tpu_custom_call" | custom-call | tf_op jit(solution)/shard_map/finish/pallas_call | solution.py:67
  (24 shorter events, 0.3 us)
Async XLA Ops:
  0.6 1.7 copy-start
  4.9 58.2 %copy-start.1 = (bf16[256,128]{1,0:T(8,128)(2,1)S(1)}, bf16[256,128]{1,0:T(8,128)(2,1)}, u32[]{:S(2)}) copy-start(bf16[256,128]{1,0:T(8,128)(2,1)} %param.7) | copy-start | bytes 196612
  4.9 57.9 %all-to-all-start = ((bf16[8,512,128]{2,1,0:T(8,128)(2,1)}), bf16[8,512,128]{2,1,0:T(8,128)(2,1)S(1)}, u32[]{:S(2)}, u32[]{:S(2)}) async-start(bf16[8,512,128]{2,1,0:T(8,128)(2,1)} %bitcast), calls=%async_computation | async-start | bytes 2097152 | tf_op jit(solution)/shard_map/all_to_all | solution.py:17
  64.1 12.0 %all-to-all-start.1 = ((bf16[4,128,128]{2,1,0:T(8,128)(2,1)}), bf16[4,128,128]{2,1,0:T(8,128)(2,1)S(1)}, u32[]{:S(2)}, u32[]{:S(2)}) async-start(bf16[4,128,128]{2,1,0:T(8,128)(2,1)} %bitcast.3), calls=%async_computation.1 | async-start | bytes 262144 | tf_op jit(solution)/shard_map/all_to_all | solution.py:17
  76.7 33.6 %all-to-all-start.2 = ((bf16[4,128,128]{2,1,0:T(8,128)(2,1)}), bf16[4,128,128]{2,1,0:T(8,128)(2,1)S(1)}, u32[]{:S(2)}, u32[]{:S(2)}) async-start(bf16[4,128,128]{2,1,0:T(8,128)(2,1)} %broadcast_in_dim.130), calls=%async_computation.2 | async-start | bytes 262144 | tf_op jit(solution)/shard_map/all_to_all | solution.py:17
  88.0 10.7 %collective-permute-start.2 = (bf16[4,8,1024]{2,1,0:T(8,128)(2,1)S(1)}, bf16[4,8,1024]{2,1,0:T(8,128)(2,1)S(1)}, u32[]{:S(2)}, u32[]{:S(2)}) collective-permute-start(bf16[4,8,1024]{2,1,0:T(8,128)(2,1)S(1)} %get-tuple-element.37), channel_id=1, source_target_pairs={{0,256},{256,512},{512,768},{768,0},{1,257},{257,513},{513,769},{7... | collective-permute-start | bytes 196616 | tf_op jit(solution)/shard_map/ppermute | solution.py:117
  89.9 8.7 %collective-permute-start.1 = (bf16[4,8,1024]{2,1,0:T(8,128)(2,1)S(1)}, bf16[4,8,1024]{2,1,0:T(8,128)(2,1)S(1)}, u32[]{:S(2)}, u32[]{:S(2)}) collective-permute-start(bf16[4,8,1024]{2,1,0:T(8,128)(2,1)S(1)} %get-tuple-element.38), channel_id=1, source_target_pairs={{0,512},{256,768},{512,0},{768,256},{1,513},{257,769},{513,1},{769... | collective-permute-start | bytes 196616 | tf_op jit(solution)/shard_map/ppermute | solution.py:117
  93.6 5.0 %collective-permute-start = (bf16[4,8,1024]{2,1,0:T(8,128)(2,1)S(1)}, bf16[4,8,1024]{2,1,0:T(8,128)(2,1)S(1)}, u32[]{:S(2)}, u32[]{:S(2)}) collective-permute-start(bf16[4,8,1024]{2,1,0:T(8,128)(2,1)S(1)} %get-tuple-element.39), channel_id=1, source_target_pairs={{0,768},{256,0},{512,256},{768,512},{1,769},{257,1},{513,257},{769... | collective-permute-start | bytes 196616 | tf_op jit(solution)/shard_map/ppermute | solution.py:117
  129.3 25.0 %all-to-all-start.4 = ((bf16[8,128,128]{2,1,0:T(8,128)(2,1)}), bf16[8,128,128]{2,1,0:T(8,128)(2,1)S(1)}, u32[]{:S(2)}, u32[]{:S(2)}) async-start(bf16[8,128,128]{2,1,0:T(8,128)(2,1)} %broadcast_in_dim.132), calls=%async_computation.4 | async-start | bytes 524288 | tf_op jit(solution)/shard_map/all_to_all | solution.py:17

commit v13 on v10

--- a/solution.py
+++ b/solution.py
@@ -79,7 +79,6 @@
     )
     wide = gradient.astype(f32)
     grad_sq = jnp.sum(wide * wide, axis=0)
-    block_sq = jnp.sum(lax.all_gather(grad_sq, "tensor"), axis=0)
 
     right = lax.dynamic_index_in_dim(right_roots[0], y, 0, keepdims=False)
     mixed = jnp.dot(roots, gradient, preferred_element_type=f32)
@@ -97,19 +96,19 @@
     inner = lax.dynamic_index_in_dim(inner.reshape(ny, nz, width), z, 1, keepdims=True).astype(bf16)
     line = jnp.arange(16)[:, None]
     extra = jnp.broadcast_to(inner, (ny, 16, width))
-    for place, values in enumerate(thirds(grad_sq) + thirds(dir_sq) + thirds(block_sq), 1):
+    for place, values in enumerate(thirds(grad_sq) + thirds(dir_sq), 1):
         extra = jnp.where(line == place, values, extra)
-    got = swap(
-        jnp.concatenate(
-            [jnp.broadcast_to(direction[None], (ny, BLOCK, width)), outer, extra], axis=1
-        ),
-        "y",
+    sent = jnp.concatenate(
+        [jnp.broadcast_to(direction[None], (ny, BLOCK, width)), outer, extra], axis=1
     )
+    sent, layer_sq = lax.optimization_barrier((sent, grad_sq))
+    layer_sq = lax.all_gather(layer_sq, ("y", "tensor"))
+    got, layer_sq = lax.optimization_barrier((swap(sent, "y"), layer_sq))
     extra = got[:, BLOCK + root_rows :].astype(f32)
-    grad_sq, dir_sq, block_sq = (
-        jnp.sum(extra[:, 1 + 3 * n : 4 + 3 * n], axis=(1, 2), keepdims=True) for n in range(3)
+    grad_sq, dir_sq = (
+        jnp.sum(extra[:, 1 + 3 * n : 4 + 3 * n], axis=(1, 2), keepdims=True) for n in range(2)
     )
-    layer_sq = jnp.sum(block_sq, axis=0, keepdims=True)
+    layer_sq = jnp.sum(layer_sq)
     factor = jnp.sqrt(grad_sq / dir_sq) / jnp.sqrt(layer_sq / (features * width * tensors))
     update = (got[:, :BLOCK].astype(f32) * factor).astype(bf16)
     update = update.reshape(blocks * BLOCK, width)

time: 180 us -> 192 us (1.067); the launches traced: 177 us -> 192 us
  waiting for transfers between devices: 22 us -> 33.1 us
  starting transfers between devices: 33.2 us -> 38.5 us
  blocking collectives: 107 us -> 104 us
    all_to_all x2 -> x1, blocking collectives: 34.6 us -> 16.8 us  [swap(): return lax.all_to_all(pieces, axis, 0, 0, tiled=True)]
    all_gather x1, blocking collectives: 20.7 us -> 36.2 us  [shards(): layer_sq = lax.all_gather(layer_sq, ('y', 'tensor'))]
    all_to_all x4 -> x5, waiting for transfers between devices: 20.1 us -> 31.1 us  [swap(): return lax.all_to_all(pieces, axis, 0, 0, tiled=True)]
    all_to_all x4 -> x5, starting transfers between devices: 24.5 us -> 29.8 us  [swap(): return lax.all_to_all(pieces, axis, 0, 0, tiled=True)]
  transfers between devices with their start and end apart: 7 -> 8, of which waited for: 3 -> 4; matrix products, arithmetic and copies ran while one was open for 1% -> 0% of each run, Pallas kernels for 0% -> 0%
where the time goes in v13:
time: 192 us
  blocking collectives  104 us (54%)
  starting transfers between devices  38.5 us (20%)
  waiting for transfers between devices  33.1 us (17%)
  other arithmetic  6.13 us (3%)
  matrix products  5.16 us (3%)
  local copies, waits for them, and re-layouts  2.6 us (1%)
    all_gather x1, blocking collectives, shards(): roots = lax.all_gather(roots, 'far')  51.4 us
    all_gather x1, blocking collectives, shards(): layer_sq = lax.all_gather(layer_sq, ('y', 'tensor'))  36.2 us
    all_to_all x5, waiting for transfers between devices, swap(): return lax.all_to_all(pieces, axis, 0, 0, tiled=True)  31.1 us
    all_to_all x5, starting transfers between devices, swap(): return lax.all_to_all(pieces, axis, 0, 0, tiled=True)  29.8 us
    all_to_all x1, blocking collectives, swap(): return lax.all_to_all(pieces, axis, 0, 0, tiled=True)  16.8 us
    ppermute x3, starting transfers between devices, shards(): held.append(lax.ppermute(block, 'y', turn))  8.68 us
  transfers between devices with their start and end apart: 8, of which 4 were waited for; matrix products, arithmetic and copies ran while one was open for 0% of the time, Pallas kernels for 0%

profile of v13, /device:TPU:1, one launch (start us, length us, event | category | flops | bytes accessed | tf_op | source)
XLA Modules:
  0.0 191.6 jit_solution(5204894505708515662)
XLA Ops:
  0.6 0.0 copy-start
  0.6 1.1 convert_bitcast_fusion
  1.7 0.6 copy-done
  2.3 2.6 %convolution_convert_fusion = bf16[4096,128]{1,0:T(8,128)(2,1)} fusion(bf16[256,4096]{1,0:T(8,128)(2,1)S(1)} %copy-done, bf16[256,128]{1,0:T(8,128)(2,1)} %param.7), kind=kOutput, calls=%fused_computation | convolution fusion | flops 268959744 | bytes 3211264 | tf_op jit(solution)/shard_map/dot_general | solution.py:32
  4.9 0.0 copy-start.1
  4.9 6.5 %all-to-all-start = ((bf16[8,512,128]{2,1,0:T(8,128)(2,1)}), bf16[8,512,128]{2,1,0:T(8,128)(2,1)S(1)}, u32[]{:S(2)}, u32[]{:S(2)}) async-start(bf16[8,512,128]{2,1,0:T(8,128)(2,1)} %bitcast), calls=%async_computation | async-start | bytes 2097152 | tf_op jit(solution)/shard_map/all_to_all | solution.py:15
  11.4 51.4 %all-gather = bf16[16,8,1024]{2,1,0:T(8,128)(2,1)S(1)} all-gather(bf16[4,8,1024]{2,1,0:T(8,128)(2,1)S(1)} %convert_bitcast_fusion), channel_id=2, replica_groups=mesh['y'=4,'far'=4,'mid'=4,'pair'=2,'tensor'=8] {'far'}, dimensions={0}, use_global_device_ids=true | all-gather | bytes 327680 | tf_op jit(solution)/shard_map/all_gather | solution.py:56
  62.8 0.0 all-to-all-done
  62.8 0.3 select_reduce_fusion
  63.1 0.0 copy-done.1
  63.1 0.9 fusion
  64.1 3.3 %all-to-all-start.1 = ((bf16[4,128,128]{2,1,0:T(8,128)(2,1)}), bf16[4,128,128]{2,1,0:T(8,128)(2,1)S(1)}, u32[]{:S(2)}, u32[]{:S(2)}) async-start(bf16[4,128,128]{2,1,0:T(8,128)(2,1)} %bitcast.3), calls=%async_computation.1 | async-start | bytes 262144 | tf_op jit(solution)/shard_map/all_to_all | solution.py:15
  67.5 8.6 %all-to-all-done.1 = bf16[4,128,128]{2,1,0:T(8,128)(2,1)S(1)} async-done(((bf16[4,128,128]{2,1,0:T(8,128)(2,1)}), bf16[4,128,128]{2,1,0:T(8,128)(2,1)S(1)}, u32[]{:S(2)}, u32[]{:S(2)}) %all-to-all-start.1) | async-done | bytes 131104 | tf_op jit(solution)/shard_map/all_to_all | solution.py:15
  76.1 0.7 broadcast_in_dim.103
  76.7 11.3 %all-to-all-start.2 = ((bf16[4,128,128]{2,1,0:T(8,128)(2,1)}), bf16[4,128,128]{2,1,0:T(8,128)(2,1)S(1)}, u32[]{:S(2)}, u32[]{:S(2)}) async-start(bf16[4,128,128]{2,1,0:T(8,128)(2,1)} %broadcast_in_dim.103), calls=%async_computation.2 | async-start | bytes 262144 | tf_op jit(solution)/shard_map/all_to_all | solution.py:15
  88.0 1.9 %collective-permute-start.2 = (bf16[4,8,1024]{2,1,0:T(8,128)(2,1)S(1)}, bf16[4,8,1024]{2,1,0:T(8,128)(2,1)S(1)}, u32[]{:S(2)}, u32[]{:S(2)}) collective-permute-start(bf16[4,8,1024]{2,1,0:T(8,128)(2,1)S(1)} %get-tuple-element.38), channel_id=1, source_target_pairs={{0,256},{256,512},{512,768},{768,0},{1,257},{257,513},{513,769},{7... | collective-permute-start | bytes 196616 | tf_op jit(solution)/shard_map/ppermute | solution.py:70
  89.9 3.7 %collective-permute-start.1 = (bf16[4,8,1024]{2,1,0:T(8,128)(2,1)S(1)}, bf16[4,8,1024]{2,1,0:T(8,128)(2,1)S(1)}, u32[]{:S(2)}, u32[]{:S(2)}) collective-permute-start(bf16[4,8,1024]{2,1,0:T(8,128)(2,1)S(1)} %get-tuple-element.39), channel_id=1, source_target_pairs={{0,512},{256,768},{512,0},{768,256},{1,513},{257,769},{513,1},{769... | collective-permute-start | bytes 196616 | tf_op jit(solution)/shard_map/ppermute | solution.py:70
  93.6 3.1 %collective-permute-start = (bf16[4,8,1024]{2,1,0:T(8,128)(2,1)S(1)}, bf16[4,8,1024]{2,1,0:T(8,128)(2,1)S(1)}, u32[]{:S(2)}, u32[]{:S(2)}) collective-permute-start(bf16[4,8,1024]{2,1,0:T(8,128)(2,1)S(1)} %get-tuple-element.40), channel_id=1, source_target_pairs={{0,768},{256,0},{512,256},{768,512},{1,769},{257,1},{513,257},{769... | collective-permute-start | bytes 196616 | tf_op jit(solution)/shard_map/ppermute | solution.py:70
  96.7 1.9 %collective-permute-done = bf16[4,8,1024]{2,1,0:T(8,128)(2,1)S(1)} collective-permute-done((bf16[4,8,1024]{2,1,0:T(8,128)(2,1)S(1)}, bf16[4,8,1024]{2,1,0:T(8,128)(2,1)S(1)}, u32[]{:S(2)}, u32[]{:S(2)}) %collective-permute-start) | collective-permute-done | bytes 65568 | tf_op jit(solution)/shard_map/ppermute | solution.py:70
  98.7 0.0 collective-permute-done.1
  98.7 0.0 collective-permute-done.2
  98.8 11.5 %all-to-all-done.2 = bf16[4,128,128]{2,1,0:T(8,128)(2,1)S(1)} async-done(((bf16[4,128,128]{2,1,0:T(8,128)(2,1)}), bf16[4,128,128]{2,1,0:T(8,128)(2,1)S(1)}, u32[]{:S(2)}, u32[]{:S(2)}) %all-to-all-start.2) | async-done | bytes 131104 | tf_op jit(solution)/shard_map/all_to_all | solution.py:15
  110.4 16.8 %all_to_all.30 = bf16[8,128,128]{2,1,0:T(8,128)(2,1)S(1)} all-to-all(bf16[8,128,128]{2,1,0:T(8,128)(2,1)S(1)} %broadcast_in_dim.104), channel_id=1, replica_groups=mesh['y'=4,'far'=4,'mid'=4,'pair'=2,'tensor'=8] {'pair','mid'}, dimensions={0} | all-to-all | bytes 524288 | tf_op jit(solution)/shard_map/all_to_all | solution.py:15
  127.3 0.2 fusion.14
  127.5 1.0 convolution_convert_fusion.2
  128.5 0.7 broadcast_in_dim.105
  129.3 3.4 %all-to-all-start.4 = ((bf16[8,128,128]{2,1,0:T(8,128)(2,1)}), bf16[8,128,128]{2,1,0:T(8,128)(2,1)S(1)}, u32[]{:S(2)}, u32[]{:S(2)}) async-start(bf16[8,128,128]{2,1,0:T(8,128)(2,1)} %broadcast_in_dim.105), calls=%async_computation.4 | async-start | bytes 524288 | tf_op jit(solution)/shard_map/all_to_all | solution.py:15
  132.7 0.2 convolution_convert_fusion.1
  132.9 0.1 reshape.114
  133.0 0.1 copy.19
  133.1 0.2 fusion.15
  133.4 0.2 multiply_reduce_fusion
  133.5 11.0 %all-to-all-done.4 = bf16[8,128,128]{2,1,0:T(8,128)(2,1)S(1)} async-done(((bf16[8,128,128]{2,1,0:T(8,128)(2,1)}), bf16[8,128,128]{2,1,0:T(8,128)(2,1)S(1)}, u32[]{:S(2)}, u32[]{:S(2)}) %all-to-all-start.4) | async-done | bytes 262176 | tf_op jit(solution)/shard_map/all_to_all | solution.py:15
  144.6 0.2 multiply_reduce_fusion.1
  144.7 0.1 copy.18
  144.8 0.1 select_select_fusion
  144.9 0.1 broadcast_in_dim.107
  145.0 1.1 pad_maximum_fusion
  146.1 0.0 copy-start.3
  146.1 0.0 copy-start.2
  146.1 5.3 %all-to-all-start.5 = ((bf16[4,1104,128]{2,1,0:T(8,128)(2,1)}), bf16[4,1104,128]{2,1,0:T(8,128)(2,1)S(1)}, u32[]{:S(2)}, u32[]{:S(2)}) async-start(bf16[4,1104,128]{2,1,0:T(8,128)(2,1)} %pad_maximum_fusion), calls=%async_computation.5 | async-start | bytes 2260992 | tf_op jit(solution)/shard_map/all_to_all | solution.py:15
  151.4 36.2 %all-gather.2 = f32[32,1,128]{2,1,0:T(1,128)S(1)} all-gather(f32[1,1,128]{2,1,0:T(1,128)S(1)} %bitcast.75), channel_id=3, replica_groups=mesh['y'=4,'far'=4,'mid'=4,'pair'=2,'tensor'=8] {'y','tensor'}, dimensions={0}, use_global_device_ids=true | all-gather | bytes 16896 | tf_op jit(solution)/shard_map/all_gather | solution.py:105
  187.5 0.0 all-to-all-done.5
  187.6 0.1 slice_reduce_fusion
  187.7 0.6 reduce_sum.85
  189.0 1.2 multiply_convert_fusion
  190.3 0.0 copy-done.3
  190.3 0.6 multiply_add_fusion.1
  190.9 0.0 copy-done.2
  190.9 0.7 multiply_add_fusion
  (25 shorter events, 0.3 us)
Async XLA Ops:
  0.6 1.7 copy-start
  4.9 58.2 %copy-start.1 = (bf16[256,128]{1,0:T(8,128)(2,1)S(1)}, bf16[256,128]{1,0:T(8,128)(2,1)}, u32[]{:S(2)}) copy-start(bf16[256,128]{1,0:T(8,128)(2,1)} %param.7) | copy-start | bytes 196612
  4.9 57.9 %all-to-all-start = ((bf16[8,512,128]{2,1,0:T(8,128)(2,1)}), bf16[8,512,128]{2,1,0:T(8,128)(2,1)S(1)}, u32[]{:S(2)}, u32[]{:S(2)}) async-start(bf16[8,512,128]{2,1,0:T(8,128)(2,1)} %bitcast), calls=%async_computation | async-start | bytes 2097152 | tf_op jit(solution)/shard_map/all_to_all | solution.py:15
  64.1 12.0 %all-to-all-start.1 = ((bf16[4,128,128]{2,1,0:T(8,128)(2,1)}), bf16[4,128,128]{2,1,0:T(8,128)(2,1)S(1)}, u32[]{:S(2)}, u32[]{:S(2)}) async-start(bf16[4,128,128]{2,1,0:T(8,128)(2,1)} %bitcast.3), calls=%async_computation.1 | async-start | bytes 262144 | tf_op jit(solution)/shard_map/all_to_all | solution.py:15
  76.7 33.6 %all-to-all-start.2 = ((bf16[4,128,128]{2,1,0:T(8,128)(2,1)}), bf16[4,128,128]{2,1,0:T(8,128)(2,1)S(1)}, u32[]{:S(2)}, u32[]{:S(2)}) async-start(bf16[4,128,128]{2,1,0:T(8,128)(2,1)} %broadcast_in_dim.103), calls=%async_computation.2 | async-start | bytes 262144 | tf_op jit(solution)/shard_map/all_to_all | solution.py:15
  88.0 10.7 %collective-permute-start.2 = (bf16[4,8,1024]{2,1,0:T(8,128)(2,1)S(1)}, bf16[4,8,1024]{2,1,0:T(8,128)(2,1)S(1)}, u32[]{:S(2)}, u32[]{:S(2)}) collective-permute-start(bf16[4,8,1024]{2,1,0:T(8,128)(2,1)S(1)} %get-tuple-element.38), channel_id=1, source_target_pairs={{0,256},{256,512},{512,768},{768,0},{1,257},{257,513},{513,769},{7... | collective-permute-start | bytes 196616 | tf_op jit(solution)/shard_map/ppermute | solution.py:70
  89.9 8.7 %collective-permute-start.1 = (bf16[4,8,1024]{2,1,0:T(8,128)(2,1)S(1)}, bf16[4,8,1024]{2,1,0:T(8,128)(2,1)S(1)}, u32[]{:S(2)}, u32[]{:S(2)}) collective-permute-start(bf16[4,8,1024]{2,1,0:T(8,128)(2,1)S(1)} %get-tuple-element.39), channel_id=1, source_target_pairs={{0,512},{256,768},{512,0},{768,256},{1,513},{257,769},{513,1},{769... | collective-permute-start | bytes 196616 | tf_op jit(solution)/shard_map/ppermute | solution.py:70
  93.6 5.0 %collective-permute-start = (bf16[4,8,1024]{2,1,0:T(8,128)(2,1)S(1)}, bf16[4,8,1024]{2,1,0:T(8,128)(2,1)S(1)}, u32[]{:S(2)}, u32[]{:S(2)}) collective-permute-start(bf16[4,8,1024]{2,1,0:T(8,128)(2,1)S(1)} %get-tuple-element.40), channel_id=1, source_target_pairs={{0,768},{256,0},{512,256},{768,512},{1,769},{257,1},{513,257},{769... | collective-permute-start | bytes 196616 | tf_op jit(solution)/shard_map/ppermute | solution.py:70
  129.3 15.3 %all-to-all-start.4 = ((bf16[8,128,128]{2,1,0:T(8,128)(2,1)}), bf16[8,128,128]{2,1,0:T(8,128)(2,1)S(1)}, u32[]{:S(2)}, u32[]{:S(2)}) async-start(bf16[8,128,128]{2,1,0:T(8,128)(2,1)} %broadcast_in_dim.105), calls=%async_computation.4 | async-start | bytes 524288 | tf_op jit(solution)/shard_map/all_to_all | solution.py:15
  146.1 44.2 %copy-start.3 = (f32[1,4,1,128]{3,2,1,0:T(1,128)S(1)}, f32[1,4,1,128]{3,2,1,0:T(1,128)}, u32[]{:S(2)}) copy-start(f32[1,4,1,128]{3,2,1,0:T(1,128)} %param.9) | copy-start | bytes 6148
  146.1 44.8 %copy-start.2 = (f32[1,4,8,1024]{3,2,1,0:T(8,128)S(1)}, f32[1,4,8,1024]{3,2,1,0:T(8,128)}, u32[]{:S(2)}) copy-start(f32[1,4,8,1024]{3,2,1,0:T(8,128)} %param.8) | copy-start | bytes 393220
  146.1 41.5 %all-to-all-start.5 = ((bf16[4,1104,128]{2,1,0:T(8,128)(2,1)}), bf16[4,1104,128]{2,1,0:T(8,128)(2,1)S(1)}, u32[]{:S(2)}, u32[]{:S(2)}) async-start(bf16[4,1104,128]{2,1,0:T(8,128)(2,1)} %pad_maximum_fusion), calls=%async_computation.5 | async-start | bytes 2260992 | tf_op jit(solution)/shard_map/all_to_all | solution.py:15
